TPU v7x, 32 devices: a whole 2x2x4 slice. The times are simulated.
32 devices in a mesh: dp: 16 (over z, x, core), tensor: 2 (over y).
Axes of the slice: x: 2, y: 2, z: 4, core: 2. Of those that a mesh axis runs over, the one named last changes fastest.
Arguments:
- tokens: bfloat16 [8192, 1536], P(('dp', 'tensor')), may hold values from -16 to 16
- w_query: bfloat16 [1536, 1536], P('dp', 'tensor'), may hold values from -0.15625 to 0.15625
- key_weight: bfloat16 [1536, 256], P('dp', 'tensor'), may hold values from -0.15625 to 0.15625
- value_weight: bfloat16 [1536, 256], P('dp', 'tensor'), may hold values from -0.15625 to 0.15625
- b_query: bfloat16 [1536], P('tensor'), may hold values from -3 to 3
- key_bias: bfloat16 [256], P('tensor'), may hold values from -3 to 3
- value_bias: bfloat16 [256], P('tensor'), may hold values from -3 to 3
- w_out: bfloat16 [1536, 1536], P('tensor', 'dp'), may hold values from -1.75 to 1.75
- gain_attn: bfloat16 [1536], replicated, may hold values from 0.5 to 1.5
- gain_mlp: bfloat16 [1536], replicated, may hold values from 0.5 to 1.5
- w_gate: bfloat16 [1536, 8960], P('dp', 'tensor'), may hold values from -0.15625 to 0.15625
- w_up: bfloat16 [1536, 8960], P('dp', 'tensor'), may hold values from -0.15625 to 0.15625
- w_down: bfloat16 [8960, 1536], P('tensor', 'dp'), may hold values from -0.0625 to 0.0625
- cotangent: bfloat16 [8192, 1536], P(('dp', 'tensor')), may hold values from -6 to 6
Outputs:
- mixed: bfloat16 [8192, 1536], P(('dp', 'tensor'))
- grad_tokens: float32 [8192, 1536], P(('dp', 'tensor'))
- grad_w_query: float32 [1536, 1536], P('dp', 'tensor')
- grad_w_key: float32 [1536, 256], P('dp', 'tensor')
- grad_w_value: float32 [1536, 256], P('dp', 'tensor')
- grad_b_query: float32 [1536], P('tensor')
- grad_b_key: float32 [256], P('tensor')
- grad_b_value: float32 [256], P('tensor')
- grad_w_out: float32 [1536, 1536], P('tensor', 'dp')
- grad_gain_attn: float32 [1536], replicated
- grad_gain_mlp: float32 [1536], replicated
- grad_w_gate: float32 [1536, 8960], P('dp', 'tensor')
- grad_w_up: float32 [1536, 8960], P('dp', 'tensor')
- grad_w_down: float32 [8960, 1536], P('tensor', 'dp')
All inputs are finite; a program needn't handle non-finite values.
Results may differ from a plain program's by a relative error of at most 0.018.
Values may be sent and summed in bfloat16 or wider, within the bound.
A program may use at most 192 MiB of HBM per device.

v0:
```python
import math

import jax
import jax.numpy as jnp
from jax import lax
from jax.sharding import PartitionSpec as P

QUERY_HEADS = 12
KEY_VALUE_HEADS = 2
HEAD_SIZE = 128
SEQUENCE_TOKENS = 512


norm_eps = 1e-06
rope_base = 1000000.0


def rotate(values):
    midway = values.shape[-1] // 2
    return jnp.concatenate([-values[..., midway:], values[..., :midway]], axis=-1)


def rope_tables(length, columns):
    midway = columns // 2
    inverse = jnp.exp(
        jnp.arange(midway, dtype=jnp.float32) * (-2.0 * math.log(rope_base) / columns)
    )
    angles = jnp.arange(length, dtype=jnp.float32)[:, None] * inverse[None, :]
    angles = jnp.concatenate([angles, angles], axis=-1)
    return (jnp.cos(angles)[None, :, None, :], jnp.sin(angles)[None, :, None, :])


def rms_scale(values):
    return lax.rsqrt(jnp.mean(values * values, axis=-1, keepdims=True) + norm_eps)


def norm_back(values, scale, gain, upstream):
    scaled = upstream * gain
    return scale * scaled - values * (scale * scale * scale) * jnp.mean(
        scaled * values, axis=-1, keepdims=True
    )


def dot_rows(left, right):
    return jnp.dot(left, right, preferred_element_type=jnp.float32)


def dot_left(left, right):
    return lax.dot_general(
        left, right, (((0,), (0,)), ((), ())), preferred_element_type=jnp.float32
    )


def dot_right(left, right):
    return lax.dot_general(
        left, right, (((1,), (1,)), ((), ())), preferred_element_type=jnp.float32
    )


def attend_forward(query_block, key_block, value_block, causal, factor):
    scores = (
        jnp.einsum("sjgd,tjd->jgst", query_block, key_block, preferred_element_type=jnp.float32)
        * factor
    )
    scores = jnp.where(causal, scores, -1e30)
    largest = jnp.max(scores, axis=-1, keepdims=True)
    exponent = jnp.exp(scores - largest)
    row_totals = jnp.sum(exponent, axis=-1, keepdims=True)
    probs_low = (exponent / row_totals).astype(jnp.bfloat16)
    result = jnp.einsum(
        "jgst,tjd->sjgd", probs_low, value_block, preferred_element_type=jnp.float32
    )
    return (result.astype(jnp.bfloat16), largest + jnp.log(row_totals))


def attend_backward(query_block, key_block, value_block, grad_block, logsum, causal, factor):
    scores = (
        jnp.einsum("sjgd,tjd->jgst", query_block, key_block, preferred_element_type=jnp.float32)
        * factor
    )
    scores = jnp.where(causal, scores, -1e30)
    probs = jnp.exp(scores - logsum)
    probs_low = probs.astype(jnp.bfloat16)
    grad_values = jnp.einsum(
        "jgst,sjgd->tjd", probs_low, grad_block, preferred_element_type=jnp.float32
    )
    grad_probs = jnp.einsum(
        "sjgd,tjd->jgst", grad_block, value_block, preferred_element_type=jnp.float32
    )
    inner = jnp.sum(grad_probs * probs, axis=-1, keepdims=True)
    grad_scores = (probs * (grad_probs - inner)).astype(jnp.bfloat16)
    grad_queries = (
        jnp.einsum("jgst,tjd->sjgd", grad_scores, key_block, preferred_element_type=jnp.float32)
        * factor
    )
    grad_keys = (
        jnp.einsum("jgst,sjgd->tjd", grad_scores, query_block, preferred_element_type=jnp.float32)
        * factor
    )
    return (grad_queries, grad_keys, grad_values)


def per_device(
    tokens,
    w_query,
    key_weight,
    value_weight,
    b_query,
    key_bias,
    value_bias,
    w_out,
    gain_attn,
    gain_mlp,
    w_gate,
    w_up,
    w_down,
    cotangent,
):
    query_full, key_full, value_full, out_full = (
        lax.all_gather(w_query, "dp", axis=0, tiled=True),
        lax.all_gather(key_weight, "dp", axis=0, tiled=True),
        lax.all_gather(value_weight, "dp", axis=0, tiled=True),
        lax.all_gather(w_out, "dp", axis=1, tiled=True),
    )
    gate_full, up_full, down_full = (
        lax.all_gather(w_gate, "dp", axis=0, tiled=True),
        lax.all_gather(w_up, "dp", axis=0, tiled=True),
        lax.all_gather(w_down, "dp", axis=1, tiled=True),
    )
    local_heads = w_query.shape[1] // HEAD_SIZE
    local_groups = key_weight.shape[1] // HEAD_SIZE
    share = local_heads // local_groups
    factor = 1.0 / math.sqrt(HEAD_SIZE)
    cosine, sine = rope_tables(SEQUENCE_TOKENS, HEAD_SIZE)
    causal = jnp.arange(SEQUENCE_TOKENS)[:, None] >= jnp.arange(SEQUENCE_TOKENS)[None, :]
    inputs = tokens.astype(jnp.float32)
    scale_attn = rms_scale(inputs)
    normed_attention = (inputs * scale_attn * gain_attn).astype(jnp.bfloat16)
    normed_all = lax.all_gather(normed_attention, "tensor", axis=0, tiled=True)
    total_rows = normed_all.shape[0]
    sequences = total_rows // SEQUENCE_TOKENS
    query_lin = (dot_rows(normed_all, query_full) + b_query).reshape(
        sequences, SEQUENCE_TOKENS, local_heads, HEAD_SIZE
    )
    key_linear = (dot_rows(normed_all, key_full) + key_bias).reshape(
        sequences, SEQUENCE_TOKENS, local_groups, HEAD_SIZE
    )
    value_linear = dot_rows(normed_all, value_full) + value_bias
    query_matrix = (query_lin * cosine + rotate(query_lin) * sine).astype(jnp.bfloat16)
    query_matrix = query_matrix.reshape(sequences, SEQUENCE_TOKENS, local_groups, share, HEAD_SIZE)
    keys = (key_linear * cosine + rotate(key_linear) * sine).astype(jnp.bfloat16)
    values = value_linear.astype(jnp.bfloat16).reshape(
        sequences, SEQUENCE_TOKENS, local_groups, HEAD_SIZE
    )

    def forward_block(blocks):
        return attend_forward(blocks[0], blocks[1], blocks[2], causal, factor)

    mixed_heads, logsum = lax.map(forward_block, (query_matrix, keys, values))
    mixed_all = mixed_heads.reshape(total_rows, local_heads * HEAD_SIZE)
    attended = lax.psum_scatter(
        dot_rows(mixed_all, out_full), "tensor", scatter_dimension=0, tiled=True
    )
    middle = inputs + attended
    scale_mlp = rms_scale(middle)
    normed_mlp = (middle * scale_mlp * gain_mlp).astype(jnp.bfloat16)
    mlp_all = lax.all_gather(normed_mlp, "tensor", axis=0, tiled=True)
    gate = dot_rows(mlp_all, gate_full)
    upper = dot_rows(mlp_all, up_full)
    hidden = (jax.nn.silu(gate) * upper).astype(jnp.bfloat16)
    branch = lax.psum_scatter(
        dot_rows(hidden, down_full).astype(jnp.bfloat16), "tensor", scatter_dimension=0, tiled=True
    ).astype(jnp.float32)
    mixed = (middle + branch).astype(jnp.bfloat16)
    back_weights = (
        lax.all_gather(w_query, "dp", axis=0, tiled=True),
        lax.all_gather(key_weight, "dp", axis=0, tiled=True),
        lax.all_gather(value_weight, "dp", axis=0, tiled=True),
        lax.all_gather(w_out, "dp", axis=1, tiled=True),
        lax.all_gather(w_gate, "dp", axis=0, tiled=True),
        lax.all_gather(w_up, "dp", axis=0, tiled=True),
        lax.all_gather(w_down, "dp", axis=1, tiled=True),
    )
    query_back, key_back, value_back, out_back, gate_back, up_back, down_back = back_weights
    upstream = cotangent.astype(jnp.float32)
    grad_rows = lax.all_gather(cotangent, "tensor", axis=0, tiled=True)
    grad_hidden = dot_right(grad_rows, down_back)
    grad_down_part = dot_left(hidden, grad_rows)
    sigma = jax.nn.sigmoid(gate)
    grad_gate = (grad_hidden * upper * sigma * (1.0 + gate * (1.0 - sigma))).astype(jnp.bfloat16)
    grad_up = (grad_hidden * gate * sigma).astype(jnp.bfloat16)
    grad_gate_part = dot_left(mlp_all, grad_gate)
    grad_up_part = dot_left(mlp_all, grad_up)
    grad_normed_mlp = lax.psum_scatter(
        dot_right(grad_gate, gate_back) + dot_right(grad_up, up_back),
        "tensor",
        scatter_dimension=0,
        tiled=True,
    )
    grad_w_gate, grad_w_up, grad_w_down = (
        lax.psum_scatter(grad_gate_part, "dp", scatter_dimension=0, tiled=True),
        lax.psum_scatter(grad_up_part, "dp", scatter_dimension=0, tiled=True),
        lax.psum_scatter(grad_down_part, "dp", scatter_dimension=1, tiled=True),
    )
    grad_middle = upstream + norm_back(middle, scale_mlp, gain_mlp, grad_normed_mlp)
    gain_mlp_term = jnp.sum(grad_normed_mlp * middle * scale_mlp, axis=0)
    grad_attended = grad_middle.astype(jnp.bfloat16)
    grad_att_all = lax.all_gather(grad_attended, "tensor", axis=0, tiled=True)
    grad_mixed = dot_right(grad_att_all, out_back).astype(jnp.bfloat16)
    grad_out_part = dot_left(mixed_all, grad_att_all)
    grad_blocks = grad_mixed.reshape(sequences, SEQUENCE_TOKENS, local_groups, share, HEAD_SIZE)

    def backward_block(blocks):
        return attend_backward(
            blocks[0], blocks[1], blocks[2], blocks[3], blocks[4], causal, factor
        )

    grad_queries, grad_keys, grad_values = lax.map(
        backward_block, (query_matrix, keys, values, grad_blocks, logsum)
    )
    grad_queries = grad_queries.reshape(sequences, SEQUENCE_TOKENS, local_heads, HEAD_SIZE)
    grad_query_lin = (grad_queries * cosine - rotate(grad_queries * sine)).astype(jnp.bfloat16)
    grad_query_lin = grad_query_lin.reshape(total_rows, local_heads * HEAD_SIZE)
    grad_key_lin = (grad_keys * cosine - rotate(grad_keys * sine)).astype(jnp.bfloat16)
    grad_key_lin = grad_key_lin.reshape(total_rows, local_groups * HEAD_SIZE)
    grad_value_lin = grad_values.astype(jnp.bfloat16).reshape(total_rows, local_groups * HEAD_SIZE)
    grad_query_part = dot_left(normed_all, grad_query_lin)
    grad_key_part = dot_left(normed_all, grad_key_lin)
    grad_value_part = dot_left(normed_all, grad_value_lin)
    grad_normed_attn = lax.psum_scatter(
        (
            dot_right(grad_query_lin, query_back)
            + dot_right(grad_key_lin, key_back)
            + dot_right(grad_value_lin, value_back)
        ).astype(jnp.bfloat16),
        "tensor",
        scatter_dimension=0,
        tiled=True,
    ).astype(jnp.float32)
    grad_w_query, grad_w_key, grad_w_value, grad_w_out = (
        lax.psum_scatter(grad_query_part, "dp", scatter_dimension=0, tiled=True),
        lax.psum_scatter(grad_key_part, "dp", scatter_dimension=0, tiled=True),
        lax.psum_scatter(grad_value_part, "dp", scatter_dimension=0, tiled=True),
        lax.psum_scatter(grad_out_part, "dp", scatter_dimension=1, tiled=True),
    )
    grad_tokens = grad_middle + norm_back(inputs, scale_attn, gain_attn, grad_normed_attn)
    gain_attn_term = jnp.sum(grad_normed_attn * inputs * scale_attn, axis=0)
    position = lax.axis_index("tensor")
    query_width = local_heads * HEAD_SIZE
    key_width = local_groups * HEAD_SIZE
    bias_query_full = lax.dynamic_update_slice(
        jnp.zeros((QUERY_HEADS * HEAD_SIZE,), jnp.float32),
        jnp.sum(grad_query_lin, axis=0, dtype=jnp.float32),
        (position * query_width,),
    )
    bias_key_full = lax.dynamic_update_slice(
        jnp.zeros((KEY_VALUE_HEADS * HEAD_SIZE,), jnp.float32),
        jnp.sum(grad_key_lin, axis=0, dtype=jnp.float32),
        (position * key_width,),
    )
    bias_value_full = lax.dynamic_update_slice(
        jnp.zeros((KEY_VALUE_HEADS * HEAD_SIZE,), jnp.float32),
        jnp.sum(grad_value_lin, axis=0, dtype=jnp.float32),
        (position * key_width,),
    )
    grad_gain_attn, grad_gain_mlp, query_sums, key_sums, value_sums = lax.psum(
        (gain_attn_term, gain_mlp_term, bias_query_full, bias_key_full, bias_value_full),
        ("dp", "tensor"),
    )
    grad_b_query = lax.dynamic_slice_in_dim(query_sums, position * query_width, query_width, 0)
    grad_b_key = lax.dynamic_slice_in_dim(key_sums, position * key_width, key_width, 0)
    grad_b_value = lax.dynamic_slice_in_dim(value_sums, position * key_width, key_width, 0)
    return (
        mixed,
        grad_tokens,
        grad_w_query,
        grad_w_key,
        grad_w_value,
        grad_b_query,
        grad_b_key,
        grad_b_value,
        grad_w_out,
        grad_gain_attn,
        grad_gain_mlp,
        grad_w_gate,
        grad_w_up,
        grad_w_down,
    )


def solution(mesh):
    in_specs = (
        P(("dp", "tensor"), None),
        P("dp", "tensor"),
        P("dp", "tensor"),
        P("dp", "tensor"),
        P("tensor"),
        P("tensor"),
        P("tensor"),
        P("tensor", "dp"),
        P(),
        P(),
        P("dp", "tensor"),
        P("dp", "tensor"),
        P("tensor", "dp"),
        P(("dp", "tensor"), None),
    )
    out_specs = (
        P(("dp", "tensor"), None),
        P(("dp", "tensor"), None),
        P("dp", "tensor"),
        P("dp", "tensor"),
        P("dp", "tensor"),
        P("tensor"),
        P("tensor"),
        P("tensor"),
        P("tensor", "dp"),
        P(),
        P(),
        P("dp", "tensor"),
        P("dp", "tensor"),
        P("tensor", "dp"),
    )
    return jax.shard_map(
        per_device, mesh=mesh, in_specs=in_specs, out_specs=out_specs, check_vma=False
    )
```

profile of v0, /device:TPU:0, one launch (start us, length us, event | category | flops | bytes accessed | tf_op | source)
XLA Modules:
  0.0 1850.3 jit_solution(1743899738790878887)
XLA Ops:
  15.2 24.1 %all_gather.42 = bf16[1536,128]{1,0:T(8,128)(2,1)S(1)} all-gather(bf16[96,128]{1,0:T(8,128)(2,1)S(1)} %copy-done.30), channel_id=1, replica_groups=mesh['dp'=16,'tensor'=2] {'dp'}, dimensions={0}, use_global_device_ids=true | all-gather | bytes 417792 | tf_op jit(solution)/shard_map/all_gather | solution.py:121
  39.3 18.6 %all_gather.41 = bf16[1536,128]{1,0:T(8,128)(2,1)S(1)} all-gather(bf16[96,128]{1,0:T(8,128)(2,1)S(1)} %copy-done.31), channel_id=1, replica_groups=mesh['dp'=16,'tensor'=2] {'dp'}, dimensions={0}, use_global_device_ids=true | all-gather | bytes 417792 | tf_op jit(solution)/shard_map/all_gather | solution.py:122
  66.1 21.4 %all-gather.12.cloned.1.call-done = bf16[1536,768]{1,0:T(8,128)(2,1)} async-done(((bf16[96,768]{1,0:T(8,128)(2,1)}), bf16[1536,768]{1,0:T(8,128)(2,1)}) %all-gather.12.cloned.1.call-update) | async-done | bytes 2359312 | tf_op jit(solution)/shard_map/all_gather | solution.py:120
  105.2 25.8 %all-gather.14.cloned.1.call-done = bf16[768,1536]{0,1:T(8,128)(2,1)} async-done(((bf16[768,96]{0,1:T(8,128)(2,1)}), bf16[768,1536]{0,1:T(8,128)(2,1)}) %all-gather.14.cloned.1.call-update) | async-done | bytes 2359312 | tf_op jit(solution)/shard_map/all_gather | solution.py:123
  130.9 4.7 fusion.57
  136.4 41.6 %reduce-scatter.12.cloned.1.call-done = f32[256,1536]{1,0:T(8,128)} async-done(((f32[512,1536]{1,0:T(8,128)}), f32[256,1536]{1,0:T(8,128)}) %reduce-scatter.12.cloned.1.call-update) | async-done | bytes 1572880 | tf_op jit(solution)/shard_map/reduce_scatter | solution.py:161
  184.0 24.2 %all-gather.16.cloned.1.call-done = bf16[512,1536]{1,0:T(8,128)(2,1)} async-done(((bf16[256,1536]{1,0:T(8,128)(2,1)}), bf16[512,1536]{1,0:T(8,128)(2,1)}) %all-gather.16.cloned.1.call-update) | async-done | bytes 1572880 | tf_op jit(solution)/shard_map/all_gather | solution.py:167
  208.2 110.6 %all-gather.20.cloned.1.call-done = bf16[1536,4480]{1,0:T(8,128)(2,1)} async-done(((bf16[96,4480]{1,0:T(8,128)(2,1)}), bf16[1536,4480]{1,0:T(8,128)(2,1)}) %all-gather.20.cloned.1.call-update) | async-done | bytes 13762576 | tf_op jit(solution)/shard_map/all_gather | solution.py:127
  318.8 13.2 fusion.59
  332.0 95.7 %all-gather.18.cloned.1.call-done = bf16[1536,4480]{1,0:T(8,128)(2,1)} async-done(((bf16[96,4480]{1,0:T(8,128)(2,1)}), bf16[1536,4480]{1,0:T(8,128)(2,1)}) %all-gather.18.cloned.1.call-update) | async-done | bytes 13762576 | tf_op jit(solution)/shard_map/all_gather | solution.py:126
  427.7 12.7 fusion.58
  440.5 14.3 all-gather.24.cloned.1.call-done
  454.8 110.8 %all-gather.22.cloned.1.call-done = bf16[4480,1536]{0,1:T(8,128)(2,1)} async-done(((bf16[4480,96]{0,1:T(8,128)(2,1)}), bf16[4480,1536]{0,1:T(8,128)(2,1)}) %all-gather.22.cloned.1.call-update) | async-done | bytes 13762576 | tf_op jit(solution)/shard_map/all_gather | solution.py:128
  565.5 22.0 %multiply_convert_fusion = (bf16[512,4480]{1,0:T(8,128)(2,1)}, bf16[512,4480]{1,0:T(8,128)(2,1)}, bf16[512,4480]{1,0:T(8,128)(2,1)}) fusion(f32[512,4480]{1,0:T(8,128)} %fusion.58, f32[512,4480]{1,0:T(8,128)} %fusion.59, bf16[512,1536]{1,0:T(8,128)(2,1)} %all-gather.24.cloned.1.call-done, bf16[4480,1536]{0,1:T(8,128)(2,1)} %all-gather.22.cloned.1.call-done), kind=kOutput, calls=%fused_computation | convolution fusion | flops 7083130880 | bytes 47448064 | tf_op jit(solution)/shard_map/dot_general | solution.py:55
  587.6 11.7 fusion.60
  599.3 11.9 convolution_add_fusion.2
  611.3 12.9 convolution_convert_fusion
  624.3 28.7 %reduce-scatter.16.cloned.1.call-done = f32[256,1536]{1,0:T(8,128)} async-done(((f32[512,1536]{1,0:T(8,128)}), f32[256,1536]{1,0:T(8,128)}) %reduce-scatter.16.cloned.1.call-update) | async-done | bytes 1572880 | tf_op jit(solution)/shard_map/reduce_scatter | solution.py:194
  654.8 27.1 %reduce-scatter.14.cloned.1.call-done = bf16[256,1536]{1,0:T(8,128)(2,1)} async-done(((bf16[512,1536]{1,0:T(8,128)(2,1)}), bf16[256,1536]{1,0:T(8,128)(2,1)}) %reduce-scatter.14.cloned.1.call-update) | async-done | bytes 786448 | tf_op jit(solution)/shard_map/reduce_scatter | solution.py:171
  685.5 8.6 reduce-scatter.18.cloned.1.call-start
  694.1 18.7 %all-gather.26.cloned.1.call-done = bf16[512,1536]{1,0:T(8,128)(2,1)} async-done(((bf16[256,1536]{1,0:T(8,128)(2,1)}), bf16[512,1536]{1,0:T(8,128)(2,1)}) %all-gather.26.cloned.1.call-update) | async-done | bytes 1572880 | tf_op jit(solution)/shard_map/all_gather | solution.py:208
  742.3 5.3 fusion.65
  753.9 14.8 fusion.67
  768.8 14.7 fusion.66
  784.9 14.7 fusion.68
  802.5 40.0 %all-reduce = (f32[1536]{0:T(1024)S(1)}, f32[256]{0:T(256)S(1)}, f32[256]{0:T(256)S(1)}, f32[1536]{0:T(1024)}, f32[1536]{0:T(1024)}) all-reduce(f32[1536]{0:T(1024)S(1)} %bitcast_dynamic-update-slice_fusion, f32[256]{0:T(256)S(1)} %dynamic_update_slice.24, ...), channel_id=1, replica_groups=mesh['dp'=16,'tensor'=2] {'dp','tensor'}, use_global_device_ids=true, to_apply=%region_15.16 | all-reduce | flops 5120 | bytes 40960 | tf_op jit(solution)/shard_map/psum | solution.py:266
  845.9 38.6 %reduce-scatter.22.cloned.1.call-done = f32[96,128]{1,0:T(8,128)} async-done(((f32[1536,128]{1,0:T(8,128)}), f32[96,128]{1,0:T(8,128)}) %reduce-scatter.22.cloned.1.call-update) | async-done | bytes 49168 | tf_op jit(solution)/shard_map/reduce_scatter | solution.py:242
  884.6 78.9 %reduce-scatter.26.cloned.1.call-done = f32[768,96]{0,1:T(8,128)} async-done(((f32[768,1536]{0,1:T(8,128)}), f32[768,96]{0,1:T(8,128)}) %reduce-scatter.26.cloned.1.call-update) | async-done | bytes 294928 | tf_op jit(solution)/shard_map/reduce_scatter | solution.py:244
  963.5 79.4 %reduce-scatter.20.cloned.1.call-done = f32[96,768]{1,0:T(8,128)} async-done(((f32[1536,768]{1,0:T(8,128)}), f32[96,768]{1,0:T(8,128)}) %reduce-scatter.20.cloned.1.call-update) | async-done | bytes 294928 | tf_op jit(solution)/shard_map/reduce_scatter | solution.py:241
  1042.9 266.4 %reduce-scatter.30.cloned.1.call-done = f32[96,4480]{1,0:T(8,128)} async-done(((f32[1536,4480]{1,0:T(8,128)}), f32[96,4480]{1,0:T(8,128)}) %reduce-scatter.30.cloned.1.call-update) | async-done | bytes 1720336 | tf_op jit(solution)/shard_map/reduce_scatter | solution.py:202
  1309.3 267.2 %reduce-scatter.28.cloned.1.call-done = f32[96,4480]{1,0:T(8,128)} async-done(((f32[1536,4480]{1,0:T(8,128)}), f32[96,4480]{1,0:T(8,128)}) %reduce-scatter.28.cloned.1.call-update) | async-done | bytes 1720336 | tf_op jit(solution)/shard_map/reduce_scatter | solution.py:201
  1576.5 266.5 %reduce-scatter.32.cloned.1.call-done = f32[4480,96]{0,1:T(8,128)} async-done(((f32[4480,1536]{0,1:T(8,128)}), f32[4480,96]{0,1:T(8,128)}) %reduce-scatter.32.cloned.1.call-update) | async-done | bytes 1720336 | tf_op jit(solution)/shard_map/reduce_scatter | solution.py:203
  (201 shorter events, 88.7 us)
Async XLA Ops:
  7.2 51.6 %all-gather.10.cloned.1.call-start = ((), (), s32[]{:S(2)}) async-start(), calls=%async_computation.11 | async-start | bytes 2359296 | tf_op jit(solution)/shard_map/all_gather | solution.py:139
  8.6 6.6 copy-start.41
  8.6 6.6 copy-start.30
  10.5 28.8 %copy-start.31 = (bf16[96,128]{1,0:T(8,128)(2,1)S(1)}, bf16[96,128]{1,0:T(8,128)(2,1)}, u32[]{:S(2)}) copy-start(bf16[96,128]{1,0:T(8,128)(2,1)} %param.17) | copy-start | bytes 73732
  12.8 74.7 %all-gather.12.cloned.1.call-start = ((), (), s32[]{:S(2)}) async-start(), calls=%async_computation.12 | async-start | bytes 2506752 | tf_op jit(solution)/shard_map/all_gather | solution.py:120
  13.6 117.4 %all-gather.14.cloned.1.call-start = ((), (), s32[]{:S(2)}) async-start(), calls=%async_computation.13 | async-start | bytes 2506752 | tf_op jit(solution)/shard_map/all_gather | solution.py:123
  14.3 163.7 %reduce-scatter.12.cloned.1.call-start = ((), (), s32[]{:S(2)}) async-start(), calls=%async_computation.14 | async-start | bytes 4718592 | tf_op jit(solution)/shard_map/reduce_scatter | solution.py:161
  39.3 21.6 %copy-start.15 = (bf16[1536,128]{1,0:T(8,128)(2,1)}, bf16[1536,128]{1,0:T(8,128)(2,1)S(1)}, u32[]{:S(2)}) copy-start(bf16[1536,128]{1,0:T(8,128)(2,1)S(1)} %all_gather.42) | copy-start | bytes 1179652
  57.9 7.0 copy-start.13
  105.2 30.5 %copy-start.43 = (bf16[128,6,512]{2,0,1:T(8,128)(2,1)}, bf16[128,6,512]{2,0,1:T(8,128)(2,1)S(1)}, u32[]{:S(2)}) copy-start(bf16[128,6,512]{2,0,1:T(8,128)(2,1)S(1)} %fusion.27) | copy-start | bytes 2359300
  135.7 42.3 %copy-start.3 = (bf16[256,1536]{1,0:T(8,128)(2,1)S(1)}, bf16[256,1536]{1,0:T(8,128)(2,1)}, u32[]{:S(2)}) copy-start(bf16[256,1536]{1,0:T(8,128)(2,1)} %param.14) | copy-start | bytes 2359300
  135.7 72.5 %all-gather.16.cloned.1.call-start = ((), (), s32[]{:S(2)}) async-start(), calls=%async_computation.15 | async-start | bytes 2359296 | tf_op jit(solution)/shard_map/all_gather | solution.py:167
  180.8 138.0 %all-gather.20.cloned.1.call-start = ((), (), s32[]{:S(2)}) async-start(), calls=%async_computation.17 | async-start | bytes 14622720 | tf_op jit(solution)/shard_map/all_gather | solution.py:127
  181.4 246.3 %all-gather.18.cloned.1.call-start = ((), (), s32[]{:S(2)}) async-start(), calls=%async_computation.16 | async-start | bytes 14622720 | tf_op jit(solution)/shard_map/all_gather | solution.py:126
  182.2 272.6 %all-gather.24.cloned.1.call-start = ((), (), s32[]{:S(2)}) async-start(), calls=%async_computation.20 | async-start | bytes 2359296 | tf_op jit(solution)/shard_map/all_gather | solution.py:186
  182.9 382.6 %all-gather.22.cloned.1.call-start = ((), (), s32[]{:S(2)}) async-start(), calls=%async_computation.18 | async-start | bytes 14622720 | tf_op jit(solution)/shard_map/all_gather | solution.py:128
  183.7 469.3 %reduce-scatter.16.cloned.1.call-start = ((), (), s32[]{:S(2)}) async-start(), calls=%async_computation.21 | async-start | bytes 4718592 | tf_op jit(solution)/shard_map/reduce_scatter | solution.py:194
  208.2 219.5 %copy-start.38 = (bf16[512,1536]{1,0:T(8,128)(2,1)S(1)}, bf16[512,1536]{1,0:T(8,128)(2,1)}, u32[]{:S(2)}) copy-start(bf16[512,1536]{1,0:T(8,128)(2,1)} %all-gather.16.cloned.1.call-done) | copy-start | bytes 4718596
  587.6 11.8 copy-start.44
  611.3 70.6 %reduce-scatter.14.cloned.1.call-start = ((), (), s32[]{:S(2)}) async-start(), calls=%async_computation.19 | async-start | bytes 2359296 | tf_op jit(solution)/shard_map/reduce_scatter | solution.py:171
  624.3 88.6 %all-gather.26.cloned.1.call-start = ((), (), s32[]{:S(2)}) async-start(), calls=%async_computation.22 | async-start | bytes 2359296 | tf_op jit(solution)/shard_map/all_gather | solution.py:208
  685.5 114.8 %reduce-scatter.18.cloned.1.call-start = ((), (), s32[]{:S(2)}) async-start(), calls=%async_computation.23 | async-start | bytes 2359296 | tf_op jit(solution)/shard_map/reduce_scatter | solution.py:230
  716.7 8.5 slice-start
  737.8 108.1 %reduce-scatter.24.cloned.1.call-start = ((), (), s32[]{:S(2)}) async-start(), calls=%async_computation.26 | async-start | bytes 835584 | tf_op jit(solution)/shard_map/reduce_scatter | solution.py:243
  740.7 143.9 %reduce-scatter.22.cloned.1.call-start = ((), (), s32[]{:S(2)}) async-start(), calls=%async_computation.25 | async-start | bytes 835584 | tf_op jit(solution)/shard_map/reduce_scatter | solution.py:242
  742.3 221.2 %reduce-scatter.26.cloned.1.call-start = ((), (), s32[]{:S(2)}) async-start(), calls=%async_computation.27 | async-start | bytes 5013504 | tf_op jit(solution)/shard_map/reduce_scatter | solution.py:244
  747.7 295.2 %reduce-scatter.20.cloned.1.call-start = ((), (), s32[]{:S(2)}) async-start(), calls=%async_computation.24 | async-start | bytes 5013504 | tf_op jit(solution)/shard_map/reduce_scatter | solution.py:241
  752.5 556.8 %reduce-scatter.30.cloned.1.call-start = ((), (), s32[]{:S(2)}) async-start(), calls=%async_computation.29 | async-start | bytes 29245440 | tf_op jit(solution)/shard_map/reduce_scatter | solution.py:202
  768.7 807.8 %reduce-scatter.28.cloned.1.call-start = ((), (), s32[]{:S(2)}) async-start(), calls=%async_computation.28 | async-start | bytes 29245440 | tf_op jit(solution)/shard_map/reduce_scatter | solution.py:201
  783.5 1059.5 %reduce-scatter.32.cloned.1.call-start = ((), (), s32[]{:S(2)}) async-start(), calls=%async_computation.30 | async-start | bytes 29245440 | tf_op jit(solution)/shard_map/reduce_scatter | solution.py:203
  799.7 44.6 %copy-start.34 = (f32[256]{0:T(256)S(1)}, f32[256]{0:T(256)}, u32[]{:S(2)}) copy-start(f32[256]{0:T(256)} %get-tuple-element.97) | copy-start | bytes 3076
  800.8 43.5 %copy-start.18 = (bf16[256,1536]{1,0:T(8,128)(2,1)S(1)}, bf16[256,1536]{1,0:T(8,128)(2,1)}, u32[]{:S(2)}) copy-start(bf16[256,1536]{1,0:T(8,128)(2,1)} %reduce-scatter.18.cloned.1.call-done) | copy-start | bytes 2359300
  (35 other events, 68.0 us)
Sparse Core Ops, SparseCore 0:
  12.9 29.8 all-gather.9
  45.2 42.3 all-gather.11
  89.8 41.0 all-gather.13
  135.8 42.1 reduce-scatter.11
  181.0 27.1 all-gather.15
  210.6 108.1 all-gather.19
  321.4 106.3 all-gather.17
  429.3 25.3 all-gather.23
  457.3 108.1 all-gather.21
  611.4 41.5 reduce-scatter.15
  655.8 26.0 reduce-scatter.13
  685.6 27.2 all-gather.25
  737.9 26.0 reduce-scatter.17
  768.0 56.6 reduce-scatter.23
  829.1 55.4 reduce-scatter.21
  888.9 74.5 reduce-scatter.25
  968.3 74.5 reduce-scatter.19
  1047.4 261.8 reduce-scatter.29
  1314.6 261.9 reduce-scatter.27
  1581.1 261.9 reduce-scatter.31
where the time goes:
time: 1860 us; the launch traced here: 1850 us
  waiting for transfers between devices  1520 us (82%)
  matrix products  174 us (9%)
  blocking collectives  82.7 us (4%)
  other arithmetic  27.7 us (1%)
  local copies, waits for them, and re-layouts  20.5 us (1%)
    reduce_scatter x1, waiting for transfers between devices, per_device(): lax.psum_scatter(grad_gate_part, 'dp', scatter_dimension=0, tiled=True)  267 us
    reduce_scatter x1, waiting for transfers between devices, per_device(): lax.psum_scatter(grad_down_part, 'dp', scatter_dimension=1, tiled=True)  267 us
    reduce_scatter x1, waiting for transfers between devices, per_device(): lax.psum_scatter(grad_up_part, 'dp', scatter_dimension=0, tiled=True)  266 us
    all_gather x1, waiting for transfers between devices, per_device(): lax.all_gather(w_down, 'dp', axis=1, tiled=True)  111 us
    all_gather x1, waiting for transfers between devices, per_device(): lax.all_gather(w_up, 'dp', axis=0, tiled=True)  111 us
    all_gather x1, waiting for transfers between devices, per_device(): lax.all_gather(w_gate, 'dp', axis=0, tiled=True)  95.7 us
    reduce_scatter x1, waiting for transfers between devices, per_device(): lax.psum_scatter(grad_query_part, 'dp', scatter_dimension=0, tiled=True)  79.4 us
    reduce_scatter x1, waiting for transfers between devices, per_device(): lax.psum_scatter(grad_out_part, 'dp', scatter_dimension=1, tiled=True)  78.9 us
  transfers between devices with their start and end apart: 20, of which 17 were waited for; matrix products, arithmetic and copies ran while one was open for 7% of the time, Pallas kernels for 0%

commit v1 on v0

v1 whole, which is shorter than its diff:
```python
import math

import jax
import jax.numpy as jnp
from jax import lax
from jax.experimental import pallas as pl
from jax.experimental.pallas import tpu as pltpu
from jax.sharding import PartitionSpec as P

QUERY_HEADS = 12
KEY_VALUE_HEADS = 2
HEAD_SIZE = 128
SEQUENCE_TOKENS = 512

QUADS = 4
WIDE = 256

norm_eps = 1e-06
rope_base = 1000000.0
BF = jnp.bfloat16
F32 = jnp.float32
MESH = pl.DeviceIdType.MESH


def rotate(values):
    midway = values.shape[-1] // 2
    return jnp.concatenate([-values[..., midway:], values[..., :midway]], axis=-1)


def rope_tables(length, columns):
    midway = columns // 2
    inverse = jnp.exp(
        jnp.arange(midway, dtype=jnp.float32) * (-2.0 * math.log(rope_base) / columns)
    )
    angles = jnp.arange(length, dtype=jnp.float32)[:, None] * inverse[None, :]
    angles = jnp.concatenate([angles, angles], axis=-1)
    return (jnp.cos(angles)[None, :, None, :], jnp.sin(angles)[None, :, None, :])


def rms_scale(values):
    return lax.rsqrt(jnp.mean(values * values, axis=-1, keepdims=True) + norm_eps)


def norm_back(values, scale, gain, upstream):
    scaled = upstream * gain
    return scale * scaled - values * (scale * scale * scale) * jnp.mean(
        scaled * values, axis=-1, keepdims=True
    )


def dot_rows(left, right):
    return jnp.dot(left, right, preferred_element_type=F32)


def dot_left(left, right):
    return lax.dot_general(left, right, (((0,), (0,)), ((), ())), preferred_element_type=F32)


def dot_right(left, right):
    return lax.dot_general(left, right, (((1,), (1,)), ((), ())), preferred_element_type=F32)


def round_up(value, step):
    return (value + step - 1) // step * step


class Sizes:
    def __init__(self, dp, rows, hidden, tokens):
        self.dp = dp
        self.outer = dp // QUADS
        self.rows = rows
        self.pad = round_up(rows, 16)
        self.whole = rows % 16 == 0
        self.wide = dp * rows
        self.slice = round_up(-(-hidden // QUADS), 128)
        self.head = self.slice % WIDE or WIDE
        self.full = (self.slice - self.head) // WIDE
        self.tokens = tokens
        self.hidden = hidden
        self.scratch = 30 if self.whole else 32


def mlp_kernel(sz, *refs):
    (
        xn_ref, cot_ref, wh_ref, wf_ref,
        gh_ref, gf_ref, gn_ref, br_ref,
        wagh, wagf, ruph, rupf, rdnh, rdnf, pairbuf, chipbuf,
        xb, cb, nacc, wvh, wv, pbh, pb, hh, hf, gg, gu, nst, nsd, tk, rth, rtf, own,
        s_a2a, r_a2a, s_ag, r_ag, s_rs, r_rs, s_fin, r_fin, s_tok, r_tok, s_sum, r_sum, loc,
    ) = refs[:16] + refs[-sz.scratch :][:30]
    abh, abf, stage, joined = (None,) * 4 if sz.whole else refs[16:18] + refs[-2:]
    O, NF, T = sz.outer, sz.full, sz.tokens
    HK, W, R, RP = sz.head, sz.wide, sz.rows, sz.pad
    R4 = QUADS * R
    me = lax.axis_index("dp")
    y = lax.axis_index("tensor")
    o, q = me // QUADS, me % QUADS
    x, c = q // 2, q % 2

    def at(o_, q_, y_):
        return (o_ * QUADS + q_, y_)

    above, below = lax.rem(o + 1, O), lax.rem(o + O - 1, O)
    up, down = at(above, q, y), at(below, q, y)
    core = at(o, x * 2 + 1 - c, y)
    chips = [(1 - x, 1 - y), (1 - x, y), (x, 1 - y)]
    order = chips + [(x, y)]

    def remote(src, dst, ssem, rsem, dev):
        return pltpu.make_async_remote_copy(
            src_ref=src, dst_ref=dst, send_sem=ssem, recv_sem=rsem,
            device_id=dev, device_id_type=MESH,
        )

    def local(src, dst, sem):
        return pltpu.make_async_copy(src, dst, sem)

    bar = pltpu.get_barrier_semaphore()

    def greet(dev):
        pl.semaphore_signal(bar, inc=1, device_id=dev, device_id_type=MESH)

    for dq in range(QUADS):
        for yy in range(2):
            if dq or yy:
                greet(at(o, lax.rem(q + dq, QUADS), (y + yy) % 2))
    pl.when(o < O - 1)(lambda: greet(up))
    pl.when(o > 0)(lambda: greet(down))
    pl.semaphore_wait(bar, 2 * QUADS - 1 + lax.min(o, 1) + lax.min(O - 1 - o, 1))

    class Chunk:
        def __init__(self, kk):
            self.head = kk is None
            if self.head:
                self.i, self.fk = 0, HK
                self.src, self.wag, self.rup, self.rdn = wh_ref, wagh, ruph, rdnh
                self.pb, self.out, self.tmp, self.hid = pbh, gh_ref, rth, hh
                self.wv, self.lw, self.ab = wvh, loc.at[0], abh
            else:
                self.i, self.fk = kk + 1, WIDE
                self.src, self.wag, self.rup, self.rdn = (
                    wf_ref.at[kk], wagf.at[kk], rupf.at[kk], rdnf.at[kk],
                )
                self.pb, self.out, self.tmp, self.hid = pb.at[kk], gf_ref.at[kk], rtf, hf.at[kk]
                self.wv, self.lw = wv.at[lax.rem(kk, 2)], loc.at[1 + lax.rem(kk, 2)]
                self.ab = None if abf is None else abf.at[kk]

        def block(self, ref, b):
            return ref.at[:, pl.ds(pl.multiple_of(b * R4, R4), R4), :]

        def part(self, ref, b, q_):
            return ref.at[:, pl.ds(pl.multiple_of((b * QUADS + q_) * R, R), R), :]

        def mine(self):
            return self.part(self.wag, o, q) if sz.whole else self.ab.at[q]

        def a2a(self, dq):
            to = lax.rem(q + dq, QUADS)
            return remote(
                self.src.at[to], self.mine(),
                s_a2a.at[self.i, dq - 1], r_a2a.at[self.i, dq - 1], at(o, to, y),
            )

        def a2a_own(self):
            return local(self.src.at[q], self.mine(), loc.at[3])

        def a2a_start(self):
            for dq in range(1, QUADS):
                self.a2a(dq).start()
            self.a2a_own().start()
            self.a2a_own().wait()

        def join(self):
            move = local(self.ab, stage.at[:, :, :, pl.ds(0, self.fk)], loc.at[3])
            move.start()
            move.wait()
            for m in range(3):
                rows = [stage[i, m, :, : self.fk].astype(F32)[:R] for i in range(QUADS)]
                joined[m, :, : self.fk] = jnp.concatenate(rows, axis=0).astype(BF)
            move = local(joined.at[:, :, pl.ds(0, self.fk)], self.block(self.wag, o), loc.at[3])
            move.start()
            move.wait()

        def ag(self, way, step, b):
            return remote(
                self.block(self.wag, b), self.block(self.wag, b),
                s_ag.at[self.i, way, step], r_ag.at[self.i, way, step], (up, down)[way],
            )

        def ag_own(self):
            for dq in range(1, QUADS):
                self.a2a(dq).wait_recv()
            if not sz.whole:
                self.join()
            pl.when(o < O - 1)(lambda: self.ag(0, 0, o).start())
            pl.when(o > 0)(lambda: self.ag(1, 0, o).start())

        def ag_pass(self, s):
            @pl.when(o - 1 - s >= 0)
            def _():
                self.ag(0, s, lax.max(o - 1 - s, 0)).wait_recv()
                if s + 1 < O - 1:
                    pl.when(o < O - 1)(lambda: self.ag(0, s + 1, lax.max(o - 1 - s, 0)).start())

            @pl.when(o + 1 + s <= O - 1)
            def _():
                self.ag(1, s, lax.min(o + 1 + s, O - 1)).wait_recv()
                if s + 1 < O - 1:
                    pl.when(o > 0)(lambda: self.ag(1, s + 1, lax.min(o + 1 + s, O - 1)).start())

        def ag_sent(self):
            for s in range(O - 1):

                @pl.when((o - s >= 0) & (o < O - 1))
                def _():
                    self.ag(0, s, lax.max(o - s, 0)).wait_send()

                @pl.when((o + s <= O - 1) & (o > 0))
                def _():
                    self.ag(1, s, lax.min(o + s, O - 1)).wait_send()

        def load(self):
            return local(self.wag, self.wv, self.lw)

        def rs(self, way, s):
            d = (O - 1 - s, s)[way]
            return remote(
                self.block(self.pb, d), self.block((self.rup, self.rdn)[way], d),
                s_rs.at[self.i, way, s], r_rs.at[self.i, way, s], (up, down)[way],
            )

        def fetch(self, way, d):
            return local(self.block((self.rup, self.rdn)[way], d), self.tmp.at[way], loc.at[4 + way])

        def add(self, way, d):
            ref = self.block(self.pb, d)
            for m in range(3):
                ref[m] = (ref[m].astype(F32) + self.tmp[way, m].astype(F32)).astype(BF)

        def rs_first(self):
            for s in range(O - 1):
                pl.when(o == 0)(lambda: self.rs(0, s).start())
                pl.when(o == O - 1)(lambda: self.rs(1, s).start())

        def rs_pass(self, s):
            d_up, d_down = O - 1 - s, s

            @pl.when((o > 0) & (d_up > o))
            def _():
                self.rs(0, s).wait_recv()
                self.fetch(0, d_up).start()
                self.fetch(0, d_up).wait()
                self.add(0, d_up)
                self.rs(0, s).start()

            @pl.when((o < O - 1) & (d_down < o))
            def _():
                self.rs(1, s).wait_recv()
                self.fetch(1, d_down).start()
                self.fetch(1, d_down).wait()
                self.add(1, d_down)
                self.rs(1, s).start()

        def result(self, q_):
            if sz.whole:
                return self.part(self.pb, o, q_)
            return self.ab.at[q_]

        def fin(self, dq):
            to = lax.rem(q + dq, QUADS)
            return remote(
                self.result(to), self.out.at[q],
                s_fin.at[self.i, dq - 1], r_fin.at[self.i, dq - 1], at(o, to, y),
            )

        def fin_own(self):
            return local(self.result(q), self.out.at[q], loc.at[3])

        def split(self):
            for m in range(3):
                rows = self.block(self.pb, o)[m].astype(F32)
                for i in range(QUADS):
                    part = rows[i * R : (i + 1) * R]
                    part = jnp.concatenate([part, jnp.zeros((RP - R, self.fk), F32)], axis=0)
                    stage[i, m, :, : self.fk] = part.astype(BF)
            move = local(stage.at[:, :, :, pl.ds(0, self.fk)], self.ab, loc.at[3])
            move.start()
            move.wait()

        def rs_last(self):
            @pl.when(o > 0)
            def _():
                self.rs(0, O - 1 - o).wait_recv()
                self.fetch(0, o).start()

            @pl.when(o < O - 1)
            def _():
                self.rs(1, o).wait_recv()
                self.fetch(1, o).start()

            @pl.when(o > 0)
            def _():
                self.fetch(0, o).wait()
                self.add(0, o)

            @pl.when(o < O - 1)
            def _():
                self.fetch(1, o).wait()
                self.add(1, o)

            if not sz.whole:
                self.split()
            for dq in range(1, QUADS):
                self.fin(dq).start()
            self.fin_own().start()
            self.fin_own().wait()

        def finished(self):
            for dq in range(1, QUADS):
                self.a2a(dq).wait_send()
                self.fin(dq).wait()
            self.ag_sent()
            for s in range(O):
                pl.when((o < O - 1) & (O - 1 - s > o))(lambda: self.rs(0, s).wait_send())
                pl.when((o > 0) & (s < o))(lambda: self.rs(1, s).wait_send())

    def chip_rows(xx, yy):
        return pl.ds(pl.multiple_of((xx * 2 + yy) * (2 * T), 2 * T), 2 * T)

    def rows_of(xx, yy, cc):
        return pl.ds(pl.multiple_of(((xx * 2 + yy) * 2 + cc) * T, T), T)

    def tok(src, buf, which, n):
        if n == 3:
            return remote(
                src, buf.at[rows_of(x, y, c), :],
                s_tok.at[which, n], r_tok.at[which, n], core,
            )
        xx, yy = chips[n]
        return remote(
            src, buf.at[rows_of(x, y, c), :],
            s_tok.at[which, n], r_tok.at[which, n], at(o, xx * 2 + c, yy),
        )

    def tok_pass(buf, which, n):
        xx, yy = chips[n]
        rows = rows_of(xx, yy, c)
        return remote(
            buf.at[rows, :], buf.at[rows, :],
            s_tok.at[which, 4 + n], r_tok.at[which, 4 + n], core,
        )

    def tok_start(src, buf, which):
        for n in (3, 2, 1, 0):
            tok(src, buf, which, n).start()
        local(src, buf.at[rows_of(x, y, c), :], loc.at[6]).start()
        local(src, buf.at[rows_of(x, y, c), :], loc.at[6]).wait()

    def tok_take(src, buf, which, n):
        tok(src, buf, which, n).wait_recv()
        if n < 3:
            tok_pass(buf, which, n).start()
            tok_pass(buf, which, n).wait_recv()

    def tok_sent(src, buf, which):
        for n in range(4):
            tok(src, buf, which, n).wait_send()
        for n in range(3):
            tok_pass(buf, which, n).wait_send()

    def sum_pair(n, stage, which):
        return remote(
            stage, pairbuf.at[which, n],
            s_sum.at[which, n], r_sum.at[which, n], core,
        )

    def sum_chip(n, stage, which):
        xx, yy = chips[n]
        return remote(
            stage, chipbuf.at[which, n],
            s_sum.at[which, 4 + n], r_sum.at[which, 4 + n], at(o, xx * 2 + c, yy),
        )

    def sum_open(n, which, stage):
        xx, yy = order[n]
        stage[...] = nacc[rows_of(xx, yy, 1 - c), :].astype(BF)
        sum_pair(n, stage, which).start()

    def take(src):
        cp = local(src, tk, loc.at[7])
        cp.start()
        cp.wait()
        return tk[...].astype(F32)

    def sum_mid(n, which, stage, onward):
        xx, yy = order[n]
        sum_pair(n, stage, which).wait_recv()
        total = nacc[rows_of(xx, yy, c), :] + take(pairbuf.at[which, n])
        if n < 3:
            onward[...] = total.astype(BF)
            sum_chip(n, onward, which).start()
        else:
            own[...] = total

    def sum_close(which, stages, onwards, out_ref):
        for n in range(3):
            sum_chip(n, onwards[n], which).wait_recv()
            own[...] = own[...] + take(chipbuf.at[which, n])
        cp = local(own, out_ref, loc.at[7])
        cp.start()
        cp.wait()
        for n in range(3):
            sum_chip(n, onwards[n], which).wait_send()
        for n in range(4):
            sum_pair(n, stages[n], which).wait_send()

    head = Chunk(None)
    head.a2a_start()
    tok_start(xn_ref, xb, 0)
    tok_start(cot_ref, cb, 1)
    Chunk(0).a2a_start()
    head.ag_own()
    for n in (2, 1, 0):
        tok_take(cot_ref, cb, 1, n)
    tok_take(cot_ref, cb, 1, 3)
    Chunk(0).ag_own()
    for s in range(O - 1):
        head.ag_pass(s)
    for kk in range(1, NF):
        Chunk(kk).a2a_start()
    head.load().start()
    if NF > 1:
        Chunk(1).ag_own()

    def tile(ch, rows, first):
        fk = ch.fk
        xv, cv = xb[rows, :], cb[rows, :]
        gate = dot_rows(xv, ch.wv[0])
        upper = dot_rows(xv, ch.wv[1])
        back = dot_rows(cv, ch.wv[2])
        sigma = jax.nn.sigmoid(gate)
        silu = gate * sigma
        ch.hid[rows, :] = (silu * upper).astype(BF)
        gg_t = (back * upper * (sigma * (1.0 + gate * (1.0 - sigma)))).astype(BF)
        gu_t = (back * silu).astype(BF)
        gg[rows, pl.ds(0, fk)] = gg_t
        gu[rows, pl.ds(0, fk)] = gu_t
        total = dot_right(gg_t, ch.wv[0]) + dot_right(gu_t, ch.wv[1])
        if first:
            nacc[rows, :] = total
        else:
            nacc[rows, :] = nacc[rows, :] + total

    TD = 512 if W % 512 == 0 else 256

    def products(ch, m):
        src, right = (
            (xb, lambda: gg[:, pl.ds(0, ch.fk)]),
            (xb, lambda: gu[:, pl.ds(0, ch.fk)]),
            (cb, lambda: ch.hid[...]),
        )[m]

        def step(i, carry):
            cols = pl.ds(pl.multiple_of(i * TD, TD), TD)
            ch.pb[m, cols, :] = dot_left(src[:, cols], right()).astype(BF)
            return carry

        lax.fori_loop(0, W // TD, step, 0)

    def ag_span(point):
        return range((O - 1) * point // 3, (O - 1) * (point + 1) // 3)

    head.load().wait()
    tok_take(xn_ref, xb, 0, 3)
    near_first = [3, 2, 1, 0]

    for p, n in enumerate(near_first):
        if n < 3:
            tok_take(xn_ref, xb, 0, n)
        xx, yy = order[n]
        tile(head, chip_rows(xx, yy), True)
        if p < 3 and NF > 0:
            for s in ag_span(p):
                Chunk(0).ag_pass(s)
    if NF > 0:
        Chunk(0).load().start()
    for m in range(3):
        products(head, m)
    head.rs_first()
    if NF > 2:
        Chunk(2).ag_own()

    def rs_at(i):
        def run():
            kk = i // O
            Chunk(kk).rs_pass(i % O)

        pl.when((i >= 0) & (i < NF * O))(run)

    per = (3 * O) // 4

    def body(kk, carry):
        ch, nxt = Chunk(kk), Chunk(lax.min(kk + 1, NF - 1))
        last = kk == NF - 1
        ch.load().wait()

        def visit(p, carry2):
            xx = jnp.where(p < 2, 1 - x, x)
            yy = jnp.where(p % 2 == 0, 1 - y, y)
            tile(ch, chip_rows(xx, yy), False)

            @pl.when(last)
            def _():
                for n in range(4):
                    pl.when(p == n)(lambda: sum_open(n, 0, nst.at[n]))
                for n in range(3):
                    pl.when(p == n + 1)(lambda: sum_mid(n, 0, nst.at[n], nsd.at[n]))

            @pl.when(kk < NF - 1)
            def _():
                for point in range(3):

                    @pl.when(p == point)
                    def _():
                        for s in ag_span(point):
                            nxt.ag_pass(s)

            @pl.when(kk == 0)
            def _():
                for s in range(O):
                    pl.when(p == s * 4 // O)(lambda: head.rs_pass(s))

            @pl.when((kk > 0) & (p < 3))
            def _():
                for e in range(-(-per // 3)):
                    pl.when(p * (-(-per // 3)) + e < per)(
                        lambda: rs_at((kk - 1) * per + p * (-(-per // 3)) + e)
                    )

            return carry2

        lax.fori_loop(0, 4, visit, 0)
        pl.when(kk < NF - 1)(lambda: nxt.load().start())
        pl.when(last)(lambda: sum_mid(3, 0, nst.at[3], None))
        for m in range(3):
            products(ch, m)
        ch.rs_first()
        pl.when(kk + 3 < NF)(lambda: Chunk(lax.min(kk + 3, NF - 1)).ag_own())
        return carry

    lax.fori_loop(0, NF, body, 0)

    done = (NF - 1) * per
    rs_total = NF * O
    sum_close(0, [nst.at[n] for n in range(4)], [nsd.at[n] for n in range(3)], gn_ref)

    mst = [cb.at[pl.ds(n * T, T), :] for n in range(4)]
    msd = [cb.at[pl.ds((4 + n) * T, T), :] for n in range(3)]

    def m_first(p, carry):
        rows = pl.ds(pl.multiple_of(p * 2 * T, 2 * T), 2 * T)
        nacc[rows, :] = dot_right(hh[rows, :], wvh[2])
        return carry

    lax.fori_loop(0, 4, m_first, 0)

    def m_chunk(kk, carry):
        cp = local(wagf.at[kk, 2], wv.at[0, 2], loc.at[8])
        cp.start()
        cp.wait()

        def m_tile(p, carry2):
            rows = pl.ds(pl.multiple_of(p * 2 * T, 2 * T), 2 * T)
            nacc[rows, :] = nacc[rows, :] + dot_right(hf[kk, rows, :], wv[0, 2])
            return carry2

        lax.fori_loop(0, 4, m_tile, 0)
        rs_at(done + kk)
        return carry

    lax.fori_loop(0, NF, m_chunk, 0)
    tok_sent(cot_ref, cb, 1)
    for n in range(4):
        sum_open(n, 1, mst[n])
    for n in range(4):
        sum_mid(n, 1, mst[n], msd[n] if n < 3 else None)
    head.rs_last()

    def rest(i, carry):
        rs_at(i)
        return carry

    lax.fori_loop(done + NF, rs_total, rest, 0)

    def lasts(kk, carry):
        Chunk(kk).rs_last()
        return carry

    lax.fori_loop(0, NF, lasts, 0)
    sum_close(1, mst, msd, br_ref)
    tok_sent(xn_ref, xb, 0)
    head.finished()

    def ends(kk, carry):
        Chunk(kk).finished()
        return carry

    lax.fori_loop(0, NF, ends, 0)


def feed_forward(sz, normed, cotangent, wh, wf):
    O, NF, T = sz.outer, sz.full, sz.tokens
    HK, W, R, RP = sz.head, sz.wide, sz.rows, sz.pad
    R4 = QUADS * R
    PT = 2 * QUADS * T
    out = jax.ShapeDtypeStruct
    any_spec = pl.BlockSpec(memory_space=pl.ANY)
    outs = [
        out((QUADS, 3, RP, HK), BF),
        out((NF, QUADS, 3, RP, WIDE), BF),
        out((T, W), F32),
        out((T, W), F32),
        out((3, W, HK), BF),
        out((NF, 3, W, WIDE), BF),
        out((3, W, HK), BF),
        out((NF, 3, W, WIDE), BF),
        out((3, W, HK), BF),
        out((NF, 3, W, WIDE), BF),
        out((2, 4, T, W), BF),
        out((2, 3, T, W), BF),
    ]
    if not sz.whole:
        outs += [out((QUADS, 3, RP, HK), BF), out((NF, QUADS, 3, RP, WIDE), BF)]
    dma = pltpu.SemaphoreType.DMA
    vm = pltpu.VMEM
    scratch = [
        vm((PT, W), BF),
        vm((PT, W), BF),
        vm((PT, W), F32),
        vm((3, W, HK), BF),
        vm((2, 3, W, WIDE), BF),
        vm((3, W, HK), BF),
        vm((NF, 3, W, WIDE), BF),
        vm((PT, HK), BF),
        vm((NF, PT, WIDE), BF),
        vm((PT, WIDE), BF),
        vm((PT, WIDE), BF),
        vm((4, T, W), BF),
        vm((3, T, W), BF),
        vm((T, W), BF),
        vm((2, 3, R4, HK), BF),
        vm((2, 3, R4, WIDE), BF),
        vm((T, W), F32),
        dma((NF + 1, 3)),
        dma((NF + 1, 3)),
        dma((NF + 1, 2, O - 1)),
        dma((NF + 1, 2, O - 1)),
        dma((NF + 1, 2, O)),
        dma((NF + 1, 2, O)),
        dma((NF + 1, 3)),
        dma((NF + 1, 3)),
        dma((2, 7)),
        dma((2, 7)),
        dma((2, 7)),
        dma((2, 7)),
        dma((9,)),
    ]
    if not sz.whole:
        scratch += [
            vm((QUADS, 3, RP, WIDE), BF),
            vm((3, R4, WIDE), BF),
        ]
    results = pl.pallas_call(
        lambda *refs: mlp_kernel(sz, *refs),
        out_shape=outs,
        in_specs=[any_spec] * 4,
        out_specs=[any_spec] * len(outs),
        scratch_shapes=scratch,
        compiler_params=pltpu.CompilerParams(
            collective_id=0, has_side_effects=True, vmem_limit_bytes=63 << 20
        ),
        name="feed_forward",
    )(normed, cotangent, wh, wf)
    return results[:4]


def per_device(
    sz,
    tokens,
    w_query,
    key_weight,
    value_weight,
    b_query,
    key_bias,
    value_bias,
    w_out,
    gain_attn,
    gain_mlp,
    w_gate,
    w_up,
    w_down,
    cotangent,
):
    rows, hidden_units = w_gate.shape
    w3 = jnp.stack([w_gate, w_up, w_down.T])
    w3 = jnp.pad(
        w3, ((0, 0), (0, sz.pad - sz.rows), (0, QUADS * sz.slice - hidden_units))
    ).reshape(3, sz.pad, QUADS, sz.slice)
    wh = w3[..., : sz.head].transpose(2, 0, 1, 3)
    wf = w3[..., sz.head :].reshape(3, sz.pad, QUADS, sz.full, WIDE).transpose(3, 2, 0, 1, 4)

    query_width, key_width = w_query.shape[1], key_weight.shape[1]
    packed = jnp.concatenate([w_query, key_weight, value_weight, w_out.T], axis=1)
    packed = lax.all_gather(packed, "dp", axis=0, tiled=True)
    cuts = (query_width, query_width + key_width, query_width + 2 * key_width)
    query_full, key_full, value_full, out_t = jnp.split(packed, cuts, axis=1)

    local_heads = query_width // HEAD_SIZE
    local_groups = key_width // HEAD_SIZE
    share = local_heads // local_groups
    factor = 1.0 / math.sqrt(HEAD_SIZE)
    cosine, sine = rope_tables(SEQUENCE_TOKENS, HEAD_SIZE)
    causal = jnp.arange(SEQUENCE_TOKENS)[:, None] >= jnp.arange(SEQUENCE_TOKENS)[None, :]
    inputs = tokens.astype(F32)
    scale_attn = rms_scale(inputs)
    normed_attention = (inputs * scale_attn * gain_attn).astype(BF)
    normed_all = lax.all_gather(normed_attention, "tensor", axis=0, tiled=True)
    total_rows = normed_all.shape[0]
    sequences = total_rows // SEQUENCE_TOKENS
    query_lin = (dot_rows(normed_all, query_full) + b_query).reshape(
        sequences, SEQUENCE_TOKENS, local_heads, HEAD_SIZE
    )
    key_linear = (dot_rows(normed_all, key_full) + key_bias).reshape(
        sequences, SEQUENCE_TOKENS, local_groups, HEAD_SIZE
    )
    value_linear = dot_rows(normed_all, value_full) + value_bias
    queries = (query_lin * cosine + rotate(query_lin) * sine).astype(BF)
    queries = queries.reshape(sequences, SEQUENCE_TOKENS, local_groups, share, HEAD_SIZE)
    keys = (key_linear * cosine + rotate(key_linear) * sine).astype(BF)
    values = value_linear.astype(BF).reshape(sequences, SEQUENCE_TOKENS, local_groups, HEAD_SIZE)

    scores = jnp.einsum("bsjgd,btjd->bjgst", queries, keys, preferred_element_type=F32) * factor
    scores = jnp.where(causal, scores, -1e30)
    largest = jnp.max(scores, axis=-1, keepdims=True)
    exponent = jnp.exp(scores - largest)
    row_totals = jnp.sum(exponent, axis=-1, keepdims=True)
    probs_low = (exponent / row_totals).astype(BF)
    mixed_heads = jnp.einsum(
        "bjgst,btjd->bsjgd", probs_low, values, preferred_element_type=F32
    ).astype(BF)
    logsum = largest + jnp.log(row_totals)
    mixed_all = mixed_heads.reshape(total_rows, query_width)
    attended = lax.psum_scatter(
        dot_right(mixed_all, out_t), "tensor", scatter_dimension=0, tiled=True
    )
    middle = inputs + attended
    scale_mlp = rms_scale(middle)
    normed_mlp = (middle * scale_mlp * gain_mlp).astype(BF)

    grad_head, grad_full, grad_normed_mlp, branch = feed_forward(
        sz, normed_mlp, cotangent, wh, wf
    )
    mixed = (middle + branch).astype(BF)
    grads = jnp.concatenate(
        [
            grad_head.transpose(1, 2, 0, 3),
            grad_full.transpose(2, 3, 1, 0, 4).reshape(3, sz.pad, QUADS, sz.full * WIDE),
        ],
        axis=-1,
    ).reshape(3, sz.pad, QUADS * sz.slice)[:, :rows, :hidden_units]
    grads = grads.astype(F32)
    grad_w_gate, grad_w_up, grad_w_down = grads[0], grads[1], grads[2].T

    upstream = cotangent.astype(F32)
    grad_middle = upstream + norm_back(middle, scale_mlp, gain_mlp, grad_normed_mlp)
    gain_mlp_term = jnp.sum(grad_normed_mlp * middle * scale_mlp, axis=0)
    grad_attended = grad_middle.astype(BF)
    grad_att_all = lax.all_gather(grad_attended, "tensor", axis=0, tiled=True)
    grad_mixed = dot_rows(grad_att_all, out_t).astype(BF)
    grad_out_part = dot_left(grad_att_all, mixed_all)
    grad_block = grad_mixed.reshape(sequences, SEQUENCE_TOKENS, local_groups, share, HEAD_SIZE)

    probs = jnp.exp(scores - logsum)
    grad_values = jnp.einsum(
        "bjgst,bsjgd->btjd", probs.astype(BF), grad_block, preferred_element_type=F32
    )
    grad_probs = jnp.einsum(
        "bsjgd,btjd->bjgst", grad_block, values, preferred_element_type=F32
    )
    inner = jnp.sum(grad_probs * probs, axis=-1, keepdims=True)
    grad_scores = (probs * (grad_probs - inner)).astype(BF)
    grad_queries = (
        jnp.einsum("bjgst,btjd->bsjgd", grad_scores, keys, preferred_element_type=F32) * factor
    )
    grad_keys = (
        jnp.einsum("bjgst,bsjgd->btjd", grad_scores, queries, preferred_element_type=F32) * factor
    )
    grad_queries = grad_queries.reshape(sequences, SEQUENCE_TOKENS, local_heads, HEAD_SIZE)
    grad_query_lin = (grad_queries * cosine - rotate(grad_queries * sine)).astype(BF)
    grad_query_lin = grad_query_lin.reshape(total_rows, query_width)
    grad_key_lin = (grad_keys * cosine - rotate(grad_keys * sine)).astype(BF)
    grad_key_lin = grad_key_lin.reshape(total_rows, key_width)
    grad_value_lin = grad_values.astype(BF).reshape(total_rows, key_width)
    grad_lin = jnp.concatenate([grad_query_lin, grad_key_lin, grad_value_lin], axis=1)
    grad_part = dot_left(normed_all, grad_lin)
    grad_normed_attn = lax.psum_scatter(
        dot_right(grad_lin, packed[:, : cuts[2]]).astype(BF),
        "tensor",
        scatter_dimension=0,
        tiled=True,
    ).astype(F32)
    grad_packed = lax.psum_scatter(
        jnp.concatenate([grad_part, grad_out_part], axis=1).astype(BF),
        "dp",
        scatter_dimension=0,
        tiled=True,
    ).astype(F32)
    grad_w_query, grad_w_key, grad_w_value, grad_w_out = jnp.split(grad_packed, cuts, axis=1)
    grad_w_out = grad_w_out.T
    grad_tokens = grad_middle + norm_back(inputs, scale_attn, gain_attn, grad_normed_attn)
    gain_attn_term = jnp.sum(grad_normed_attn * inputs * scale_attn, axis=0)
    position = lax.axis_index("tensor")

    def place(values, width):
        return lax.dynamic_update_slice(
            jnp.zeros((2 * width,), F32), values, (position * width,)
        )

    grad_gain_attn, grad_gain_mlp, query_sums, key_sums, value_sums = lax.psum(
        (
            gain_attn_term,
            gain_mlp_term,
            place(jnp.sum(grad_query_lin, axis=0, dtype=F32), query_width),
            place(jnp.sum(grad_key_lin, axis=0, dtype=F32), key_width),
            place(jnp.sum(grad_value_lin, axis=0, dtype=F32), key_width),
        ),
        ("dp", "tensor"),
    )
    grad_b_query = lax.dynamic_slice_in_dim(query_sums, position * query_width, query_width, 0)
    grad_b_key = lax.dynamic_slice_in_dim(key_sums, position * key_width, key_width, 0)
    grad_b_value = lax.dynamic_slice_in_dim(value_sums, position * key_width, key_width, 0)
    return (
        mixed,
        grad_tokens,
        grad_w_query,
        grad_w_key,
        grad_w_value,
        grad_b_query,
        grad_b_key,
        grad_b_value,
        grad_w_out,
        grad_gain_attn,
        grad_gain_mlp,
        grad_w_gate,
        grad_w_up,
        grad_w_down,
    )


def solution(mesh):
    dp = mesh.shape["dp"]

    def whole(*args):
        def shard(*blocks):
            w_gate, tokens = blocks[10], blocks[0]
            sz = Sizes(dp, w_gate.shape[0], w_gate.shape[1], tokens.shape[0])
            return per_device(sz, *blocks)

        return jax.shard_map(
            shard, mesh=mesh, in_specs=in_specs, out_specs=out_specs, check_vma=False
        )(*args)

    in_specs = (
        P(("dp", "tensor"), None),
        P("dp", "tensor"),
        P("dp", "tensor"),
        P("dp", "tensor"),
        P("tensor"),
        P("tensor"),
        P("tensor"),
        P("tensor", "dp"),
        P(),
        P(),
        P("dp", "tensor"),
        P("dp", "tensor"),
        P("tensor", "dp"),
        P(("dp", "tensor"), None),
    )
    out_specs = (
        P(("dp", "tensor"), None),
        P(("dp", "tensor"), None),
        P("dp", "tensor"),
        P("dp", "tensor"),
        P("dp", "tensor"),
        P("tensor"),
        P("tensor"),
        P("tensor"),
        P("tensor", "dp"),
        P(),
        P(),
        P("dp", "tensor"),
        P("dp", "tensor"),
        P("tensor", "dp"),
    )
    return whole
```

time: 1860 us -> 919 us (0.49)
  waiting for transfers between devices: 1520 us -> 227 us
  Pallas kernels: 0 us -> 502 us
  matrix products: 174 us -> 37.9 us
  blocking collectives: 82.7 us -> 40.3 us
  local copies, waits for them, and re-layouts: 20.5 us -> 50.4 us
    reduce_scatter x11 -> x2, waiting for transfers between devices: 1090 us -> 28.5 us  [the longest x1 28.5 us: per_device(): lax.psum_scatter(dot_right(mixed_all, out_t), 'tensor', scatter_dimension...]
    pallas_call x0 -> x1, Pallas kernels: none -> 502 us  [feed_forward(): pl.pallas_call(lambda *refs: mlp_kernel(sz, *refs), out_shape=outs, in_sp...]
    all_gather x7 -> x1, waiting for transfers between devices: 403 us -> 60.3 us  [per_device(): packed = lax.all_gather(packed, 'dp', axis=0, tiled=True)]
    all_gather x1, waiting for transfers between devices: 18.7 us -> 74 us  [per_device(): grad_att_all = lax.all_gather(grad_attended, 'tensor', axis=0, tiled=True)]
    dot_general x7 -> x2, matrix products: 57.3 us -> 4.95 us  [dot_left(): lax.dot_general(left, right, (((0,), (0,)), ((), ())), preferred_element_...]
    dot_general x7 -> x2, matrix products: 53 us -> 7.79 us  [dot_right(): lax.dot_general(left, right, (((1,), (1,)), ((), ())), preferred_element_...]
    all_gather x2 -> x0, blocking collectives: 42.7 us -> none  [the longest x1 24.1 us: per_device(): lax.all_gather(key_weight, 'dp', axis=0, tiled=True)]
    dot_general x13 -> x10, matrix products: 63.6 us -> 25.1 us  [the longest x4 11.5 us: dot_rows(): return jnp.dot(left, right, preferred_element_type=F32)]
  transfers between devices with their start and end apart: 20 -> 6, of which waited for: 17 -> 5; matrix products, arithmetic and copies ran while one was open for 7% -> 5% of each run, Pallas kernels for 0% -> 0%
where the time goes in v1:
time: 919 us; the launch traced here: 909 us
  Pallas kernels  502 us (55%)
  waiting for transfers between devices  227 us (25%)
  local copies, waits for them, and re-layouts  50.4 us (5%)
  blocking collectives  40.3 us (4%)
  matrix products  37.9 us (4%)
  other arithmetic  36 us (4%)
  between operations  15.1 us (2%)
    pallas_call x1, Pallas kernels, feed_forward(): pl.pallas_call(lambda *refs: mlp_kernel(sz, *refs), out_shape=outs, in_sp...  502 us
    all_gather x1, waiting for transfers between devices, per_device(): grad_att_all = lax.all_gather(grad_attended, 'tensor', axis=0, tiled=True)  74 us
    all_gather x1, waiting for transfers between devices, per_device(): packed = lax.all_gather(packed, 'dp', axis=0, tiled=True)  60.3 us
    psum x1, blocking collectives, per_device(): lax.psum((gain_attn_term, gain_mlp_term, place(jnp.sum(grad_query_lin, ax...  40.3 us
    unnamed x7, waiting for transfers between devices  36 us
    reduce_scatter x1, waiting for transfers between devices, per_device(): lax.psum_scatter(dot_right(mixed_all, out_t), 'tensor', scatter_dimension...  28.5 us
    all_gather x1, waiting for transfers between devices, per_device(): normed_all = lax.all_gather(normed_attention, 'tensor', axis=0, tiled=True)  27.7 us
    unnamed x91, local copies, waits for them, and re-layouts  20.3 us
  transfers between devices with their start and end apart: 6, of which 5 were waited for; matrix products, arithmetic and copies ran while one was open for 5% of the time, Pallas kernels for 0%

profile of v1, /device:TPU:0, one launch (start us, length us, event | category | flops | bytes accessed | tf_op | source)
XLA Modules:
  0.0 908.9 jit_solution(4848137253614376955)
XLA Ops:
  10.0 2.3 fusion.33
  14.6 27.7 %all-gather.4.cloned.1.call-done = bf16[512,1536]{1,0:T(8,128)(2,1)} async-done(((bf16[256,1536]{1,0:T(8,128)(2,1)}), bf16[512,1536]{1,0:T(8,128)(2,1)}) %all-gather.4.cloned.1.call-update) | async-done | bytes 1572880 | tf_op jit(solution)/shard_map/all_gather | solution.py:727
  42.4 60.3 %all-gather.6.cloned.1.call-done = bf16[1536,1792]{1,0:T(8,128)(2,1)} async-done(((bf16[96,1792]{1,0:T(8,128)(2,1)}), bf16[1536,1792]{1,0:T(8,128)(2,1)}) %all-gather.6.cloned.1.call-update) | async-done | bytes 5505040 | tf_op jit(solution)/shard_map/all_gather | solution.py:714
  102.6 2.1 convolution_add_fusion
  104.8 4.2 fusion.42
  109.0 1.9 copy.99
  113.3 3.0 copy.98
  118.4 2.6 add_convert_fusion.2
  129.0 4.8 fusion.26
  135.9 2.3 reshape.385
  140.4 2.3 reshape.403
  142.8 3.9 copy.142
  147.5 28.5 %reduce-scatter.6.cloned.1.call-done = f32[256,1536]{1,0:T(8,128)} async-done(((f32[512,1536]{1,0:T(8,128)}), f32[256,1536]{1,0:T(8,128)}) %reduce-scatter.6.cloned.1.call-update) | async-done | bytes 1572880 | tf_op jit(solution)/shard_map/reduce_scatter | solution.py:753
  179.9 502.0 %feed_forward.1 = (bf16[4,3,96,128]{3,2,1,0:T(8,128)(2,1)}, bf16[4,4,3,96,256]{4,3,2,1,0:T(8,128)(2,1)}, f32[256,1536]{1,0:T(8,128)}, f32[256,1536]{1,0:T(8,128)...) custom-call(bf16[256,1536]{1,0:T(8,128)(2,1)} %multiply_convert_fusi, ...), custom_call_target="tpu_custom_call" | custom-call | tf_op jit(solution)/shard_map/feed_forward/pallas_call | solution.py:673
  681.9 2.4 multiply_reduce_fusion
  684.8 3.9 fusion.85
  688.7 74.0 %all-gather.8.cloned.1.call-done = bf16[512,1536]{1,0:T(8,128)(2,1)} async-done(((bf16[256,1536]{1,0:T(8,128)(2,1)}), bf16[512,1536]{1,0:T(8,128)(2,1)}) %all-gather.8.cloned.1.call-update) | async-done | bytes 1572880 | tf_op jit(solution)/shard_map/all_gather | solution.py:778
  762.7 3.5 fusion.45
  766.6 4.2 convert_reduce_fusion.1
  770.8 4.2 fusion
  778.9 2.0 fusion.77
  783.5 3.0 fusion.17
  786.8 3.2 convolution_convert_fusion.1
  791.8 2.8 pad_maximum_fusion
  794.6 8.3 copy.134
  802.9 3.5 copy.115
  806.4 3.0 reshape.395
  809.3 1.9 maximum_bitcast_fusion
  811.9 2.4 slice_bitcast_fusion
  816.5 40.3 %all-reduce.1 = (f32[1536]{0:T(1024)S(1)}, f32[256]{0:T(256)S(1)}, f32[256]{0:T(256)S(1)}, f32[1536]{0:T(1024)}, f32[1536]{0:T(1024)}) all-reduce(f32[1536]{0:T(1024)S(1)} %bitcast_dynamic-update-slice_fusion, f32[256]{0:T(256)S(1)} %dynamic_update_slice.10, ...), channel_id=1, replica_groups=mesh['dp'=16,'tensor'=2] {'dp','tensor'}, use_global_device_ids=true, to_apply=%region_11.12 | all-reduce | flops 5120 | bytes 40960 | tf_op jit(solution)/shard_map/psum | solution.py:829
  858.6 2.7 fusion.30
  861.3 35.9 %reduce-scatter.10.cloned.1.call-done = bf16[96,1792]{1,0:T(8,128)(2,1)} async-done(((bf16[1536,1792]{1,0:T(8,128)(2,1)}), bf16[96,1792]{1,0:T(8,128)(2,1)}) %reduce-scatter.10.cloned.1.call-update) | async-done | bytes 344080
  (163 shorter events, 44.6 us)
Async XLA Ops:
  7.2 5.2 copy-start.21
  7.2 5.2 copy-start.27
  7.2 5.2 copy-start.28
  7.2 5.2 copy-start.22
  7.2 35.2 %all-gather.4.cloned.1.call-start = ((), (), s32[]{:S(2)}) async-start(), calls=%async_computation.3 | async-start | bytes 2359296 | tf_op jit(solution)/shard_map/all_gather | solution.py:727
  8.7 4.5 copy-start.34
  8.7 4.5 copy-start.35
  8.7 5.0 copy-start.33
  9.3 4.6 copy-start.29
  10.0 3.9 copy-start.25
  12.3 90.3 %all-gather.6.cloned.1.call-start = ((), (), s32[]{:S(2)}) async-start(), calls=%async_computation.4 | async-start | bytes 5849088 | tf_op jit(solution)/shard_map/all_gather | solution.py:714
  13.2 162.8 %reduce-scatter.6.cloned.1.call-start = ((), (), s32[]{:S(2)}) async-start(), calls=%async_computation.5 | async-start | bytes 4718592 | tf_op jit(solution)/shard_map/reduce_scatter | solution.py:753
  42.4 62.4 %copy-start.14 = (bf16[512,1536]{1,0:T(8,128)(2,1)S(1)}, bf16[512,1536]{1,0:T(8,128)(2,1)}, u32[]{:S(2)}) copy-start(bf16[512,1536]{1,0:T(8,128)(2,1)} %all-gather.4.cloned.1.call-done) | copy-start | bytes 4718596
  110.9 5.4 copy-start.4
  111.9 4.4 copy-start.8
  111.9 4.6 copy-start.12
  111.9 9.3 %copy-start.17 = (bf16[512,128,1]{0,1,2:T(8,128)(2,1)}, bf16[512,128,1]{0,1,2:T(8,128)(2,1)S(1)}, u32[]{:S(2)}) copy-start(bf16[512,128,1]{0,1,2:T(8,128)(2,1)S(1)} %get-tuple-element.110) | copy-start | bytes 393220
  116.7 4.2 copy-start.6
  122.5 4.3 copy-start
  133.9 628.9 %all-gather.8.cloned.1.call-start = ((), (), s32[]{:S(2)}) async-start(), calls=%async_computation.6 | async-start | bytes 2359296 | tf_op jit(solution)/shard_map/all_gather | solution.py:778
  142.8 3.9 slice-start.2
  142.8 33.2 %copy-start.3 = (bf16[256,1536]{1,0:T(8,128)(2,1)S(1)}, bf16[256,1536]{1,0:T(8,128)(2,1)}, u32[]{:S(2)}) copy-start(bf16[256,1536]{1,0:T(8,128)(2,1)} %param.14) | copy-start | bytes 2359300
  688.6 126.2 %reduce-scatter.8.cloned.1.call-start = ((), (), s32[]{:S(2)}) async-start(), calls=%async_computation.7 | async-start | bytes 2359296 | tf_op jit(solution)/shard_map/reduce_scatter | solution.py:806
  766.5 4.2 copy-start.24
  766.5 8.5 slice-start
  770.8 4.3 slice-start.1
  786.5 3.4 copy-start.16
  786.5 110.7 %reduce-scatter.10.cloned.1.call-start = ((), (), s32[]{:S(2)}) async-start(), calls=%async_computation.8 | async-start | bytes 5849088
  806.4 3.0 copy-start.20
  811.9 3.0 copy-start.26
  811.9 46.7 %copy-start.31 = (f32[256]{0:T(256)S(1)}, f32[256]{0:T(256)}, u32[]{:S(2)}) copy-start(f32[256]{0:T(256)} %get-tuple-element.112) | copy-start | bytes 3076
  814.4 44.2 %copy-start.10 = (f32[256,1536]{1,0:T(8,128)S(1)}, f32[256,1536]{1,0:T(8,128)}, u32[]{:S(2)}) copy-start(f32[256,1536]{1,0:T(8,128)} %get-tuple-element.90) | copy-start | bytes 4718596
  (18 other events, 35.1 us)
Sparse Core Ops, SparseCore 0:
  12.4 29.8 all-gather.3
  45.2 57.3 all-gather.5
  134.0 41.9 reduce-scatter.5
  688.7 73.9 all-gather.7
  786.6 26.0 reduce-scatter.7
  816.5 80.6 reduce-scatter.9

commit v2 on v0

v2 whole, which is shorter than its diff:
```python
import math

import jax
import jax.numpy as jnp
from jax import lax
from jax.experimental import pallas as pl
from jax.experimental.pallas import tpu as pltpu
from jax.sharding import PartitionSpec as P

QUERY_HEADS = 12
KEY_VALUE_HEADS = 2
HEAD_SIZE = 128
SEQUENCE_TOKENS = 512

QUADS = 4
WIDE = 256

norm_eps = 1e-06
rope_base = 1000000.0
BF = jnp.bfloat16
F32 = jnp.float32
MESH = pl.DeviceIdType.MESH


def rope_tables(length, columns):
    midway = columns // 2
    inverse = jnp.exp(
        jnp.arange(midway, dtype=jnp.float32) * (-2.0 * math.log(rope_base) / columns)
    )
    angles = jnp.arange(length, dtype=jnp.float32)[:, None] * inverse[None, :]
    angles = jnp.concatenate([angles, angles], axis=-1)
    return (jnp.cos(angles)[None, :, None, :], jnp.sin(angles)[None, :, None, :])


def dot_rows(left, right):
    return jnp.dot(left, right, preferred_element_type=F32)


def dot_left(left, right):
    return lax.dot_general(left, right, (((0,), (0,)), ((), ())), preferred_element_type=F32)


def dot_right(left, right):
    return lax.dot_general(left, right, (((1,), (1,)), ((), ())), preferred_element_type=F32)


def round_up(value, step):
    return (value + step - 1) // step * step


class Sizes:
    def __init__(self, dp, gate_shape, tokens, query, key):
        self.dp = dp
        self.outer = dp // QUADS
        self.rows, self.hidden = gate_shape
        self.pad = round_up(self.rows, 16)
        self.whole = self.pad == self.rows
        self.wide = dp * self.rows
        self.slice = round_up(-(-self.hidden // QUADS), 128)
        self.head = self.slice % WIDE or WIDE
        self.full = (self.slice - self.head) // WIDE
        self.tokens, self.query, self.key = tokens, query, key


def layer_kernel(sz, *refs):
    refs = iter(refs)

    def some(n):
        return [next(refs) for _ in range(n)]

    tok_ref, cot_ref, wq_ref, wo_ref, wh_ref, wf_ref, vec, rope = some(8)
    gh_ref, gf_ref, gaq_ref, gao_ref, mixed_ref, gtok_ref, sums_ref = some(7)
    wagh, wagf, colh, colf, nearh, nearf, outh, outf = some(8)
    pairbuf, chipbuf, gq, go = some(4)
    rcq, rco, rxq, rxo, colq, colo, nearq, nearo, outq, outo = some(10)
    abh, abf = (None, None) if sz.whole else some(2)
    xb, cb, nacc, wv, pbh, pb, hh, hf, gu, nsd, tk, rt, own = some(13)
    xa, qkv, mh, ar, st, mid, ga, sv, svr, svz = some(10)
    s_a2a, r_a2a, s_own, r_own, s_far, r_far, s_fwd, r_fwd = some(8)
    s_col, r_col, s_nr, r_nr, s_out, r_out, s_fin, r_fin = some(8)
    s_tok, r_tok, s_sum, r_sum, s_y, r_y, s_gz, r_gz, s_gx, r_gx, s_gc, r_gc = some(12)
    s_pc, r_pc, s_px, r_px, s_v, r_v, s_vz, r_vz, loc = some(9)
    stage, joined = (None, None) if sz.whole else some(2)

    O, NF, T = sz.outer, sz.full, sz.tokens
    H = O // 2
    HK, W, R, RP = sz.head, sz.wide, sz.rows, sz.pad
    R4, LR = QUADS * R, O * RP
    QW = sz.query
    GW = sz.query + 2 * sz.key
    HEADS = QW // HEAD_SIZE
    FACTOR = 1.0 / math.sqrt(HEAD_SIZE)
    me = lax.axis_index("dp")
    y = lax.axis_index("tensor")
    o, q = me // QUADS, me % QUADS
    x, c = q // 2, q % 2
    half, pos = o // H, o % H
    base, far = half * H, (1 - half) * H
    middle_pos = (1 - half) * (H - 1)
    is_middle = pos == middle_pos

    def at(o_, q_, y_):
        return (o_ * QUADS + q_, y_)

    mid_dev = at(base + middle_pos, q, y)
    far_mid = at(far + half * (H - 1), q, y)
    core = at(o, x * 2 + 1 - c, y)
    over_x = at(o, (1 - x) * 2 + c, y)
    over_y = at(o, q, 1 - y)
    chips = [(1 - x, 1 - y), (1 - x, y), (x, 1 - y)]
    order = chips + [(x, y)]

    def remote(src, dst, ssem, rsem, dev):
        return pltpu.make_async_remote_copy(
            src_ref=src, dst_ref=dst, send_sem=ssem, recv_sem=rsem,
            device_id=dev, device_id_type=MESH,
        )

    def local(src, dst, sem):
        return pltpu.make_async_copy(src, dst, sem)

    def move(src, dst, sem):
        local(src, dst, sem).start()
        local(src, dst, sem).wait()

    def span(start, size, unit):
        return pl.ds(pl.multiple_of(start, unit), size)

    def loop(n, step):
        def run(i, carry):
            step(i)
            return carry

        lax.fori_loop(0, n, run, 0)

    bar = pltpu.get_barrier_semaphore()

    def greet(dev):
        pl.semaphore_signal(bar, inc=1, device_id=dev, device_id_type=MESH)

    for dq in range(QUADS):
        for yy in range(2):
            if dq or yy:
                greet(at(o, lax.rem(q + dq, QUADS), (y + yy) % 2))
    for step in range(1, O):
        greet(at(lax.rem(o + step, O), q, y))
    pl.semaphore_wait(bar, 2 * QUADS - 1 + O - 1)

    def add_into(dst, src, n):
        rows = 32

        def step(i):
            here = span(i * rows, rows, rows)
            dst[here, :] = (dst[here, :].astype(F32) + src[here, :].astype(F32)).astype(BF)

        loop(n // rows, step)

    class Line:
        def __init__(self, i, rows, pieces, col, near, out, temps):
            self.i, self.rows, self.pieces = i, rows, pieces
            self.col, self.near_, self.out, self.temps = col, near, out, temps

        def block(self, k, b, n=1):
            return self.pieces[k].at[span(b * self.rows, n * self.rows, self.rows), :]

        def temp(self, k, start, n):
            return self.temps[k].at[pl.ds(start * self.rows, n * self.rows), :]

        def to_middle(self, k, t):
            return remote(
                self.block(k, far, H), self.col[k].at[t],
                s_col.at[self.i + k], r_col.at[self.i + k, t], mid_dev,
            )

        def near(self, k, to, t):
            return remote(
                self.block(k, base + to), self.near_[k].at[t],
                s_nr.at[self.i + k, to], r_nr.at[self.i + k, t], at(base + to, q, y),
            )

        def cross(self, k, to):
            return remote(
                self.block(k, far + to), self.out[k],
                s_out.at[self.i + k, to], r_out.at[self.i + k], at(far + to, q, y),
            )

        def first(self):
            for k in range(len(self.pieces)):
                pl.when(jnp.logical_not(is_middle))(lambda: self.to_middle(k, pos).start())
                for t in range(H):
                    pl.when(pos != t)(lambda: self.near(k, t, pos).start())

        def middle(self):
            ks = range(len(self.pieces))

            @pl.when(is_middle)
            def _():
                for t in range(H):

                    @pl.when(pos != t)
                    def _():
                        for k in ks:
                            self.to_middle(k, t).wait_recv()
                            local(self.col[k].at[t], self.temp(k, 0, H), loc.at[4 + k]).start()
                        for k in ks:
                            local(self.col[k].at[t], self.temp(k, 0, H), loc.at[4 + k]).wait()
                            add_into(self.block(k, far, H), self.temp(k, 0, H), H * self.rows)

                for k in ks:
                    for t in range(H):
                        self.cross(k, t).start()

        def last(self):
            ks = range(len(self.pieces))
            for t in range(H):

                @pl.when(pos != t)
                def _():
                    for k in ks:
                        self.near(k, pos, t).wait_recv()
                        local(self.near_[k].at[t], self.temp(k, 0, 1), loc.at[4 + k]).start()
                    for k in ks:
                        local(self.near_[k].at[t], self.temp(k, 0, 1), loc.at[4 + k]).wait()
                        add_into(self.block(k, o), self.temp(k, 0, 1), self.rows)

            for k in ks:
                self.cross(k, pos).wait_recv()
                local(self.out[k], self.temp(k, 1, 1), loc.at[4 + k]).start()
            for k in ks:
                local(self.out[k], self.temp(k, 1, 1), loc.at[4 + k]).wait()
                add_into(self.block(k, o), self.temp(k, 1, 1), self.rows)

        def sent(self):
            for k in range(len(self.pieces)):
                pl.when(jnp.logical_not(is_middle))(lambda: self.to_middle(k, pos).wait_send())
                for t in range(H):
                    pl.when(pos != t)(lambda: self.near(k, t, pos).wait_send())
                    pl.when(is_middle)(lambda: self.cross(k, t).wait_send())

    class Chunk:
        def __init__(self, kk):
            self.head = kk is None
            if self.head:
                self.i, self.fk = 0, HK
                self.src, self.wag, self.pb, self.out = wh_ref, wagh, pbh, gh_ref
                self.hid, self.ab = hh, abh
                col, near, out = colh, nearh, outh
            else:
                self.i, self.fk = kk + 1, WIDE
                self.src, self.wag, self.pb, self.out = (
                    wf_ref.at[kk], wagf.at[kk], pb.at[kk], gf_ref.at[kk],
                )
                self.hid, self.ab = hf.at[kk], None if abf is None else abf.at[kk]
                col, near, out = colf.at[kk], nearf.at[kk], outf.at[kk]
            self.cols = pl.ds(0, 3 * self.fk)
            self.wv = wv.at[:, self.cols]
            self.line = Line(self.i, R4, [self.pb], [col], [near], [out], [rt.at[:, self.cols]])

        def block(self, ref, b, n=1):
            return ref.at[span(b * R4, n * R4, R4), :]

        def part(self, ref, b, q_):
            return ref.at[span((b * QUADS + q_) * R, R, R), :]

        def mine(self):
            return self.part(self.wag, o, q) if sz.whole else self.ab.at[q]

        def a2a(self, dq):
            to = lax.rem(q + dq, QUADS)
            return remote(
                self.src.at[to], self.mine(),
                s_a2a.at[self.i, dq - 1], r_a2a.at[self.i, dq - 1], at(o, to, y),
            )

        def a2a_own(self):
            return local(self.src.at[q], self.mine(), s_a2a.at[self.i, 3])

        def a2a_start(self):
            self.a2a_own().start()
            for dq in (1, 2, 3):
                self.a2a(dq).start()

        def join(self):
            for i in range(QUADS):
                move(self.ab.at[i], stage.at[pl.ds(i * RP, RP), self.cols], loc.at[3])
            rows = [stage[i * RP : i * RP + RP, self.cols].astype(F32)[:R] for i in range(QUADS)]
            joined[:, self.cols] = jnp.concatenate(rows, axis=0).astype(BF)
            move(joined.at[:, self.cols], self.block(self.wag, o), loc.at[3])

        def own_to(self, to, t):
            return remote(
                self.block(self.wag, base + t), self.block(self.wag, base + t),
                s_own.at[self.i, to], r_own.at[self.i, t], at(base + to, q, y),
            )

        def own_far(self, half_, t):
            b = half_ * H + t
            return remote(
                self.block(self.wag, b), self.block(self.wag, b),
                s_far.at[self.i], r_far.at[self.i, t], far_mid,
            )

        def forward(self, half_, to):
            rows = self.block(self.wag, half_ * H, H)
            return remote(
                rows, rows, s_fwd.at[self.i, to], r_fwd.at[self.i], at(base + to, q, y),
            )

        def gather_own(self):
            self.a2a_own().wait()
            for dq in (1, 2, 3):
                self.a2a(dq).wait_recv()
            if not sz.whole:
                self.join()
            self.own_far(half, pos).start()
            for t in range(H):
                pl.when(pos != t)(lambda: self.own_to(t, pos).start())

        def gather_middle(self):
            @pl.when(is_middle)
            def _():
                for t in range(H):
                    self.own_far(1 - half, t).wait_recv()
                for t in range(H):
                    pl.when(pos != t)(lambda: self.forward(1 - half, t).start())

        def gather_wait(self):
            for t in range(H):
                pl.when(pos != t)(lambda: self.own_to(pos, t).wait_recv())
            pl.when(jnp.logical_not(is_middle))(lambda: self.forward(1 - half, pos).wait_recv())

        def gather_sent(self):
            for dq in (1, 2, 3):
                self.a2a(dq).wait_send()
            self.own_far(half, pos).wait_send()
            for t in range(H):

                @pl.when(pos != t)
                def _():
                    self.own_to(t, pos).wait_send()
                    pl.when(is_middle)(lambda: self.forward(1 - half, t).wait_send())

        def load(self):
            return local(self.wag, self.wv, loc.at[0])

        def result(self, q_):
            return self.part(self.pb, o, q_) if sz.whole else self.ab.at[q_]

        def give(self, dq):
            to = lax.rem(q + dq, QUADS)
            return remote(
                self.result(to), self.out.at[q],
                s_fin.at[self.i, dq - 1], r_fin.at[self.i, dq - 1], at(o, to, y),
            )

        def give_own(self):
            return local(self.result(q), self.out.at[q], s_fin.at[self.i, 3])

        def split(self):
            rows = self.block(self.pb, o)[...].astype(F32)
            for i in range(QUADS):
                part = rows[i * R : (i + 1) * R]
                part = jnp.concatenate([part, jnp.zeros((RP - R, 3 * self.fk), F32)], axis=0)
                stage[i * RP : i * RP + RP, self.cols] = part.astype(BF)
            for i in range(QUADS):
                move(stage.at[pl.ds(i * RP, RP), self.cols], self.ab.at[i], loc.at[3])

        def finish(self):
            self.line.last()
            if not sz.whole:
                self.split()
            self.give_own().start()
            for dq in (1, 2, 3):
                self.give(dq).start()

        def finished(self):
            self.give_own().wait()
            for dq in (1, 2, 3):
                self.give(dq).wait()
            self.gather_sent()
            self.line.sent()

    def chip_rows(xx, yy):
        return span((xx * 2 + yy) * (2 * T), 2 * T, 2 * T)

    def rows_of(xx, yy, cc):
        return span(((xx * 2 + yy) * 2 + cc) * T, T, T)

    mine = rows_of(x, y, c)

    def tok(src, buf, which, n):
        dev = core if n == 3 else at(o, chips[n][0] * 2 + c, chips[n][1])
        return remote(src, buf.at[mine, :], s_tok.at[which, n], r_tok.at[which, n], dev)

    def tok_pass(buf, which, n):
        rows = rows_of(*chips[n], c)
        return remote(
            buf.at[rows, :], buf.at[rows, :],
            s_tok.at[which, 4 + n], r_tok.at[which, 4 + n], core,
        )

    def tok_start(src, buf, which):
        for n in (3, 2, 1, 0):
            tok(src, buf, which, n).start()

    def tok_take(src, buf, which, n):
        tok(src, buf, which, n).wait_recv()
        if n < 3:
            tok_pass(buf, which, n).start()
            tok_pass(buf, which, n).wait_recv()

    def tok_sent(src, buf, which):
        for n in range(4):
            tok(src, buf, which, n).wait_send()
        for n in range(3):
            tok_pass(buf, which, n).wait_send()

    def sum_pair(n, which):
        return remote(
            nacc.at[rows_of(*order[n], 1 - c), :], pairbuf.at[which, n],
            s_sum.at[which, n], r_sum.at[which, n], core,
        )

    def sum_chip(n, which):
        xx, yy = chips[n]
        return remote(
            nsd.at[n], chipbuf.at[which, n],
            s_sum.at[which, 4 + n], r_sum.at[which, 4 + n], at(o, xx * 2 + c, yy),
        )

    def sum_mid(n, which):
        here, spare = nacc.at[rows_of(*order[n], c), :], nacc.at[rows_of(*order[n], 1 - c), :]
        sum_pair(n, which).wait()
        move(pairbuf.at[which, n], spare, loc.at[7])

        def step(i):
            a = span(i * 32, 32, 32)
            total = here[a, :] + spare[a, :]
            if n < 3:
                nsd[n, a, :] = total.astype(BF)
            else:
                here[a, :] = total

        loop(T // 32, step)
        if n < 3:
            sum_chip(n, which).start()

    def sum_close(which, finish):
        here = nacc.at[mine, :]
        for n in range(3):
            sum_chip(n, which).wait_recv()
            move(chipbuf.at[which, n], tk, loc.at[7])

            def step(i):
                a = span(i * 32, 32, 32)
                total = here[a, :] + tk[a, :].astype(F32)
                if n < 2:
                    here[a, :] = total
                else:
                    finish(a, total)

            loop(T // 32, step)
        for n in range(3):
            sum_chip(n, which).wait_send()

    class Gather:
        def __init__(self, i, src, buf):
            self.i, self.src, self.buf = i, src, buf

        def rows(self, o_, x_, c_):
            return self.buf.at[span(((o_ * 2 + x_) * 2 + c_) * RP, RP, RP), :]

        def place(self, step):
            return lax.rem(o - step + O, O)

        def send(self, step):
            return remote(
                self.src, self.rows(o, x, c), s_gz.at[self.i, step], r_gz.at[self.i, step],
                at(lax.rem(o + step, O), q, y),
            )

        def over(self, step):
            rows = self.rows(self.place(step), x, c)
            src = self.src if step == 0 else rows
            return remote(src, rows, s_gx.at[self.i, step], r_gx.at[self.i, step], over_x)

        def across(self, step, far_x):
            rows = self.rows(self.place(step), (1 - x) if far_x else x, c)
            src = self.src if step == 0 and not far_x else rows
            return remote(
                src, rows, s_gc.at[self.i, far_x, step], r_gc.at[self.i, far_x, step], core,
            )

        def own(self):
            return local(self.src, self.rows(o, x, c), s_gz.at[self.i, 0])

        def start(self):
            for step in range(1, O):
                self.send(step).start()
            self.over(0).start()
            self.across(0, 0).start()
            self.own().start()

        def pass_on(self):
            for step in range(1, O):
                self.send(step).wait_recv()
                self.over(step).start()
                self.across(step, 0).start()

        def pass_over(self):
            for step in range(O):
                self.over(step).wait_recv()
                self.across(step, 1).start()

        def wait(self):
            for far_x in range(2):
                for step in range(O):
                    self.across(step, far_x).wait_recv()
            self.own().wait()

        def sent(self):
            for step in range(1, O):
                self.send(step).wait_send()
            for step in range(O):
                self.over(step).wait_send()
                self.across(step, 0).wait_send()
                self.across(step, 1).wait_send()

    def fetch(parts, sem):
        if sz.whole:
            copies = [local(buf.at[:, cols], dst, loc.at[sem + i]) for i, (buf, cols, dst) in enumerate(parts)]
            for copy in copies:
                copy.start()

            def wait():
                for copy in copies:
                    copy.wait()

            return wait
        for buf, cols, dst in parts:
            n = dst.shape[-1]

            def step(b):
                rows = span(b * QUADS * RP, QUADS * RP, QUADS * RP)
                move(buf.at[rows, cols], stage.at[:, pl.ds(0, n)], loc.at[sem])
                part = [stage[i * RP : i * RP + RP, :n].astype(F32)[:R] for i in range(QUADS)]
                dst[span(b * R4, R4, R4), :] = jnp.concatenate(part, axis=0).astype(BF)

            loop(O, step)
        return lambda: None

    def y_copy(src, dst, i):
        return remote(src, dst, s_y.at[i], r_y.at[i], over_y)

    QUERY, KEY, VALUE = pl.ds(0, QW), pl.ds(QW, sz.key), pl.ds(QW + sz.key, sz.key)
    REST = pl.ds(QW, 2 * sz.key)
    TT = 2 * T
    seq = TT // 2

    def head_cols(h):
        return pl.ds(h * HEAD_SIZE, HEAD_SIZE)

    def turn(u, sign, rows):
        return u * rope[0, rows, :] + sign * pltpu.roll(u, HEAD_SIZE // 2, 1) * rope[1, rows, :]

    gather_q = Gather(0, wq_ref, gq)
    gather_o = Gather(1, wo_ref, go)
    head = Chunk(None)

    gather_q.start()
    local(tok_ref, tk, loc.at[1]).start()
    gather_o.start()
    local(tok_ref, tk, loc.at[1]).wait()

    def norm_first(i):
        a = span(i * 32, 32, 32)
        values = tk[a, :].astype(F32)
        scale = lax.rsqrt(jnp.mean(values * values, axis=-1, keepdims=True) + norm_eps)
        xa[span(y * T + i * 32, 32, 32), :] = (values * scale * vec[0:1, :]).astype(BF)

    loop(T // 32, norm_first)
    own_half, other_half = span(y * T, T, T), span((1 - y) * T, T, T)
    y_copy(xa.at[own_half, :], xa.at[own_half, :], 0).start()
    sv[...] = jnp.zeros_like(sv)
    gather_q.pass_on()
    gather_q.pass_over()
    gather_q.wait()
    wq_v, wr_v, wo_v = pb.at[0], pb.at[1, :, pl.ds(0, 2 * sz.key)], pb.at[2]
    ready = fetch([(gq, QUERY, wq_v), (gq, REST, wr_v)], 1)
    head.a2a_start()
    if NF > 0:
        Chunk(0).a2a_start()
    y_copy(xa.at[own_half, :], xa.at[other_half, :], 0).wait_recv()
    ready()

    def project(i):
        rows = span(i * seq, seq, seq)
        lin = dot_rows(xa[rows, :], wq_v[...]) + vec[2:3, :QW]
        for h in range(HEADS):
            qkv[rows, head_cols(h)] = turn(lin[:, h * HEAD_SIZE : (h + 1) * HEAD_SIZE], 1.0, rows).astype(BF)
        lin = dot_rows(xa[rows, :], wr_v[...]) + vec[2:3, QW:GW]
        for h in range(sz.key // HEAD_SIZE):
            cut = slice(h * HEAD_SIZE, (h + 1) * HEAD_SIZE)
            qkv[rows, head_cols(HEADS + h)] = turn(lin[:, cut], 1.0, rows).astype(BF)
        qkv[rows, VALUE] = lin[:, sz.key :].astype(BF)

    loop(2, project)
    gather_o.pass_on()
    head.gather_own()
    SHARE = QW // sz.key

    def chances(h, part, queries):
        keys = slice(0, (part + 1) * seq)
        kcol = span(QW + (h // SHARE) * HEAD_SIZE, HEAD_SIZE, HEAD_SIZE)
        scores = dot_right(queries, qkv[keys, kcol]) * FACTOR
        row = lax.broadcasted_iota(jnp.int32, scores.shape, 0) + part * seq
        col = lax.broadcasted_iota(jnp.int32, scores.shape, 1)
        scores = jnp.where(row >= col, scores, -1e30)
        exponent = jnp.exp(scores - jnp.max(scores, axis=-1, keepdims=True))
        return exponent / jnp.sum(exponent, axis=-1, keepdims=True)

    def attend(h):
        qcol = span(h * HEAD_SIZE, HEAD_SIZE, HEAD_SIZE)
        vcol = span(QW + sz.key + (h // SHARE) * HEAD_SIZE, HEAD_SIZE, HEAD_SIZE)
        for part in range(2):
            rows = slice(part * seq, (part + 1) * seq)
            probs = chances(h, part, qkv[rows, qcol]).astype(BF)
            mh[rows, qcol] = dot_rows(probs, qkv[0 : (part + 1) * seq, vcol]).astype(BF)

    loop(HEADS, attend)
    gather_o.pass_over()
    gather_o.wait()
    ready = fetch([(go, pl.ds(0, QW), wo_v)], 1)
    if NF > 0:
        Chunk(0).gather_own()
    ready()
    st[...] = dot_right(mh[other_half, :], wo_v[...]).astype(BF)
    y_copy(st, ar.at[0], 1).start()
    tok_start(cot_ref, cb, 1)
    local(cot_ref, cb.at[mine, :], loc.at[1]).start()
    mid[...] = dot_right(mh[own_half, :], wo_v[...]) + tk[...].astype(F32)
    for kk in range(1, NF):
        Chunk(kk).a2a_start()
    head.gather_middle()
    y_copy(st, ar.at[0], 1).wait_recv()

    def norm_second(i):
        a = span(i * 32, 32, 32)
        values = mid[a, :] + ar[0, a, :].astype(F32)
        mid[a, :] = values
        scale = lax.rsqrt(jnp.mean(values * values, axis=-1, keepdims=True) + norm_eps)
        xb[span(((x * 2 + y) * 2 + c) * T + i * 32, 32, 32), :] = (values * scale * vec[1:2, :]).astype(BF)

    loop(T // 32, norm_second)

    xsrc = xb.at[mine, :]
    tok_start(xsrc, xb, 0)
    local(cot_ref, cb.at[mine, :], loc.at[1]).wait()
    for n in (3, 2, 1, 0):
        tok_take(cot_ref, cb, 1, n)
    if NF > 1:
        Chunk(1).gather_own()
    head.gather_wait()
    head.load().start()
    if NF > 0:
        Chunk(0).gather_middle()
    head.load().wait()

    def tile(ch, rows, first):
        fk = ch.fk
        both = dot_rows(xb[rows, :], ch.wv[:, : 2 * fk])
        back = dot_rows(cb[rows, :], ch.wv[:, 2 * fk :])
        gate, upper = both[:, :fk], both[:, fk:]
        sigma = jax.nn.sigmoid(gate)
        silu = gate * sigma
        ch.hid[rows, :] = (silu * upper).astype(BF)
        gu[rows, :fk] = (back * upper * (sigma * (1.0 + gate * (1.0 - sigma)))).astype(BF)
        gu[rows, fk : 2 * fk] = (back * silu).astype(BF)
        for j in range(0, W, 512):
            cols = slice(j, j + 512)
            total = dot_right(gu[rows, : 2 * fk], ch.wv[cols, : 2 * fk])
            if first:
                nacc[rows, cols] = total
            else:
                nacc[rows, cols] = nacc[rows, cols] + total

    TD = 512 if W % 512 == 0 else 256

    def products(ch):
        fk = ch.fk

        def step(i):
            cols = span(i * TD, TD, TD)
            ch.pb[cols, : 2 * fk] = dot_left(xb[:, cols], gu[:, : 2 * fk]).astype(BF)
            ch.pb[cols, 2 * fk :] = dot_left(cb[:, cols], ch.hid[...]).astype(BF)

        loop(W // TD, step)

    for n in (3, 2, 1, 0):
        tok_take(xsrc, xb, 0, n)
        tile(head, chip_rows(*order[n]), True)
    if NF > 0:
        Chunk(0).gather_wait()
        Chunk(0).load().start()
    products(head)
    head.line.first()

    def body(kk):
        ch, nxt = Chunk(kk), Chunk(lax.min(kk + 1, NF - 1))
        before, two = Chunk(lax.max(kk - 1, 0)), Chunk(lax.max(kk - 2, 0))
        last = kk == NF - 1
        pl.when(kk + 2 < NF)(lambda: Chunk(lax.min(kk + 2, NF - 1)).gather_own())
        ch.load().wait()

        def visit(p):
            xx = jnp.where(p < 2, 1 - x, x)
            yy = jnp.where(p % 2 == 0, 1 - y, y)
            tile(ch, chip_rows(xx, yy), False)

            @pl.when(last)
            def _():
                for n in range(4):
                    pl.when(p == n)(lambda: sum_pair(n, 0).start())
                for n in range(3):
                    pl.when(p == n + 1)(lambda: sum_mid(n, 0))

        loop(4, visit)
        pl.when(last)(lambda: sum_mid(3, 0))
        pl.when(kk < NF - 1)(lambda: nxt.gather_middle())
        products(ch)
        ch.line.first()
        pl.when(kk == 0)(lambda: head.line.middle())
        pl.when(kk == 1)(lambda: head.finish())
        pl.when((kk >= 1) & (kk < NF - 1))(lambda: before.line.middle())
        pl.when((kk >= 2) & (kk < NF - 1))(lambda: two.finish())

        @pl.when(kk < NF - 1)
        def _():
            nxt.gather_wait()
            nxt.load().start()

    loop(NF, body)

    y_copy(st, ar.at[0], 1).wait_send()
    local(cot_ref, st, loc.at[1]).start()
    wo_b, wq_b = cb.at[pl.ds(0, W), pl.ds(0, QW)], xb.at[pl.ds(0, W), pl.ds(0, GW)]
    tok_sent(cot_ref, cb, 1)
    tok_sent(xsrc, xb, 0)
    ready = fetch([(go, pl.ds(0, QW), wo_b), (gq, pl.ds(0, GW), wq_b)], 2)
    local(cot_ref, st, loc.at[1]).wait()

    def back_second(a, grad):
        values = mid[a, :]
        scale = lax.rsqrt(jnp.mean(values * values, axis=-1, keepdims=True) + norm_eps)
        scaled = grad * vec[1:2, :]
        mean = jnp.mean(scaled * values, axis=-1, keepdims=True)
        total = st[a, :].astype(F32) + (scale * scaled - values * (scale * scale * scale) * mean)
        own[a, :] = total
        tk[a, :] = total.astype(BF)
        sv[1:2, :] = sv[1:2, :] + jnp.sum(grad * values * scale, axis=0, keepdims=True)

    sum_close(0, back_second)
    ga[own_half, :] = tk[...]
    y_copy(ga.at[own_half, :], ga.at[own_half, :], 2).start()
    if NF > 1:
        Chunk(NF - 2).line.middle()

    def m_load(kk):
        return local(
            wagf.at[kk, :, pl.ds(2 * WIDE, WIDE)], wv.at[:, span(lax.rem(kk, 2) * WIDE, WIDE, WIDE)], loc.at[8],
        )

    local(wagh.at[:, pl.ds(2 * HK, HK)], wv.at[:, pl.ds(2 * WIDE, HK)], loc.at[0]).start()
    local(wagh.at[:, pl.ds(2 * HK, HK)], wv.at[:, pl.ds(2 * WIDE, HK)], loc.at[0]).wait()
    m_load(0).start()

    def m_first(p):
        rows = span(p * TT, TT, TT)
        nacc[rows, :] = dot_right(hh[rows, :], wv[:, 2 * WIDE : 2 * WIDE + HK])

    loop(4, m_first)

    def m_chunk(kk):
        m_load(kk).wait()
        pl.when(kk + 1 < NF)(lambda: m_load(lax.min(kk + 1, NF - 1)).start())
        cut = span(lax.rem(kk, 2) * WIDE, WIDE, WIDE)

        def m_tile(p):
            rows = span(p * TT, TT, TT)
            for j in range(0, W, 512):
                cols = slice(j, j + 512)
                nacc[rows, cols] = nacc[rows, cols] + dot_right(hf[kk, rows, :], wv[cols, cut])

        loop(4, m_tile)

    loop(NF, m_chunk)
    for n in range(4):
        sum_pair(n, 1).start()
    for n in range(4):
        sum_mid(n, 1)
    ready()
    y_copy(ga.at[own_half, :], ga.at[other_half, :], 2).wait_recv()

    PER = 2 * WIDE // HEAD_SIZE

    def cell(h, level):
        return (level * 2 + h // PER) * TT, span(h % PER * HEAD_SIZE, HEAD_SIZE, HEAD_SIZE)

    grad_mixed = dot_rows(ga[...], wo_b[...]).astype(BF)
    for h in range(HEADS):
        row, cut = cell(h, 1)
        gu[pl.ds(row, TT), cut] = grad_mixed[:, h * HEAD_SIZE : (h + 1) * HEAD_SIZE]

    HR = 2 * LR
    tile_rows = R4 * 128 // math.gcd(R4, 128)
    quads = tile_rows // R4

    def spread_rows(i, values, store):
        for b in range(quads):
            for q_ in range(QUADS):
                rows = values[(b * QUADS + q_) * R : (b * QUADS + q_ + 1) * R]
                if not sz.whole:
                    rows = jnp.concatenate([rows, jnp.zeros((RP - R, rows.shape[1]), F32)], axis=0)
                where = ((q_ % 2) * 2 + q_ // 2) * O + i * quads + b
                store(span(where * RP, RP, RP), rows.astype(BF))

    out_cols = pl.ds(QW, QW)

    def out_products(i):
        cols = span(i * tile_rows, tile_rows, 128)
        values = dot_left(ga[:, cols], mh[...])

        def store(rows, part):
            cb[rows, out_cols] = part

        spread_rows(i, values, store)

    loop(W // tile_rows, out_products)

    class Part:
        def __init__(self, i, pieces, temps, cores, overs, col, near, out):
            self.i, self.pieces, self.temps, self.cores, self.overs = i, pieces, temps, cores, overs
            first = (c * 2 + x) * LR
            self.line = Line(
                NF + 1 + i, RP, [p.at[span(first, LR, RP), :] for p in pieces], col, near, out, temps
            )

        def to_core(self, k):
            rows = span((1 - c) * HR, HR, RP)
            return remote(
                self.pieces[k].at[rows, :], self.cores[k], s_pc.at[self.i + k], r_pc.at[self.i + k], core
            )

        def to_x(self, k):
            rows = span((c * 2 + 1 - x) * LR, LR, RP)
            return remote(
                self.pieces[k].at[rows, :], self.overs[k], s_px.at[self.i + k], r_px.at[self.i + k], over_x
            )

        def send_core(self):
            for k in range(len(self.pieces)):
                self.to_core(k).start()

        def take(self, copies, bufs, start, n):
            for k, p in enumerate(self.pieces):
                copies(k).wait_recv()
                local(bufs[k], self.temps[k].at[pl.ds(0, n), :], loc.at[4 + k]).start()
            for k, p in enumerate(self.pieces):
                local(bufs[k], self.temps[k].at[pl.ds(0, n), :], loc.at[4 + k]).wait()
                add_into(p.at[span(start, n, RP), :], self.temps[k], n)

        def send_x(self):
            self.take(self.to_core, self.cores, c * HR, HR)
            for k in range(len(self.pieces)):
                self.to_x(k).start()

        def send_along(self):
            self.take(self.to_x, self.overs, (c * 2 + x) * LR, LR)
            self.line.first()

        def sent(self):
            for k in range(len(self.pieces)):
                self.to_core(k).wait_send()
                self.to_x(k).wait_send()
            self.line.sent()

    NQ = GW // WIDE
    temp_q = [
        xb.at[pl.ds((k // 2) * HR, HR), pl.ds(GW + (k % 2) * WIDE, WIDE)] for k in range(NQ)
    ]
    part_q = Part(
        0, [hf.at[k] for k in range(NQ)], temp_q,
        [rcq.at[k] for k in range(NQ)], [rxq.at[k] for k in range(NQ)],
        [colq.at[k] for k in range(NQ)], [nearq.at[k] for k in range(NQ)],
        [outq.at[k] for k in range(NQ)],
    )
    part_o = Part(
        NQ, [cb.at[:, out_cols]], [rt.at[:, pl.ds(0, QW)]], [rco], [rxo], [colo], [nearo], [outo]
    )
    part_o.send_core()
    if NF > 2:
        Chunk(NF - 3).finish()

    kv_sums = nacc.at[rows_of(*order[1], c), :]
    kv_sums[:, : 4 * HEAD_SIZE] = jnp.zeros((T, 4 * HEAD_SIZE), F32)

    def attend_back(h):
        qcol = span(h * HEAD_SIZE, HEAD_SIZE, HEAD_SIZE)
        row, cut = cell(h, 1)
        to_row, to_cut = cell(h, 0)
        for part in range(2):
            rows = slice(part * seq, (part + 1) * seq)
            keys = slice(0, (part + 1) * seq)
            queries = qkv[rows, qcol]
            probs = chances(h, part, queries)
            upstream = gu[span(row + part * seq, seq, seq), cut]
            grad_probs = dot_right(upstream, qkv[keys, VALUE])
            inner = jnp.sum(grad_probs * probs, axis=-1, keepdims=True)
            grad_scores = (probs * (grad_probs - inner)).astype(BF)
            grad_queries = dot_rows(grad_scores, qkv[keys, KEY]) * FACTOR
            gu[span(to_row + part * seq, seq, seq), to_cut] = turn(grad_queries, -1.0, rows).astype(BF)
            grad_keys = dot_left(grad_scores, queries) * FACTOR
            grad_values = dot_left(probs.astype(BF), upstream)
            for i in range(part + 1):
                kcut, vcut = head_cols(i), head_cols(2 + i)
                piece = slice(i * seq, (i + 1) * seq)
                kv_sums[:, kcut] = kv_sums[:, kcut] + grad_keys[piece]
                kv_sums[:, vcut] = kv_sums[:, vcut] + grad_values[piece]

    loop(HEADS, attend_back)
    for i in range(2):
        rows = slice(i * seq, (i + 1) * seq)
        row, cut = cell(HEADS, 0)
        gu[pl.ds(row + i * seq, seq), cut] = turn(kv_sums[:, head_cols(i)], -1.0, rows).astype(BF)
        row, cut = cell(HEADS + 1, 0)
        gu[pl.ds(row + i * seq, seq), cut] = kv_sums[:, head_cols(2 + i)].astype(BF)

    half_cols = 2 * WIDE

    def lin_back(start):
        return dot_right(
            gu[span(start, T, T), :], wq_b[:, :half_cols]
        ) + dot_right(gu[span(TT + start, T, T), :], wq_b[:, half_cols:])

    st[...] = lin_back((1 - y) * T).astype(BF)
    y_copy(st, ar.at[1], 3).start()

    def lin_products(i):
        cols = span(i * tile_rows, tile_rows, 128)
        for side in range(2):
            values = dot_left(xa[:, cols], gu[side * TT : (side + 1) * TT, :])

            def store(rows, part):
                hf[2 * side, rows, :] = part[:, :WIDE]
                hf[2 * side + 1, rows, :] = part[:, WIDE:]

            spread_rows(i, values, store)

    loop(W // tile_rows, lin_products)
    part_q.send_core()
    part_o.send_x()
    grad_lin = nacc.at[rows_of(*order[0], c), :]
    grad_lin[...] = lin_back(y * T)
    for side in range(2):
        cut = slice(side * half_cols, (side + 1) * half_cols)
        sums = jnp.sum(gu[side * TT : (side + 1) * TT, :].astype(F32), axis=0, keepdims=True)
        sv[2:3, cut] = sums
    part_q.send_x()
    tokens_again = ga.at[other_half, :]
    y_copy(ga.at[own_half, :], ga.at[own_half, :], 2).wait_send()
    local(tok_ref, tokens_again, loc.at[1]).start()
    part_o.send_along()
    Chunk(NF - 1).line.middle()
    if NF > 1:
        Chunk(NF - 2).finish()
    part_q.send_along()
    local(tok_ref, tokens_again, loc.at[1]).wait()
    y_copy(st, ar.at[1], 3).wait()

    def back_first(i):
        a = span(i * 32, 32, 32)
        values = tokens_again[a, :].astype(F32)
        grad = grad_lin[a, :] + ar[1, a, :].astype(F32)
        scale = lax.rsqrt(jnp.mean(values * values, axis=-1, keepdims=True) + norm_eps)
        scaled = grad * vec[0:1, :]
        mean = jnp.mean(scaled * values, axis=-1, keepdims=True)
        own[a, :] = own[a, :] + (scale * scaled - values * (scale * scale * scale) * mean)
        sv[0:1, :] = sv[0:1, :] + jnp.sum(grad * values * scale, axis=0, keepdims=True)

    loop(T // 32, back_first)
    local(own, gtok_ref, loc.at[1]).start()

    def small(dq, dy):
        to_q, to_y = lax.rem(q + dq, QUADS), lax.rem(y + dy, 2)
        return remote(
            sv, svr.at[q * 2 + y], s_v.at[dq * 2 + dy], r_v.at[q * 2 + y], at(o, to_q, to_y)
        )

    def small_from(dq, dy):
        from_q, from_y = lax.rem(q + dq, QUADS), lax.rem(y + dy, 2)
        return remote(
            sv, svr.at[from_q * 2 + from_y], s_v.at[dq * 2 + dy],
            r_v.at[from_q * 2 + from_y], at(o, from_q, from_y),
        )

    def small_along(step):
        return remote(sv, svz.at[o], s_vz.at[step], r_vz.at[o], at(lax.rem(o + step, O), q, y))

    def small_along_from(step):
        place = lax.rem(o + step, O)
        return remote(sv, svz.at[place], s_vz.at[step], r_vz.at[place], at(place, q, y))

    peers = [(dq, dy) for dq in range(QUADS) for dy in range(2) if dq or dy]
    for dq, dy in peers:
        small(dq, dy).start()
    svr[q * 2 + y] = sv[...]

    part_o.line.middle()

    def layer_out(a, total):
        tk[a, :] = (mid[a, :] + total).astype(BF)

    sum_close(1, layer_out)
    local(tk, mixed_ref, loc.at[2]).start()
    for dq, dy in peers:
        small_from(dq, dy).wait_recv()
        small(dq, dy).wait_send()
    gains = svr[0]
    for i in range(1, 2 * QUADS):
        gains = gains + svr[i]
    biases = svr[y]
    for i in range(1, QUADS):
        biases = biases + svr[i * 2 + y]
    sv[...] = gains
    sv[2:3, :] = biases[2:3, :]
    for step in range(1, O):
        small_along(step).start()
    svz[o] = sv[...]
    part_q.line.middle()
    Chunk(NF - 1).finish()
    part_o.line.last()
    local(part_o.line.block(0, o), gao_ref, loc.at[3]).start()
    for step in range(1, O):
        small_along_from(step).wait_recv()
        small_along(step).wait_send()
    total = svz[0]
    for i in range(1, O):
        total = total + svz[i]
    sv[...] = total
    local(sv, sums_ref, loc.at[8]).start()
    part_q.line.last()
    for k in range(NQ):
        local(part_q.line.block(k, o), gaq_ref.at[k], loc.at[4 + k]).start()

    gather_q.sent()
    gather_o.sent()
    y_copy(xa.at[own_half, :], xa.at[own_half, :], 0).wait_send()
    part_o.sent()
    part_q.sent()
    head.finished()
    loop(NF, lambda kk: Chunk(kk).finished())
    local(own, gtok_ref, loc.at[1]).wait()
    local(tk, mixed_ref, loc.at[2]).wait()
    local(part_o.line.block(0, o), gao_ref, loc.at[3]).wait()
    local(sv, sums_ref, loc.at[8]).wait()
    for k in range(NQ):
        local(part_q.line.block(k, o), gaq_ref.at[k], loc.at[4 + k]).wait()


def layer(sz, tokens, cotangent, wq, wo, wh, wf, vec, rope):
    O, NF, T = sz.outer, sz.full, sz.tokens
    H = O // 2
    HK, W, RP = sz.head, sz.wide, sz.pad
    R4, LR = QUADS * sz.rows, O * sz.pad
    HR = 2 * LR
    QW, GW = sz.query, sz.query + 2 * sz.key
    NQ = GW // WIDE
    PT = 2 * QUADS * T
    NL = NF + 1 + NQ + 1
    A, B = 3 * HK, 3 * WIDE
    out = jax.ShapeDtypeStruct
    outs = [
        out((QUADS, RP, A), BF),
        out((NF, QUADS, RP, B), BF),
        out((NQ, RP, WIDE), BF),
        out((RP, QW), BF),
        out((T, W), BF),
        out((T, W), F32),
        out((8, W), F32),
        out((W, A), BF),
        out((NF, W, B), BF),
        out((H, H * R4, A), BF),
        out((NF, H, H * R4, B), BF),
        out((H, R4, A), BF),
        out((NF, H, R4, B), BF),
        out((R4, A), BF),
        out((NF, R4, B), BF),
        out((2, 4, T, W), F32),
        out((2, 3, T, W), BF),
        out((sz.dp * RP, GW), BF),
        out((sz.dp * RP, QW), BF),
        out((NQ, HR, WIDE), BF),
        out((HR, QW), BF),
        out((NQ, LR, WIDE), BF),
        out((LR, QW), BF),
        out((NQ, H, H * RP, WIDE), BF),
        out((H, H * RP, QW), BF),
        out((NQ, H, RP, WIDE), BF),
        out((H, RP, QW), BF),
        out((NQ, RP, WIDE), BF),
        out((RP, QW), BF),
    ]
    if not sz.whole:
        outs += [out((QUADS, RP, A), BF), out((NF, QUADS, RP, B), BF)]
    dma = pltpu.SemaphoreType.DMA
    vm = pltpu.VMEM
    scratch = [
        vm((PT, W), BF),
        vm((PT, W), BF),
        vm((PT, W), F32),
        vm((W, B), BF),
        vm((W, A), BF),
        vm((NF, W, B), BF),
        vm((PT, HK), BF),
        vm((NF, PT, WIDE), BF),
        vm((PT, 2 * WIDE), BF),
        vm((3, T, W), BF),
        vm((T, W), BF),
        vm((max(W // 2, HR), B), BF),
        vm((T, W), F32),
        vm((2 * T, W), BF),
        vm((2 * T, GW), BF),
        vm((2 * T, QW), BF),
        vm((2, T, W), BF),
        vm((T, W), BF),
        vm((T, W), F32),
        vm((2 * T, W), BF),
        vm((8, W), F32),
        vm((2 * QUADS, 8, W), F32),
        vm((O, 8, W), F32),
        dma((NF + 1, 4)),
        dma((NF + 1, 3)),
        dma((NF + 1, H)),
        dma((NF + 1, H)),
        dma((NF + 1,)),
        dma((NF + 1, H)),
        dma((NF + 1, H)),
        dma((NF + 1,)),
        dma((NL,)),
        dma((NL, H)),
        dma((NL, H)),
        dma((NL, H)),
        dma((NL, H)),
        dma((NL,)),
        dma((NF + 1, 4)),
        dma((NF + 1, 3)),
        dma((2, 7)),
        dma((2, 7)),
        dma((2, 7)),
        dma((2, 7)),
        dma((4,)),
        dma((4,)),
        dma((2, O)),
        dma((2, O)),
        dma((2, O)),
        dma((2, O)),
        dma((2, 2, O)),
        dma((2, 2, O)),
        dma((NQ + 1,)),
        dma((NQ + 1,)),
        dma((NQ + 1,)),
        dma((NQ + 1,)),
        dma((2 * QUADS,)),
        dma((2 * QUADS,)),
        dma((O,)),
        dma((O,)),
        dma((12,)),
    ]
    if not sz.whole:
        scratch += [vm((QUADS * RP, max(B, GW)), BF), vm((R4, B), BF)]
    any_spec = pl.BlockSpec(memory_space=pl.ANY)
    vmem_spec = pl.BlockSpec(memory_space=pltpu.VMEM)
    results = pl.pallas_call(
        lambda *refs: layer_kernel(sz, *refs),
        out_shape=outs,
        in_specs=[any_spec] * 6 + [vmem_spec] * 2,
        out_specs=[any_spec] * len(outs),
        scratch_shapes=scratch,
        compiler_params=pltpu.CompilerParams(
            collective_id=0, has_side_effects=True, vmem_limit_bytes=64 << 20
        ),
        name="layer",
    )(tokens, cotangent, wq, wo, wh, wf, vec, rope)
    return results[:7]


def per_device(
    sz,
    tokens,
    w_query,
    key_weight,
    value_weight,
    b_query,
    key_bias,
    value_bias,
    w_out,
    gain_attn,
    gain_mlp,
    w_gate,
    w_up,
    w_down,
    cotangent,
):
    rows, hidden_units = w_gate.shape
    more = sz.pad - sz.rows
    w3 = jnp.stack([w_gate, w_up, w_down.T])
    w3 = jnp.pad(w3, ((0, 0), (0, more), (0, QUADS * sz.slice - hidden_units)))
    w3 = w3.reshape(3, sz.pad, QUADS, sz.slice)
    wh = w3[..., : sz.head].transpose(2, 1, 0, 3).reshape(QUADS, sz.pad, 3 * sz.head)
    wf = w3[..., sz.head :].reshape(3, sz.pad, QUADS, sz.full, WIDE)
    wf = wf.transpose(3, 2, 1, 0, 4).reshape(sz.full, QUADS, sz.pad, 3 * WIDE)
    wq = jnp.concatenate([w_query, key_weight, value_weight], axis=1)
    wq = jnp.pad(wq, ((0, more), (0, 0)))
    wo = jnp.pad(w_out.T, ((0, more), (0, 0)))
    bias = jnp.concatenate([b_query, key_bias, value_bias]).astype(F32)
    bias = jnp.pad(bias, (0, sz.wide - bias.shape[0]))
    vec = jnp.stack([gain_attn.astype(F32), gain_mlp.astype(F32), bias])
    vec = jnp.pad(vec, ((0, 5), (0, 0)))
    cosine, sine = rope_tables(SEQUENCE_TOKENS, HEAD_SIZE)
    midway = HEAD_SIZE // 2
    signed = jnp.concatenate([-sine[..., :midway], sine[..., midway:]], axis=-1)
    rope = jnp.stack([cosine[0, :, 0, :], signed[0, :, 0, :]])

    grad_head, grad_full, grad_q, grad_o, mixed, grad_tokens, sums = layer(
        sz, tokens, cotangent, wq, wo, wh, wf, vec, rope
    )
    grad_head = grad_head.reshape(QUADS, sz.pad, 3, sz.head).transpose(2, 1, 0, 3)
    grad_full = grad_full.reshape(sz.full, QUADS, sz.pad, 3, WIDE).transpose(3, 2, 1, 0, 4)
    grad_full = grad_full.reshape(3, sz.pad, QUADS, sz.full * WIDE)
    grads = jnp.concatenate([grad_head, grad_full], axis=-1)
    grads = grads.reshape(3, sz.pad, QUADS * sz.slice)[:, :rows, :hidden_units].astype(F32)
    grad_q = grad_q.transpose(1, 0, 2).reshape(sz.pad, -1)[:rows].astype(F32)
    grad_o = grad_o[:rows].astype(F32)
    cuts = (sz.query, sz.query + sz.key, sz.query + 2 * sz.key)
    return (
        mixed,
        grad_tokens,
        grad_q[:, : cuts[0]],
        grad_q[:, cuts[0] : cuts[1]],
        grad_q[:, cuts[1] :],
        sums[2, : cuts[0]],
        sums[2, cuts[0] : cuts[1]],
        sums[2, cuts[1] : cuts[2]],
        grad_o.T,
        sums[0],
        sums[1],
        grads[0],
        grads[1],
        grads[2].T,
    )


def solution(mesh):
    dp = mesh.shape["dp"]

    def whole(*args):
        def shard(*blocks):
            tokens, w_query, key_weight, w_gate = blocks[0], blocks[1], blocks[2], blocks[10]
            sz = Sizes(dp, w_gate.shape, tokens.shape[0], w_query.shape[1], key_weight.shape[1])
            return per_device(sz, *blocks)

        return jax.shard_map(
            shard, mesh=mesh, in_specs=in_specs, out_specs=out_specs, check_vma=False
        )(*args)

    in_specs = (
        P(("dp", "tensor"), None),
        P("dp", "tensor"),
        P("dp", "tensor"),
        P("dp", "tensor"),
        P("tensor"),
        P("tensor"),
        P("tensor"),
        P("tensor", "dp"),
        P(),
        P(),
        P("dp", "tensor"),
        P("dp", "tensor"),
        P("tensor", "dp"),
        P(("dp", "tensor"), None),
    )
    out_specs = (
        P(("dp", "tensor"), None),
        P(("dp", "tensor"), None),
        P("dp", "tensor"),
        P("dp", "tensor"),
        P("dp", "tensor"),
        P("tensor"),
        P("tensor"),
        P("tensor"),
        P("tensor", "dp"),
        P(),
        P(),
        P("dp", "tensor"),
        P("dp", "tensor"),
        P("tensor", "dp"),
    )
    return whole
```

time: 1860 us -> 548 us (0.29)
  waiting for transfers between devices: 1520 us -> 0 us
  Pallas kernels: 0 us -> 489 us
  matrix products: 174 us -> 0 us
  blocking collectives: 82.7 us -> 0 us
  local copies, waits for them, and re-layouts: 20.5 us -> 40.9 us
    reduce_scatter x11 -> x0, waiting for transfers between devices: 1090 us -> none  [the longest x1 267 us: per_device(): lax.psum_scatter(grad_gate_part, 'dp', scatter_dimension=0, tiled=True)]
    pallas_call x0 -> x1, Pallas kernels: none -> 489 us  [layer(): pl.pallas_call(lambda *refs: layer_kernel(sz, *refs), out_shape=outs, in_...]
    all_gather x9 -> x0, waiting for transfers between devices: 421 us -> none  [the longest x1 111 us: per_device(): lax.all_gather(w_down, 'dp', axis=1, tiled=True)]
    dot_general x27 -> x0, matrix products: 174 us -> none  [the longest x7 57.3 us: dot_left(): lax.dot_general(left, right, (((0,), (0,)), ((), ())), preferred_element_...]
    all_gather x2 -> x0, blocking collectives: 42.7 us -> none  [the longest x1 24.1 us: per_device(): lax.all_gather(key_weight, 'dp', axis=0, tiled=True)]
    psum x1 -> x0, blocking collectives: 40 us -> none  [per_device(): lax.psum((gain_attn_term, gain_mlp_term, bias_query_full, bias_key_full,...]
    reshape x0 -> x8, local copies, waits for them, and re-layouts: none -> 19.4 us  [the longest x1 4.57 us: per_device(): wf = wf.transpose(3, 2, 1, 0, 4).reshape(sz.full, QUADS, sz.pad, 3 * WIDE)]
  transfers between devices with their start and end apart: 20 -> 0, of which waited for: 17 -> 0; matrix products, arithmetic and copies ran while one was open for 7% -> 0% of each run, Pallas kernels for 0% -> 0%
where the time goes in v2:
time: 548 us; the launch traced here: 540 us
  Pallas kernels  489 us (89%)
  local copies, waits for them, and re-layouts  40.9 us (7%)
  other arithmetic  9.94 us (2%)
    pallas_call x1, Pallas kernels, layer(): pl.pallas_call(lambda *refs: layer_kernel(sz, *refs), out_shape=outs, in_...  489 us

profile of v2, /device:TPU:0, one launch (start us, length us, event | category | flops | bytes accessed | tf_op | source)
XLA Modules:
  0.0 540.2 jit_solution(6982138109072278884)
XLA Ops:
  0.7 0.9 fusion.17
  1.6 0.7 stack.35
  2.3 0.7 stack.36
  3.0 0.6 fusion.12.refs_6_
  3.6 1.6 pad_maximum_fusion.1.refs_2_
  5.3 0.9 maximum_cosine_fusion
  6.2 0.9 maximum_sine_fusion
  7.5 0.8 pad_maximum_fusion.refs_7_
  8.3 0.5 fusion.4
  8.8 2.3 reshape.163
  11.1 1.7 slice-done.1
  12.8 2.3 reshape.172
  15.3 1.0 reshape.164.refs_4_
  16.3 3.7 copy.38
  20.0 4.6 reshape.166.refs_5_
  24.6 488.5 %layer.1 = (bf16[4,96,384]{2,1,0:T(8,128)(2,1)}, bf16[4,4,96,768]{3,2,1,0:T(8,128)(2,1)}, bf16[4,96,256]{2,1,0:T(8,128)(2,1)}, bf16[96,768]{1,0:T(8,128)(2,1)}, ...) custom-call(bf16[256,1536]{1,0:T(8,128)(2,1)} %refs_0_.1, ...), custom_call_target="tpu_custom_call" | custom-call | tf_op jit(solution)/shard_map/layer/pallas_call | solution.py:1183
  513.1 1.3 slice_bitcast_fusion.3
  514.4 1.3 slice_reduce_fusion.2
  515.7 1.5 slice_reduce_fusion
  517.2 1.6 convert_bitcast_fusion.1
  518.9 1.0 convert_bitcast_fusion
  519.9 0.7 fusion.18
  520.5 0.7 slice.68
  521.4 4.6 reshape.168
  526.0 3.6 copy.40
  529.6 4.3 reshape.169
  533.9 0.3 maximum_bitcast_fusion
  534.5 0.3 slice_convert_fusion
  534.9 2.4 slice_bitcast_fusion
  537.3 0.9 copy.53
  538.2 0.8 copy-done
  539.0 1.1 copy.54
  (24 shorter events, 1.1 us)
Async XLA Ops:
  0.6 7.7 %copy-start.1 = (bf16[4480,96]{0,1:T(8,128)(2,1)S(1)}, bf16[4480,96]{0,1:T(8,128)(2,1)}, u32[]{:S(2)}) copy-start(bf16[4480,96]{0,1:T(8,128)(2,1)} %param.26) | copy-start | bytes 2580484
  0.7 7.6 %copy-start.2 = (bf16[96,4480]{1,0:T(8,128)(2,1)S(1)}, bf16[96,4480]{1,0:T(8,128)(2,1)}, u32[]{:S(2)}) copy-start(bf16[96,4480]{1,0:T(8,128)(2,1)} %param.25) | copy-start | bytes 2580484
  0.7 7.6 %copy-start.3 = (bf16[96,4480]{1,0:T(8,128)(2,1)S(1)}, bf16[96,4480]{1,0:T(8,128)(2,1)}, u32[]{:S(2)}) copy-start(bf16[96,4480]{1,0:T(8,128)(2,1)} %param.24) | copy-start | bytes 2580484
  11.1 1.7 slice-start.1
  12.8 2.3 slice-start
  513.1 8.1 %copy-start.5 = (bf16[4,96,384]{2,1,0:T(8,128)(2,1)S(1)}, bf16[4,96,384]{2,1,0:T(8,128)(2,1)}, u32[]{:S(2)}) copy-start(bf16[4,96,384]{2,1,0:T(8,128)(2,1)} %get-tuple-element.26) | copy-start | bytes 884740
  534.9 2.5 copy-start.4
  537.3 1.7 copy-start

commit v3 on v2

--- a/solution.py
+++ b/solution.py
@@ -178,64 +178,91 @@
                 s_nr.at[self.i + k, to], r_nr.at[self.i + k, t], at(base + to, q, y),
             )
 
-        def cross(self, k, to):
+        def cross(self, k):
             return remote(
-                self.block(k, far + to), self.out[k],
-                s_out.at[self.i + k, to], r_out.at[self.i + k], at(far + to, q, y),
+                self.block(k, far, H), self.out[k], s_out.at[self.i + k], r_out.at[self.i + k], far_mid
             )
 
         def first(self):
+            @pl.when(jnp.logical_not(is_middle))
+            def _():
+                for k in range(len(self.pieces)):
+                    self.to_middle(k, pos).start()
+                for k in range(len(self.pieces)):
+                    for t in range(H):
+                        pl.when(pos != t)(lambda: self.near(k, t, pos).start())
+
+        def far_copy(self, k, t):
+            return local(self.col[k].at[t], self.temp(k, 0, H), loc.at[4 + k])
+
+        def far_add(self, t):
             for k in range(len(self.pieces)):
-                pl.when(jnp.logical_not(is_middle))(lambda: self.to_middle(k, pos).start())
-                for t in range(H):
-                    pl.when(pos != t)(lambda: self.near(k, t, pos).start())
-
-        def middle(self):
-            ks = range(len(self.pieces))
-
+                self.far_copy(k, t).wait()
+                add_into(self.block(k, far, H), self.temp(k, 0, H), H * self.rows)
+
+        def far_take(self):
             @pl.when(is_middle)
             def _():
-                for t in range(H):
-
-                    @pl.when(pos != t)
-                    def _():
-                        for k in ks:
-                            self.to_middle(k, t).wait_recv()
-                            local(self.col[k].at[t], self.temp(k, 0, H), loc.at[4 + k]).start()
-                        for k in ks:
-                            local(self.col[k].at[t], self.temp(k, 0, H), loc.at[4 + k]).wait()
-                            add_into(self.block(k, far, H), self.temp(k, 0, H), H * self.rows)
-
-                for k in ks:
+                for i in range(H - 1):
+                    t = jnp.where(half == 0, i, i + 1)
+                    for k in range(len(self.pieces)):
+                        self.to_middle(k, t).wait_recv()
+                        self.far_copy(k, t).start()
+                    if i < H - 2:
+                        self.far_add(t)
+
+        def far_give(self):
+            @pl.when(is_middle)
+            def _():
+                self.far_add(jnp.where(half == 0, H - 2, H - 1))
+                for k in range(len(self.pieces)):
+                    self.cross(k).start()
+
+        def out_copy(self, k):
+            return local(self.out[k], self.temp(k, 0, H), loc.at[4 + k])
+
+        def cross_take(self):
+            @pl.when(is_middle)
+            def _():
+                for k in range(len(self.pieces)):
+                    self.cross(k).wait_recv()
+                    self.out_copy(k).start()
+
+        def cross_give(self):
+            @pl.when(is_middle)
+            def _():
+                for k in range(len(self.pieces)):
+                    self.out_copy(k).wait()
+                    add_into(self.block(k, base, H), self.temp(k, 0, H), H * self.rows)
                     for t in range(H):
-                        self.cross(k, t).start()
-
-        def last(self):
-            ks = range(len(self.pieces))
-            for t in range(H):
-
-                @pl.when(pos != t)
-                def _():
-                    for k in ks:
-                        self.near(k, pos, t).wait_recv()
-                        local(self.near_[k].at[t], self.temp(k, 0, 1), loc.at[4 + k]).start()
-                    for k in ks:
-                        local(self.near_[k].at[t], self.temp(k, 0, 1), loc.at[4 + k]).wait()
-                        add_into(self.block(k, o), self.temp(k, 0, 1), self.rows)
-
-            for k in ks:
-                self.cross(k, pos).wait_recv()
-                local(self.out[k], self.temp(k, 1, 1), loc.at[4 + k]).start()
-            for k in ks:
-                local(self.out[k], self.temp(k, 1, 1), loc.at[4 + k]).wait()
-                add_into(self.block(k, o), self.temp(k, 1, 1), self.rows)
+                        pl.when(pos != t)(lambda: self.near(k, t, pos).start())
+
+        def near_copy(self, k, t):
+            return local(self.near_[k].at[t], self.temp(k, 0, 1), loc.at[4 + k])
+
+        def near_add(self, t):
+            for k in range(len(self.pieces)):
+                self.near_copy(k, t).wait()
+                add_into(self.block(k, o), self.temp(k, 0, 1), self.rows)
+
+        def last_take(self):
+            for i in range(H - 1):
+                t = jnp.where(pos <= i, i + 1, i)
+                for k in range(len(self.pieces)):
+                    self.near(k, pos, t).wait_recv()
+                    self.near_copy(k, t).start()
+                if i < H - 2:
+                    self.near_add(t)
+
+        def last_give(self):
+            self.near_add(jnp.where(pos <= H - 2, H - 1, H - 2))
 
         def sent(self):
             for k in range(len(self.pieces)):
                 pl.when(jnp.logical_not(is_middle))(lambda: self.to_middle(k, pos).wait_send())
+                pl.when(is_middle)(lambda: self.cross(k).wait_send())
                 for t in range(H):
                     pl.when(pos != t)(lambda: self.near(k, t, pos).wait_send())
-                    pl.when(is_middle)(lambda: self.cross(k, t).wait_send())
 
     class Chunk:
         def __init__(self, kk):
@@ -293,12 +320,9 @@
                 s_own.at[self.i, to], r_own.at[self.i, t], at(base + to, q, y),
             )
 
-        def own_far(self, half_, t):
-            b = half_ * H + t
-            return remote(
-                self.block(self.wag, b), self.block(self.wag, b),
-                s_far.at[self.i], r_far.at[self.i, t], far_mid,
-            )
+        def half_far(self, half_):
+            rows = self.block(self.wag, half_ * H, H)
+            return remote(rows, rows, s_far.at[self.i], r_far.at[self.i], far_mid)
 
         def forward(self, half_, to):
             rows = self.block(self.wag, half_ * H, H)
@@ -312,27 +336,34 @@
                 self.a2a(dq).wait_recv()
             if not sz.whole:
                 self.join()
-            self.own_far(half, pos).start()
             for t in range(H):
                 pl.when(pos != t)(lambda: self.own_to(t, pos).start())
 
-        def gather_middle(self):
+        def gather_half(self):
             @pl.when(is_middle)
             def _():
                 for t in range(H):
-                    self.own_far(1 - half, t).wait_recv()
+                    pl.when(pos != t)(lambda: self.own_to(pos, t).wait_recv())
+                self.half_far(half).start()
+
+        def gather_far(self):
+            @pl.when(is_middle)
+            def _():
+                self.half_far(1 - half).wait_recv()
                 for t in range(H):
                     pl.when(pos != t)(lambda: self.forward(1 - half, t).start())
 
         def gather_wait(self):
-            for t in range(H):
-                pl.when(pos != t)(lambda: self.own_to(pos, t).wait_recv())
-            pl.when(jnp.logical_not(is_middle))(lambda: self.forward(1 - half, pos).wait_recv())
+            @pl.when(jnp.logical_not(is_middle))
+            def _():
+                for t in range(H):
+                    pl.when(pos != t)(lambda: self.own_to(pos, t).wait_recv())
+                self.forward(1 - half, pos).wait_recv()
 
         def gather_sent(self):
             for dq in (1, 2, 3):
                 self.a2a(dq).wait_send()
-            self.own_far(half, pos).wait_send()
+            pl.when(is_middle)(lambda: self.half_far(half).wait_send())
             for t in range(H):
 
                 @pl.when(pos != t)
@@ -366,7 +397,11 @@
                 move(stage.at[pl.ds(i * RP, RP), self.cols], self.ab.at[i], loc.at[3])
 
         def finish(self):
-            self.line.last()
+            self.line.last_take()
+            self.finish_give()
+
+        def finish_give(self):
+            self.line.last_give()
             if not sz.whole:
                 self.split()
             self.give_own().start()
@@ -389,8 +424,16 @@
     mine = rows_of(x, y, c)
 
     def tok(src, buf, which, n):
-        dev = core if n == 3 else at(o, chips[n][0] * 2 + c, chips[n][1])
+        dev = core if n == 3 else (over_x, over_y)[n - 1]
         return remote(src, buf.at[mine, :], s_tok.at[which, n], r_tok.at[which, n], dev)
+
+    def tok_half(buf, which, n):
+        start = rows_of(*chips[n], c).start
+        rows = span(start + (n - 1) * (T // 2), T // 2, T // 2)
+        return remote(
+            buf.at[rows, :], buf.at[rows, :],
+            s_tok.at[which, 6 + n], r_tok.at[which, 6 + n], (over_y, over_x)[n - 1],
+        )
 
     def tok_pass(buf, which, n):
         rows = rows_of(*chips[n], c)
@@ -400,18 +443,25 @@
         )
 
     def tok_start(src, buf, which):
-        for n in (3, 2, 1, 0):
+        for n in (3, 2, 1):
             tok(src, buf, which, n).start()
 
-    def tok_take(src, buf, which, n):
-        tok(src, buf, which, n).wait_recv()
-        if n < 3:
+    def tok_next(src, buf, which):
+        for n in (2, 1):
+            tok(src, buf, which, n).wait_recv()
+            tok_half(buf, which, n).start()
             tok_pass(buf, which, n).start()
-            tok_pass(buf, which, n).wait_recv()
+
+    def tok_across(buf, which):
+        for n in (2, 1):
+            tok_half(buf, which, n).wait_recv()
+        tok_pass(buf, which, 0).start()
 
     def tok_sent(src, buf, which):
-        for n in range(4):
+        for n in (1, 2, 3):
             tok(src, buf, which, n).wait_send()
+        for n in (1, 2):
+            tok_half(buf, which, n).wait_send()
         for n in range(3):
             tok_pass(buf, which, n).wait_send()
 
@@ -428,10 +478,16 @@
             s_sum.at[which, 4 + n], r_sum.at[which, 4 + n], at(o, xx * 2 + c, yy),
         )
 
-    def sum_mid(n, which):
+    def sum_fetch(n, which):
+        return local(pairbuf.at[which, n], nacc.at[rows_of(*order[n], 1 - c), :], loc.at[12 + n])
+
+    def sum_take(n, which):
+        sum_pair(n, which).wait()
+        sum_fetch(n, which).start()
+
+    def sum_give(n, which):
         here, spare = nacc.at[rows_of(*order[n], c), :], nacc.at[rows_of(*order[n], 1 - c), :]
-        sum_pair(n, which).wait()
-        move(pairbuf.at[which, n], spare, loc.at[7])
+        sum_fetch(n, which).wait()
 
         def step(i):
             a = span(i * 32, 32, 32)
@@ -569,7 +625,8 @@
 
     gather_q.start()
     local(tok_ref, tk, loc.at[1]).start()
-    gather_o.start()
+    head.a2a_start()
+    Chunk(0).a2a_start()
     local(tok_ref, tk, loc.at[1]).wait()
 
     def norm_first(i):
@@ -582,14 +639,18 @@
     own_half, other_half = span(y * T, T, T), span((1 - y) * T, T, T)
     y_copy(xa.at[own_half, :], xa.at[own_half, :], 0).start()
     sv[...] = jnp.zeros_like(sv)
+    head.gather_own()
     gather_q.pass_on()
+    gather_o.start()
+    head.gather_half()
     gather_q.pass_over()
+    Chunk(0).gather_own()
     gather_q.wait()
     wq_v, wr_v, wo_v = pb.at[0], pb.at[1, :, pl.ds(0, 2 * sz.key)], pb.at[2]
     ready = fetch([(gq, QUERY, wq_v), (gq, REST, wr_v)], 1)
-    head.a2a_start()
-    if NF > 0:
-        Chunk(0).a2a_start()
+    Chunk(1).a2a_start()
+    tok_start(cot_ref, cb, 1)
+    local(cot_ref, cb.at[mine, :], loc.at[3]).start()
     y_copy(xa.at[own_half, :], xa.at[other_half, :], 0).wait_recv()
     ready()
 
@@ -606,7 +667,8 @@
 
     loop(2, project)
     gather_o.pass_on()
-    head.gather_own()
+    head.gather_far()
+    Chunk(0).gather_half()
     SHARE = QW // sz.key
 
     def chances(h, part, queries):
@@ -629,19 +691,18 @@
 
     loop(HEADS, attend)
     gather_o.pass_over()
+    Chunk(1).gather_own()
     gather_o.wait()
     ready = fetch([(go, pl.ds(0, QW), wo_v)], 1)
-    if NF > 0:
-        Chunk(0).gather_own()
+    tok_next(cot_ref, cb, 1)
     ready()
     st[...] = dot_right(mh[other_half, :], wo_v[...]).astype(BF)
     y_copy(st, ar.at[0], 1).start()
-    tok_start(cot_ref, cb, 1)
-    local(cot_ref, cb.at[mine, :], loc.at[1]).start()
     mid[...] = dot_right(mh[own_half, :], wo_v[...]) + tk[...].astype(F32)
-    for kk in range(1, NF):
-        Chunk(kk).a2a_start()
-    head.gather_middle()
+    Chunk(2).a2a_start()
+    Chunk(0).gather_far()
+    Chunk(1).gather_half()
+    tok_across(cb, 1)
     y_copy(st, ar.at[0], 1).wait_recv()
 
     def norm_second(i):
@@ -655,15 +716,13 @@
 
     xsrc = xb.at[mine, :]
     tok_start(xsrc, xb, 0)
-    local(cot_ref, cb.at[mine, :], loc.at[1]).wait()
-    for n in (3, 2, 1, 0):
-        tok_take(cot_ref, cb, 1, n)
-    if NF > 1:
-        Chunk(1).gather_own()
+    local(cot_ref, cb.at[mine, :], loc.at[3]).wait()
+    tok(cot_ref, cb, 1, 3).wait_recv()
+    for n in range(3):
+        tok_pass(cb, 1, n).wait_recv()
     head.gather_wait()
     head.load().start()
-    if NF > 0:
-        Chunk(0).gather_middle()
+    Chunk(2).gather_own()
     head.load().wait()
 
     def tile(ch, rows, first):
@@ -696,48 +755,70 @@
 
         loop(W // TD, step)
 
-    for n in (3, 2, 1, 0):
-        tok_take(xsrc, xb, 0, n)
-        tile(head, chip_rows(*order[n]), True)
-    if NF > 0:
-        Chunk(0).gather_wait()
-        Chunk(0).load().start()
+    tok(xsrc, xb, 0, 3).wait_recv()
+    tile(head, chip_rows(*order[3]), True)
+    tok_next(xsrc, xb, 0)
+    tok_pass(xb, 0, 2).wait_recv()
+    tile(head, chip_rows(*order[2]), True)
+    Chunk(1).gather_far()
+    Chunk(2).gather_half()
+    tok_pass(xb, 0, 1).wait_recv()
+    tile(head, chip_rows(*order[1]), True)
+    tok_across(xb, 0)
+    for kk in range(3, NF):
+        Chunk(kk).a2a_start()
+    Chunk(0).gather_wait()
+    tok_pass(xb, 0, 0).wait_recv()
+    tile(head, chip_rows(*order[0]), True)
+    Chunk(0).load().start()
     products(head)
     head.line.first()
 
     def body(kk):
         ch, nxt = Chunk(kk), Chunk(lax.min(kk + 1, NF - 1))
-        before, two = Chunk(lax.max(kk - 1, 0)), Chunk(lax.max(kk - 2, 0))
+        two, three = Chunk(lax.max(kk - 2, 0)), Chunk(lax.max(kk - 3, 0))
         last = kk == NF - 1
-        pl.when(kk + 2 < NF)(lambda: Chunk(lax.min(kk + 2, NF - 1)).gather_own())
+        later = Chunk(lax.min(kk + 3, NF - 1))
+        pl.when(kk + 3 < NF)(later.gather_own)
         ch.load().wait()
 
         def visit(p):
+            for n in range(3):
+                pl.when(last & (p == n + 1))(lambda: sum_take(n, 0))
+            pl.when((kk == 1) & (p == 1))(head.line.far_take)
+            pl.when((kk == 2) & (p == 0))(head.line.cross_take)
+            pl.when((kk >= 2) & (kk < NF - 1) & (p == 2))(two.line.far_take)
+            pl.when((kk == 3) & (p == 0))(head.line.last_take)
             xx = jnp.where(p < 2, 1 - x, x)
             yy = jnp.where(p % 2 == 0, 1 - y, y)
             tile(ch, chip_rows(xx, yy), False)
-
-            @pl.when(last)
-            def _():
-                for n in range(4):
-                    pl.when(p == n)(lambda: sum_pair(n, 0).start())
-                for n in range(3):
-                    pl.when(p == n + 1)(lambda: sum_mid(n, 0))
+            for n in range(4):
+                pl.when(last & (p == n))(lambda: sum_pair(n, 0).start())
+            for n in range(3):
+                pl.when(last & (p == n + 1))(lambda: sum_give(n, 0))
+
+            pl.when((kk == 1) & (p == 1))(head.line.far_give)
+            pl.when((kk == 2) & (p == 0))(head.line.cross_give)
+            pl.when((kk >= 2) & (kk < NF - 1) & (p == 2))(two.line.far_give)
+            pl.when((kk == 3) & (p == 0))(head.finish_give)
+            pl.when((kk + 3 < NF) & (p == 2))(later.gather_half)
 
         loop(4, visit)
-        pl.when(last)(lambda: sum_mid(3, 0))
-        pl.when(kk < NF - 1)(lambda: nxt.gather_middle())
+        pl.when(last)(lambda: sum_take(3, 0))
+
+        @pl.when(kk < NF - 1)
+        def _():
+            pl.when(kk == 0)(Chunk(1).gather_wait)
+            pl.when(kk > 1)(nxt.gather_far)
+            pl.when(kk > 0)(nxt.gather_wait)
+            nxt.load().start()
+
+        pl.when(kk >= 3)(three.line.cross_take)
         products(ch)
         ch.line.first()
-        pl.when(kk == 0)(lambda: head.line.middle())
-        pl.when(kk == 1)(lambda: head.finish())
-        pl.when((kk >= 1) & (kk < NF - 1))(lambda: before.line.middle())
-        pl.when((kk >= 2) & (kk < NF - 1))(lambda: two.finish())
-
-        @pl.when(kk < NF - 1)
-        def _():
-            nxt.gather_wait()
-            nxt.load().start()
+        pl.when(kk >= 3)(three.line.cross_give)
+        pl.when(last)(lambda: sum_give(3, 0))
+        pl.when(kk == 0)(Chunk(2).gather_far)
 
     loop(NF, body)
 
@@ -762,16 +843,14 @@
     sum_close(0, back_second)
     ga[own_half, :] = tk[...]
     y_copy(ga.at[own_half, :], ga.at[own_half, :], 2).start()
-    if NF > 1:
-        Chunk(NF - 2).line.middle()
+    Chunk(NF - 3).line.far_take()
 
     def m_load(kk):
         return local(
             wagf.at[kk, :, pl.ds(2 * WIDE, WIDE)], wv.at[:, span(lax.rem(kk, 2) * WIDE, WIDE, WIDE)], loc.at[8],
         )
 
-    local(wagh.at[:, pl.ds(2 * HK, HK)], wv.at[:, pl.ds(2 * WIDE, HK)], loc.at[0]).start()
-    local(wagh.at[:, pl.ds(2 * HK, HK)], wv.at[:, pl.ds(2 * WIDE, HK)], loc.at[0]).wait()
+    move(wagh.at[:, pl.ds(2 * HK, HK)], wv.at[:, pl.ds(2 * WIDE, HK)], loc.at[0])
     m_load(0).start()
 
     def m_first(p):
@@ -779,6 +858,7 @@
         nacc[rows, :] = dot_right(hh[rows, :], wv[:, 2 * WIDE : 2 * WIDE + HK])
 
     loop(4, m_first)
+    Chunk(NF - 3).line.far_give()
 
     def m_chunk(kk):
         m_load(kk).wait()
@@ -797,7 +877,9 @@
     for n in range(4):
         sum_pair(n, 1).start()
     for n in range(4):
-        sum_mid(n, 1)
+        sum_take(n, 1)
+    for n in range(4):
+        sum_give(n, 1)
     ready()
     y_copy(ga.at[own_half, :], ga.at[other_half, :], 2).wait_recv()
 
@@ -898,8 +980,7 @@
         NQ, [cb.at[:, out_cols]], [rt.at[:, pl.ds(0, QW)]], [rco], [rxo], [colo], [nearo], [outo]
     )
     part_o.send_core()
-    if NF > 2:
-        Chunk(NF - 3).finish()
+    Chunk(NF - 2).line.far_take()
 
     kv_sums = nacc.at[rows_of(*order[1], c), :]
     kv_sums[:, : 4 * HEAD_SIZE] = jnp.zeros((T, 4 * HEAD_SIZE), F32)
@@ -928,6 +1009,7 @@
                 kv_sums[:, vcut] = kv_sums[:, vcut] + grad_values[piece]
 
     loop(HEADS, attend_back)
+    Chunk(NF - 2).line.far_give()
     for i in range(2):
         rows = slice(i * seq, (i + 1) * seq)
         row, cut = cell(HEADS, 0)
@@ -944,6 +1026,7 @@
 
     st[...] = lin_back((1 - y) * T).astype(BF)
     y_copy(st, ar.at[1], 3).start()
+    Chunk(NF - 3).line.cross_take()
 
     def lin_products(i):
         cols = span(i * tile_rows, tile_rows, 128)
@@ -958,21 +1041,26 @@
 
     loop(W // tile_rows, lin_products)
     part_q.send_core()
+    Chunk(NF - 3).line.cross_give()
     part_o.send_x()
+    Chunk(NF - 4).line.last_take()
     grad_lin = nacc.at[rows_of(*order[0], c), :]
     grad_lin[...] = lin_back(y * T)
     for side in range(2):
         cut = slice(side * half_cols, (side + 1) * half_cols)
         sums = jnp.sum(gu[side * TT : (side + 1) * TT, :].astype(F32), axis=0, keepdims=True)
         sv[2:3, cut] = sums
+    Chunk(NF - 4).finish_give()
     part_q.send_x()
+    Chunk(NF - 2).line.cross_take()
     tokens_again = ga.at[other_half, :]
     y_copy(ga.at[own_half, :], ga.at[own_half, :], 2).wait_send()
     local(tok_ref, tokens_again, loc.at[1]).start()
+    Chunk(NF - 2).line.cross_give()
     part_o.send_along()
-    Chunk(NF - 1).line.middle()
-    if NF > 1:
-        Chunk(NF - 2).finish()
+    Chunk(NF - 3).finish()
+    Chunk(NF - 1).line.far_take()
+    Chunk(NF - 1).line.far_give()
     part_q.send_along()
     local(tok_ref, tokens_again, loc.at[1]).wait()
     y_copy(st, ar.at[1], 3).wait()
@@ -1015,7 +1103,9 @@
         small(dq, dy).start()
     svr[q * 2 + y] = sv[...]
 
-    part_o.line.middle()
+    Chunk(NF - 2).finish()
+    part_o.line.far_take()
+    part_o.line.far_give()
 
     def layer_out(a, total):
         tk[a, :] = (mid[a, :] + total).astype(BF)
@@ -1036,9 +1126,17 @@
     for step in range(1, O):
         small_along(step).start()
     svz[o] = sv[...]
-    part_q.line.middle()
+    part_q.line.far_take()
+    part_q.line.far_give()
+    Chunk(NF - 1).line.cross_take()
+    Chunk(NF - 1).line.cross_give()
+    part_o.line.cross_take()
+    part_o.line.cross_give()
+    part_q.line.cross_take()
+    part_q.line.cross_give()
     Chunk(NF - 1).finish()
-    part_o.line.last()
+    part_o.line.last_take()
+    part_o.line.last_give()
     local(part_o.line.block(0, o), gao_ref, loc.at[3]).start()
     for step in range(1, O):
         small_along_from(step).wait_recv()
@@ -1048,7 +1146,8 @@
         total = total + svz[i]
     sv[...] = total
     local(sv, sums_ref, loc.at[8]).start()
-    part_q.line.last()
+    part_q.line.last_take()
+    part_q.line.last_give()
     for k in range(NQ):
         local(part_q.line.block(k, o), gaq_ref.at[k], loc.at[4 + k]).start()
 
@@ -1093,8 +1192,8 @@
         out((NF, H, H * R4, B), BF),
         out((H, R4, A), BF),
         out((NF, H, R4, B), BF),
-        out((R4, A), BF),
-        out((NF, R4, B), BF),
+        out((H * R4, A), BF),
+        out((NF, H * R4, B), BF),
         out((2, 4, T, W), F32),
         out((2, 3, T, W), BF),
         out((sz.dp * RP, GW), BF),
@@ -1107,8 +1206,8 @@
         out((H, H * RP, QW), BF),
         out((NQ, H, RP, WIDE), BF),
         out((H, RP, QW), BF),
-        out((NQ, RP, WIDE), BF),
-        out((RP, QW), BF),
+        out((NQ, H * RP, WIDE), BF),
+        out((H * RP, QW), BF),
     ]
     if not sz.whole:
         outs += [out((QUADS, RP, A), BF), out((NF, QUADS, RP, B), BF)]
@@ -1143,19 +1242,19 @@
         dma((NF + 1, H)),
         dma((NF + 1, H)),
         dma((NF + 1,)),
-        dma((NF + 1, H)),
+        dma((NF + 1,)),
         dma((NF + 1, H)),
         dma((NF + 1,)),
         dma((NL,)),
         dma((NL, H)),
         dma((NL, H)),
         dma((NL, H)),
-        dma((NL, H)),
+        dma((NL,)),
         dma((NL,)),
         dma((NF + 1, 4)),
         dma((NF + 1, 3)),
-        dma((2, 7)),
-        dma((2, 7)),
+        dma((2, 9)),
+        dma((2, 9)),
         dma((2, 7)),
         dma((2, 7)),
         dma((4,)),
@@ -1174,7 +1273,7 @@
         dma((2 * QUADS,)),
         dma((O,)),
         dma((O,)),
-        dma((12,)),
+        dma((20,)),
     ]
     if not sz.whole:
         scratch += [vm((QUADS * RP, max(B, GW)), BF), vm((R4, B), BF)]

time: 548 us -> 487 us (0.89); the launches traced: 540 us -> 485 us
  Pallas kernels: 489 us -> 434 us
    pallas_call x1, Pallas kernels: 489 us -> 434 us  [layer(): pl.pallas_call(lambda *refs: layer_kernel(sz, *refs), out_shape=outs, in_...]
where the time goes in v3:
time: 487 us; the launch traced here: 485 us
  Pallas kernels  434 us (89%)
  local copies, waits for them, and re-layouts  40.9 us (8%)
  other arithmetic  9.94 us (2%)
    pallas_call x1, Pallas kernels, layer(): pl.pallas_call(lambda *refs: layer_kernel(sz, *refs), out_shape=outs, in_...  434 us

profile of v3, /device:TPU:0, one launch (start us, length us, event | category | flops | bytes accessed | tf_op | source)
XLA Modules:
  0.0 485.3 jit_solution(16355517384002851624)
XLA Ops:
  0.7 0.9 fusion.17
  1.6 0.7 stack.35
  2.3 0.7 stack.36
  3.0 0.6 fusion.12.refs_6_
  3.6 1.6 pad_maximum_fusion.1.refs_2_
  5.3 0.9 maximum_cosine_fusion
  6.2 0.9 maximum_sine_fusion
  7.5 0.8 pad_maximum_fusion.refs_7_
  8.3 0.5 fusion.4
  8.8 2.3 reshape.163
  11.1 1.7 slice-done.1
  12.8 2.3 reshape.172
  15.3 1.0 reshape.164.refs_4_
  16.3 3.7 copy.38
  20.0 4.6 reshape.166.refs_5_
  24.6 433.6 %layer.1 = (bf16[4,96,384]{2,1,0:T(8,128)(2,1)}, bf16[4,4,96,768]{3,2,1,0:T(8,128)(2,1)}, bf16[4,96,256]{2,1,0:T(8,128)(2,1)}, bf16[96,768]{1,0:T(8,128)(2,1)}, ...) custom-call(bf16[256,1536]{1,0:T(8,128)(2,1)} %refs_0_.1, ...), custom_call_target="tpu_custom_call" | custom-call | tf_op jit(solution)/shard_map/layer/pallas_call | solution.py:1282
  458.3 1.2 slice_bitcast_fusion.3
  459.5 1.3 slice_reduce_fusion.2
  460.9 1.5 slice_reduce_fusion
  462.4 1.6 convert_bitcast_fusion.1
  464.0 1.0 convert_bitcast_fusion
  465.0 0.7 fusion.18
  465.7 0.7 slice.68
  466.5 4.6 reshape.168
  471.1 3.6 copy.40
  474.8 4.3 reshape.169
  479.1 0.3 maximum_bitcast_fusion
  479.7 0.3 slice_convert_fusion
  480.0 2.4 slice_bitcast_fusion
  482.5 0.9 copy.53
  483.4 0.8 copy-done
  484.2 1.1 copy.54
  (24 shorter events, 1.1 us)
Async XLA Ops:
  0.6 7.7 %copy-start.1 = (bf16[4480,96]{0,1:T(8,128)(2,1)S(1)}, bf16[4480,96]{0,1:T(8,128)(2,1)}, u32[]{:S(2)}) copy-start(bf16[4480,96]{0,1:T(8,128)(2,1)} %param.26) | copy-start | bytes 2580484
  0.7 7.6 %copy-start.2 = (bf16[96,4480]{1,0:T(8,128)(2,1)S(1)}, bf16[96,4480]{1,0:T(8,128)(2,1)}, u32[]{:S(2)}) copy-start(bf16[96,4480]{1,0:T(8,128)(2,1)} %param.25) | copy-start | bytes 2580484
  0.7 7.6 %copy-start.3 = (bf16[96,4480]{1,0:T(8,128)(2,1)S(1)}, bf16[96,4480]{1,0:T(8,128)(2,1)}, u32[]{:S(2)}) copy-start(bf16[96,4480]{1,0:T(8,128)(2,1)} %param.24) | copy-start | bytes 2580484
  11.1 1.7 slice-start.1
  12.8 2.3 slice-start
  458.3 8.1 %copy-start.5 = (bf16[4,96,384]{2,1,0:T(8,128)(2,1)S(1)}, bf16[4,96,384]{2,1,0:T(8,128)(2,1)}, u32[]{:S(2)}) copy-start(bf16[4,96,384]{2,1,0:T(8,128)(2,1)} %get-tuple-element.26) | copy-start | bytes 884740
  480.0 2.5 copy-start.4
  482.5 1.7 copy-start

commit v4 on v3

--- a/solution.py
+++ b/solution.py
@@ -2,6 +2,7 @@
 
 import jax
 import jax.numpy as jnp
+import numpy as np
 from jax import lax
 from jax.experimental import pallas as pl
 from jax.experimental.pallas import tpu as pltpu
@@ -24,12 +25,13 @@
 
 def rope_tables(length, columns):
     midway = columns // 2
-    inverse = jnp.exp(
-        jnp.arange(midway, dtype=jnp.float32) * (-2.0 * math.log(rope_base) / columns)
+    inverse = np.exp(
+        np.arange(midway, dtype=np.float32) * np.float32(-2.0 * math.log(rope_base) / columns)
     )
-    angles = jnp.arange(length, dtype=jnp.float32)[:, None] * inverse[None, :]
-    angles = jnp.concatenate([angles, angles], axis=-1)
-    return (jnp.cos(angles)[None, :, None, :], jnp.sin(angles)[None, :, None, :])
+    angles = np.arange(length, dtype=np.float32)[:, None] * inverse[None, :].astype(np.float32)
+    cosine, sine = np.cos(angles.astype(np.float64)), np.sin(angles.astype(np.float64))
+    tables = np.stack([np.concatenate([cosine, cosine], -1), np.concatenate([-sine, sine], -1)])
+    return tables.astype(np.float32)
 
 
 def dot_rows(left, right):
@@ -56,9 +58,9 @@
         self.pad = round_up(self.rows, 16)
         self.whole = self.pad == self.rows
         self.wide = dp * self.rows
-        self.slice = round_up(-(-self.hidden // QUADS), 128)
-        self.head = self.slice % WIDE or WIDE
-        self.full = (self.slice - self.head) // WIDE
+        self.full = (self.hidden - 1) // (QUADS * WIDE)
+        self.rest = self.hidden - self.full * QUADS * WIDE
+        self.head = round_up(-(-self.rest // QUADS), 128)
         self.tokens, self.query, self.key = tokens, query, key
 
 
@@ -68,8 +70,9 @@
     def some(n):
         return [next(refs) for _ in range(n)]
 
-    tok_ref, cot_ref, wq_ref, wo_ref, wh_ref, wf_ref, vec, rope = some(8)
-    gh_ref, gf_ref, gaq_ref, gao_ref, mixed_ref, gtok_ref, sums_ref = some(7)
+    tok_ref, cot_ref, wq_ref, wo_ref, wh_ref, wg_ref, wu_ref, wd_ref, vec, rope = some(10)
+    gw_refs = some(3)
+    gwq_ref, gwk_ref, gwv_ref, gao_ref, mixed_ref, gtok_ref, sums_ref, gh_ref, gf_ref = some(9)
     wagh, wagf, colh, colf, nearh, nearf, outh, outf = some(8)
     pairbuf, chipbuf, gq, go = some(4)
     rcq, rco, rxq, rxo, colq, colo, nearq, nearo, outq, outo = some(10)
@@ -89,6 +92,7 @@
     QW = sz.query
     GW = sz.query + 2 * sz.key
     HEADS = QW // HEAD_SIZE
+    PIECES = -(-sz.hidden // W)
     FACTOR = 1.0 / math.sqrt(HEAD_SIZE)
     me = lax.axis_index("dp")
     y = lax.axis_index("tensor")
@@ -269,14 +273,16 @@
             self.head = kk is None
             if self.head:
                 self.i, self.fk = 0, HK
-                self.src, self.wag, self.pb, self.out = wh_ref, wagh, pbh, gh_ref
+                self.wag, self.pb, self.out = wagh, pbh, gh_ref
+                self.moves = [(wh_ref.at, pl.ds(0, 3 * HK))]
                 self.hid, self.ab = hh, abh
                 col, near, out = colh, nearh, outh
             else:
                 self.i, self.fk = kk + 1, WIDE
-                self.src, self.wag, self.pb, self.out = (
-                    wf_ref.at[kk], wagf.at[kk], pb.at[kk], gf_ref.at[kk],
-                )
+                self.kk, self.wag, self.pb, self.out = kk, wagf.at[kk], pb.at[kk], gf_ref.at[kk]
+                self.moves = [
+                    (ref, pl.ds(m * WIDE, WIDE)) for m, ref in enumerate((wg_ref, wu_ref, wd_ref))
+                ]
                 self.hid, self.ab = hf.at[kk], None if abf is None else abf.at[kk]
                 col, near, out = colf.at[kk], nearf.at[kk], outf.at[kk]
             self.cols = pl.ds(0, 3 * self.fk)
@@ -292,20 +298,25 @@
         def mine(self):
             return self.part(self.wag, o, q) if sz.whole else self.ab.at[q]
 
-        def a2a(self, dq):
+        def source(self, m, to):
+            ref = self.moves[m][0]
+            return wh_ref.at[to] if self.head else ref.at[:, span((self.kk * QUADS + to) * WIDE, WIDE, WIDE)]
+
+        def a2a(self, m, dq):
             to = lax.rem(q + dq, QUADS)
             return remote(
-                self.src.at[to], self.mine(),
-                s_a2a.at[self.i, dq - 1], r_a2a.at[self.i, dq - 1], at(o, to, y),
+                self.source(m, to), self.mine().at[:, self.moves[m][1]],
+                s_a2a.at[self.i, m, dq - 1], r_a2a.at[self.i, m, dq - 1], at(o, to, y),
             )
 
-        def a2a_own(self):
-            return local(self.src.at[q], self.mine(), s_a2a.at[self.i, 3])
+        def a2a_own(self, m):
+            return local(self.source(m, q), self.mine().at[:, self.moves[m][1]], s_a2a.at[self.i, m, 3])
 
         def a2a_start(self):
-            self.a2a_own().start()
-            for dq in (1, 2, 3):
-                self.a2a(dq).start()
+            for m in range(len(self.moves)):
+                self.a2a_own(m).start()
+                for dq in (1, 2, 3):
+                    self.a2a(m, dq).start()
 
         def join(self):
             for i in range(QUADS):
@@ -331,9 +342,10 @@
             )
 
         def gather_own(self):
-            self.a2a_own().wait()
-            for dq in (1, 2, 3):
-                self.a2a(dq).wait_recv()
+            for m in range(len(self.moves)):
+                self.a2a_own(m).wait()
+                for dq in (1, 2, 3):
+                    self.a2a(m, dq).wait_recv()
             if not sz.whole:
                 self.join()
             for t in range(H):
@@ -361,8 +373,9 @@
                 self.forward(1 - half, pos).wait_recv()
 
         def gather_sent(self):
-            for dq in (1, 2, 3):
-                self.a2a(dq).wait_send()
+            for m in range(len(self.moves)):
+                for dq in (1, 2, 3):
+                    self.a2a(m, dq).wait_send()
             pl.when(is_middle)(lambda: self.half_far(half).wait_send())
             for t in range(H):
 
@@ -408,10 +421,30 @@
             for dq in (1, 2, 3):
                 self.give(dq).start()
 
-        def finished(self):
+        def collect(self):
             self.give_own().wait()
             for dq in (1, 2, 3):
-                self.give(dq).wait()
+                self.give(dq).wait_recv()
+
+            def rows(i):
+                return wv.at[span(i * RP, RP, RP), self.cols]
+
+            for i in range(QUADS):
+                local(self.out.at[i], rows(i), loc.at[16 + i]).start()
+            for i in range(QUADS):
+                local(self.out.at[i], rows(i), loc.at[16 + i]).wait()
+                if self.head:
+                    first, n = NF * QUADS * WIDE + i * HK, min(HK, sz.rest - i * HK)
+                else:
+                    first, n = (self.kk * QUADS + i) * WIDE, WIDE
+                if n > 0:
+                    for m in range(3):
+                        to = span((m * PIECES + first // W) * RP, RP, RP)
+                        nacc[to, span(first % W, n, 128)] = rows(i)[:, m * self.fk : m * self.fk + n].astype(F32)
+
+        def finished(self):
+            for dq in (1, 2, 3):
+                self.give(dq).wait_send()
             self.gather_sent()
             self.line.sent()
 
@@ -494,6 +527,8 @@
             total = here[a, :] + spare[a, :]
             if n < 3:
                 nsd[n, a, :] = total.astype(BF)
+            elif which == 0:
+                own[a, :] = total
             else:
                 here[a, :] = total
 
@@ -502,7 +537,7 @@
             sum_chip(n, which).start()
 
     def sum_close(which, finish):
-        here = nacc.at[mine, :]
+        here = own if which == 0 else nacc.at[mine, :]
         for n in range(3):
             sum_chip(n, which).wait_recv()
             move(chipbuf.at[which, n], tk, loc.at[7])
@@ -562,11 +597,11 @@
                 self.send(step).wait_recv()
                 self.over(step).start()
                 self.across(step, 0).start()
-
-        def pass_over(self):
-            for step in range(O):
-                self.over(step).wait_recv()
-                self.across(step, 1).start()
+                self.pass_over(step - 1)
+
+        def pass_over(self, step):
+            self.over(step).wait_recv()
+            self.across(step, 1).start()
 
         def wait(self):
             for far_x in range(2):
@@ -642,9 +677,9 @@
     head.gather_own()
     gather_q.pass_on()
     gather_o.start()
+    gather_q.pass_over(O - 1)
+    Chunk(0).gather_own()
     head.gather_half()
-    gather_q.pass_over()
-    Chunk(0).gather_own()
     gather_q.wait()
     wq_v, wr_v, wo_v = pb.at[0], pb.at[1, :, pl.ds(0, 2 * sz.key)], pb.at[2]
     ready = fetch([(gq, QUERY, wq_v), (gq, REST, wr_v)], 1)
@@ -690,7 +725,7 @@
             mh[rows, qcol] = dot_rows(probs, qkv[0 : (part + 1) * seq, vcol]).astype(BF)
 
     loop(HEADS, attend)
-    gather_o.pass_over()
+    gather_o.pass_over(O - 1)
     Chunk(1).gather_own()
     gather_o.wait()
     ready = fetch([(go, pl.ds(0, QW), wo_v)], 1)
@@ -840,11 +875,6 @@
         tk[a, :] = total.astype(BF)
         sv[1:2, :] = sv[1:2, :] + jnp.sum(grad * values * scale, axis=0, keepdims=True)
 
-    sum_close(0, back_second)
-    ga[own_half, :] = tk[...]
-    y_copy(ga.at[own_half, :], ga.at[own_half, :], 2).start()
-    Chunk(NF - 3).line.far_take()
-
     def m_load(kk):
         return local(
             wagf.at[kk, :, pl.ds(2 * WIDE, WIDE)], wv.at[:, span(lax.rem(kk, 2) * WIDE, WIDE, WIDE)], loc.at[8],
@@ -858,7 +888,6 @@
         nacc[rows, :] = dot_right(hh[rows, :], wv[:, 2 * WIDE : 2 * WIDE + HK])
 
     loop(4, m_first)
-    Chunk(NF - 3).line.far_give()
 
     def m_chunk(kk):
         m_load(kk).wait()
@@ -876,6 +905,11 @@
     loop(NF, m_chunk)
     for n in range(4):
         sum_pair(n, 1).start()
+    Chunk(NF - 3).line.far_take()
+    sum_close(0, back_second)
+    ga[own_half, :] = tk[...]
+    y_copy(ga.at[own_half, :], ga.at[own_half, :], 2).start()
+    Chunk(NF - 3).line.far_give()
     for n in range(4):
         sum_take(n, 1)
     for n in range(4):
@@ -967,15 +1001,19 @@
             self.line.sent()
 
     NQ = GW // WIDE
-    temp_q = [
-        xb.at[pl.ds((k // 2) * HR, HR), pl.ds(GW + (k % 2) * WIDE, WIDE)] for k in range(NQ)
-    ]
-    part_q = Part(
-        0, [hf.at[k] for k in range(NQ)], temp_q,
-        [rcq.at[k] for k in range(NQ)], [rxq.at[k] for k in range(NQ)],
-        [colq.at[k] for k in range(NQ)], [nearq.at[k] for k in range(NQ)],
-        [outq.at[k] for k in range(NQ)],
-    )
+
+    def side_part(side):
+        ks = range(side * NQ // 2, (side + 1) * NQ // 2)
+        temps = [xb.at[pl.ds((k // 2) * HR, HR), pl.ds(GW + (k % 2) * WIDE, WIDE)] for k in ks]
+
+        def each(ref):
+            return [ref.at[k] for k in ks]
+
+        return Part(
+            ks[0], each(hf), temps, each(rcq), each(rxq), each(colq), each(nearq), each(outq)
+        )
+
+    part_a, part_b = side_part(0), side_part(1)
     part_o = Part(
         NQ, [cb.at[:, out_cols]], [rt.at[:, pl.ds(0, QW)]], [rco], [rxo], [colo], [nearo], [outo]
     )
@@ -1008,41 +1046,50 @@
                 kv_sums[:, kcut] = kv_sums[:, kcut] + grad_keys[piece]
                 kv_sums[:, vcut] = kv_sums[:, vcut] + grad_values[piece]
 
-    loop(HEADS, attend_back)
+    half_cols = 2 * WIDE
+
+    def lin_products(side):
+        def step(i):
+            cols = span(i * tile_rows, tile_rows, 128)
+            values = dot_left(xa[:, cols], gu[side * TT : (side + 1) * TT, :])
+
+            def store(rows, part):
+                hf[2 * side, rows, :] = part[:, :WIDE]
+                hf[2 * side + 1, rows, :] = part[:, WIDE:]
+
+            spread_rows(i, values, store)
+
+        loop(W // tile_rows, step)
+
+    def lin_back(start):
+        return dot_right(
+            gu[span(start, T, T), :], wq_b[:, :half_cols]
+        ) + dot_right(gu[span(TT + start, T, T), :], wq_b[:, half_cols:])
+
+    def heads_back(first, n):
+        loop(n, lambda h: attend_back(first + h))
+
+    heads_back(0, PER)
     Chunk(NF - 2).line.far_give()
+    lin_products(0)
+    part_a.send_core()
+    part_o.send_x()
+    heads_back(PER, HEADS - PER)
     for i in range(2):
         rows = slice(i * seq, (i + 1) * seq)
         row, cut = cell(HEADS, 0)
         gu[pl.ds(row + i * seq, seq), cut] = turn(kv_sums[:, head_cols(i)], -1.0, rows).astype(BF)
         row, cut = cell(HEADS + 1, 0)
         gu[pl.ds(row + i * seq, seq), cut] = kv_sums[:, head_cols(2 + i)].astype(BF)
-
-    half_cols = 2 * WIDE
-
-    def lin_back(start):
-        return dot_right(
-            gu[span(start, T, T), :], wq_b[:, :half_cols]
-        ) + dot_right(gu[span(TT + start, T, T), :], wq_b[:, half_cols:])
-
+    lin_products(1)
+    part_b.send_core()
+    part_a.send_x()
+    Chunk(NF - 3).line.cross_take()
     st[...] = lin_back((1 - y) * T).astype(BF)
     y_copy(st, ar.at[1], 3).start()
-    Chunk(NF - 3).line.cross_take()
-
-    def lin_products(i):
-        cols = span(i * tile_rows, tile_rows, 128)
-        for side in range(2):
-            values = dot_left(xa[:, cols], gu[side * TT : (side + 1) * TT, :])
-
-            def store(rows, part):
-                hf[2 * side, rows, :] = part[:, :WIDE]
-                hf[2 * side + 1, rows, :] = part[:, WIDE:]
-
-            spread_rows(i, values, store)
-
-    loop(W // tile_rows, lin_products)
-    part_q.send_core()
     Chunk(NF - 3).line.cross_give()
-    part_o.send_x()
+    part_b.send_x()
+    part_o.send_along()
     Chunk(NF - 4).line.last_take()
     grad_lin = nacc.at[rows_of(*order[0], c), :]
     grad_lin[...] = lin_back(y * T)
@@ -1051,17 +1098,20 @@
         sums = jnp.sum(gu[side * TT : (side + 1) * TT, :].astype(F32), axis=0, keepdims=True)
         sv[2:3, cut] = sums
     Chunk(NF - 4).finish_give()
-    part_q.send_x()
+    part_a.send_along()
     Chunk(NF - 2).line.cross_take()
     tokens_again = ga.at[other_half, :]
     y_copy(ga.at[own_half, :], ga.at[own_half, :], 2).wait_send()
     local(tok_ref, tokens_again, loc.at[1]).start()
     Chunk(NF - 2).line.cross_give()
-    part_o.send_along()
+    part_b.send_along()
     Chunk(NF - 3).finish()
     Chunk(NF - 1).line.far_take()
     Chunk(NF - 1).line.far_give()
-    part_q.send_along()
+    part_o.line.far_take()
+    part_o.line.far_give()
+    part_a.line.far_take()
+    part_a.line.far_give()
     local(tok_ref, tokens_again, loc.at[1]).wait()
     y_copy(st, ar.at[1], 3).wait()
 
@@ -1103,9 +1153,9 @@
         small(dq, dy).start()
     svr[q * 2 + y] = sv[...]
 
+    part_b.line.far_take()
+    part_b.line.far_give()
     Chunk(NF - 2).finish()
-    part_o.line.far_take()
-    part_o.line.far_give()
 
     def layer_out(a, total):
         tk[a, :] = (mid[a, :] + total).astype(BF)
@@ -1126,18 +1176,14 @@
     for step in range(1, O):
         small_along(step).start()
     svz[o] = sv[...]
-    part_q.line.far_take()
-    part_q.line.far_give()
     Chunk(NF - 1).line.cross_take()
     Chunk(NF - 1).line.cross_give()
-    part_o.line.cross_take()
-    part_o.line.cross_give()
-    part_q.line.cross_take()
-    part_q.line.cross_give()
+    for part in (part_o, part_a, part_b):
+        part.line.cross_take()
+        part.line.cross_give()
+    head.collect()
+    loop(NF - 1, lambda kk: Chunk(kk).collect())
     Chunk(NF - 1).finish()
-    part_o.line.last_take()
-    part_o.line.last_give()
-    local(part_o.line.block(0, o), gao_ref, loc.at[3]).start()
     for step in range(1, O):
         small_along_from(step).wait_recv()
         small_along(step).wait_send()
@@ -1146,27 +1192,48 @@
         total = total + svz[i]
     sv[...] = total
     local(sv, sums_ref, loc.at[8]).start()
-    part_q.line.last_take()
-    part_q.line.last_give()
-    for k in range(NQ):
-        local(part_q.line.block(k, o), gaq_ref.at[k], loc.at[4 + k]).start()
-
+    low = span(3 * PIECES * RP, RP, RP)
+    lower = span((3 * PIECES + 1) * RP, RP, RP)
+    for part in (part_o, part_a, part_b):
+        part.line.last_take()
+        part.line.last_give()
+    nacc[low, :QW] = part_o.line.block(0, o)[...].astype(F32)
+    for side, part in enumerate((part_a, part_b)):
+        for k in range(NQ // 2):
+            cut = slice((side * NQ // 2 + k) * WIDE, (side * NQ // 2 + k + 1) * WIDE)
+            nacc[lower, cut] = part.line.block(k, o)[...].astype(F32)
+    outputs = [
+        local(nacc.at[low, pl.ds(0, QW)], gao_ref, loc.at[3]),
+        local(nacc.at[lower, QUERY], gwq_ref, loc.at[4]),
+        local(nacc.at[lower, KEY], gwk_ref, loc.at[5]),
+        local(nacc.at[lower, VALUE], gwv_ref, loc.at[6]),
+    ]
+    for copy in outputs:
+        copy.start()
+    Chunk(NF - 1).collect()
+    for m in range(3):
+        for j in range(PIECES):
+            n = min(W, sz.hidden - j * W)
+            here = nacc.at[pl.ds((m * PIECES + j) * RP, RP), pl.ds(0, n)]
+            outputs.append(local(here, gw_refs[m].at[:, pl.ds(j * W, n)], loc.at[20 + m * PIECES + j]))
+            outputs[-1].start()
+
+    for copy in outputs:
+        copy.wait()
     gather_q.sent()
     gather_o.sent()
     y_copy(xa.at[own_half, :], xa.at[own_half, :], 0).wait_send()
     part_o.sent()
-    part_q.sent()
+    part_a.sent()
+    part_b.sent()
     head.finished()
     loop(NF, lambda kk: Chunk(kk).finished())
     local(own, gtok_ref, loc.at[1]).wait()
     local(tk, mixed_ref, loc.at[2]).wait()
-    local(part_o.line.block(0, o), gao_ref, loc.at[3]).wait()
     local(sv, sums_ref, loc.at[8]).wait()
-    for k in range(NQ):
-        local(part_q.line.block(k, o), gaq_ref.at[k], loc.at[4 + k]).wait()
-
-
-def layer(sz, tokens, cotangent, wq, wo, wh, wf, vec, rope):
+
+
+def layer(sz, tokens, cotangent, wq, wo, wh, wg, wu, wd, vec, rope):
     O, NF, T = sz.outer, sz.full, sz.tokens
     H = O // 2
     HK, W, RP = sz.head, sz.wide, sz.pad
@@ -1177,15 +1244,21 @@
     PT = 2 * QUADS * T
     NL = NF + 1 + NQ + 1
     A, B = 3 * HK, 3 * WIDE
+    PIECES = -(-sz.hidden // W)
     out = jax.ShapeDtypeStruct
     outs = [
-        out((QUADS, RP, A), BF),
-        out((NF, QUADS, RP, B), BF),
-        out((NQ, RP, WIDE), BF),
-        out((RP, QW), BF),
+        out((RP, sz.hidden), F32),
+        out((RP, sz.hidden), F32),
+        out((RP, sz.hidden), F32),
+        out((RP, QW), F32),
+        out((RP, sz.key), F32),
+        out((RP, sz.key), F32),
+        out((RP, QW), F32),
         out((T, W), BF),
         out((T, W), F32),
         out((8, W), F32),
+        out((QUADS, RP, A), BF),
+        out((NF, QUADS, RP, B), BF),
         out((W, A), BF),
         out((NF, W, B), BF),
         out((H, H * R4, A), BF),
@@ -1237,8 +1310,8 @@
         vm((8, W), F32),
         vm((2 * QUADS, 8, W), F32),
         vm((O, 8, W), F32),
-        dma((NF + 1, 4)),
-        dma((NF + 1, 3)),
+        dma((NF + 1, 3, 4)),
+        dma((NF + 1, 3, 3)),
         dma((NF + 1, H)),
         dma((NF + 1, H)),
         dma((NF + 1,)),
@@ -1273,7 +1346,7 @@
         dma((2 * QUADS,)),
         dma((O,)),
         dma((O,)),
-        dma((20,)),
+        dma((20 + 3 * PIECES,)),
     ]
     if not sz.whole:
         scratch += [vm((QUADS * RP, max(B, GW)), BF), vm((R4, B), BF)]
@@ -1282,15 +1355,15 @@
     results = pl.pallas_call(
         lambda *refs: layer_kernel(sz, *refs),
         out_shape=outs,
-        in_specs=[any_spec] * 6 + [vmem_spec] * 2,
+        in_specs=[any_spec] * 8 + [vmem_spec] * 2,
         out_specs=[any_spec] * len(outs),
         scratch_shapes=scratch,
         compiler_params=pltpu.CompilerParams(
             collective_id=0, has_side_effects=True, vmem_limit_bytes=64 << 20
         ),
         name="layer",
-    )(tokens, cotangent, wq, wo, wh, wf, vec, rope)
-    return results[:7]
+    )(tokens, cotangent, wq, wo, wh, wg, wu, wd, vec, rope)
+    return results[:10]
 
 
 def per_device(
@@ -1310,52 +1383,45 @@
     w_down,
     cotangent,
 ):
-    rows, hidden_units = w_gate.shape
+    rows = sz.rows
     more = sz.pad - sz.rows
-    w3 = jnp.stack([w_gate, w_up, w_down.T])
-    w3 = jnp.pad(w3, ((0, 0), (0, more), (0, QUADS * sz.slice - hidden_units)))
-    w3 = w3.reshape(3, sz.pad, QUADS, sz.slice)
-    wh = w3[..., : sz.head].transpose(2, 1, 0, 3).reshape(QUADS, sz.pad, 3 * sz.head)
-    wf = w3[..., sz.head :].reshape(3, sz.pad, QUADS, sz.full, WIDE)
-    wf = wf.transpose(3, 2, 1, 0, 4).reshape(sz.full, QUADS, sz.pad, 3 * WIDE)
+
+    def fill(values):
+        return jnp.pad(values, ((0, more), (0, 0))) if more else values
+
+    wg, wu, wd = fill(w_gate), fill(w_up), fill(w_down.T)
+    start = sz.hidden - sz.rest
+    wh = jnp.stack([wg[:, start:], wu[:, start:], wd[:, start:]], axis=1)
+    wh = jnp.pad(wh, ((0, 0), (0, 0), (0, QUADS * sz.head - sz.rest)))
+    wh = wh.reshape(sz.pad, 3, QUADS, sz.head).transpose(2, 0, 1, 3)
+    wh = wh.reshape(QUADS, sz.pad, 3 * sz.head)
     wq = jnp.concatenate([w_query, key_weight, value_weight], axis=1)
-    wq = jnp.pad(wq, ((0, more), (0, 0)))
-    wo = jnp.pad(w_out.T, ((0, more), (0, 0)))
+    wq, wo = fill(wq), fill(w_out.T)
     bias = jnp.concatenate([b_query, key_bias, value_bias]).astype(F32)
     bias = jnp.pad(bias, (0, sz.wide - bias.shape[0]))
     vec = jnp.stack([gain_attn.astype(F32), gain_mlp.astype(F32), bias])
     vec = jnp.pad(vec, ((0, 5), (0, 0)))
-    cosine, sine = rope_tables(SEQUENCE_TOKENS, HEAD_SIZE)
-    midway = HEAD_SIZE // 2
-    signed = jnp.concatenate([-sine[..., :midway], sine[..., midway:]], axis=-1)
-    rope = jnp.stack([cosine[0, :, 0, :], signed[0, :, 0, :]])
-
-    grad_head, grad_full, grad_q, grad_o, mixed, grad_tokens, sums = layer(
-        sz, tokens, cotangent, wq, wo, wh, wf, vec, rope
+    rope = jnp.asarray(rope_tables(SEQUENCE_TOKENS, HEAD_SIZE))
+
+    grad_gate, grad_up, grad_down, grad_q, grad_k, grad_v, grad_o, mixed, grad_tokens, sums = layer(
+        sz, tokens, cotangent, wq, wo, wh, wg, wu, wd, vec, rope
     )
-    grad_head = grad_head.reshape(QUADS, sz.pad, 3, sz.head).transpose(2, 1, 0, 3)
-    grad_full = grad_full.reshape(sz.full, QUADS, sz.pad, 3, WIDE).transpose(3, 2, 1, 0, 4)
-    grad_full = grad_full.reshape(3, sz.pad, QUADS, sz.full * WIDE)
-    grads = jnp.concatenate([grad_head, grad_full], axis=-1)
-    grads = grads.reshape(3, sz.pad, QUADS * sz.slice)[:, :rows, :hidden_units].astype(F32)
-    grad_q = grad_q.transpose(1, 0, 2).reshape(sz.pad, -1)[:rows].astype(F32)
-    grad_o = grad_o[:rows].astype(F32)
     cuts = (sz.query, sz.query + sz.key, sz.query + 2 * sz.key)
     return (
         mixed,
         grad_tokens,
-        grad_q[:, : cuts[0]],
-        grad_q[:, cuts[0] : cuts[1]],
-        grad_q[:, cuts[1] :],
+        grad_q[:rows],
+        grad_k[:rows],
+        grad_v[:rows],
         sums[2, : cuts[0]],
         sums[2, cuts[0] : cuts[1]],
         sums[2, cuts[1] : cuts[2]],
-        grad_o.T,
+        grad_o[:rows].T,
         sums[0],
         sums[1],
-        grads[0],
-        grads[1],
-        grads[2].T,
+        grad_gate[:rows],
+        grad_up[:rows],
+        grad_down[:rows].T,
     )
 
 

time: 487 us -> 453 us (0.930)
  local copies, waits for them, and re-layouts: 40.9 us -> 20 us
  other arithmetic: 9.94 us -> 2.14 us
  Pallas kernels: 434 us -> 428 us
    reshape x8 -> x3, local copies, waits for them, and re-layouts: 19.4 us -> 1.3 us  [the longest x1 0.97 us: per_device(): wh = wh.reshape(QUADS, sz.pad, 3 * sz.head)]
    transpose x4 -> x0, local copies, waits for them, and re-layouts: 9.81 us -> none  [the longest x1 3.69 us: per_device(): wf = wf.transpose(3, 2, 1, 0, 4).reshape(sz.full, QUADS, sz.pad, 3 * WIDE)]
    unnamed x15 -> x31, local copies, waits for them, and re-layouts: 3.11 us -> 11.3 us
    pallas_call x1, Pallas kernels: 434 us -> 428 us  [layer(): pl.pallas_call(lambda *refs: layer_kernel(sz, *refs), out_shape=outs, in_...]
where the time goes in v4:
time: 453 us; the launch traced here: 451 us
  Pallas kernels  428 us (94%)
  local copies, waits for them, and re-layouts  20 us (4%)
    pallas_call x1, Pallas kernels, layer(): pl.pallas_call(lambda *refs: layer_kernel(sz, *refs), out_shape=outs, in_...  428 us
    unnamed x31, local copies, waits for them, and re-layouts  11.3 us

profile of v4, /device:TPU:0, one launch (start us, length us, event | category | flops | bytes accessed | tf_op | source)
XLA Modules:
  0.0 451.0 jit_solution(5200539201784294309)
XLA Ops:
  0.6 0.0 copy-start.9
  0.7 0.0 copy-start.10
  0.7 0.0 copy-start.6
  0.7 0.8 fusion.15
  1.4 0.7 stack.32
  2.1 0.7 stack.33
  2.8 0.6 fusion.10.refs_8_
  3.5 0.9 slice_bitcast_fusion.2
  4.4 0.9 slice_bitcast_fusion
  5.3 0.1 reshape.34
  5.4 0.3 copy.32
  5.7 1.0 reshape.35.refs_4_
  6.7 0.0 copy-done.9
  6.7 0.0 copy-done.10
  6.7 0.7 pad_maximum_fusion.refs_2_
  7.4 428.1 %layer.1 = (f32[96,4480]{1,0:T(8,128)}, f32[96,4480]{1,0:T(8,128)}, f32[96,4480]{1,0:T(8,128)}, f32[96,768]{1,0:T(8,128)}, f32[96,128]{1,0:T(8,128)}, /*index=5*...) custom-call(bf16[256,1536]{1,0:T(8,128)(2,1)} %refs_0_.1, ...), custom_call_target="tpu_custom_call" | custom-call | tf_op jit(solution)/shard_map/layer/pallas_call | solution.py:1355
  435.5 1.3 slice_bitcast_fusion.3
  436.8 1.3 slice_reduce_fusion.2
  438.2 1.5 slice_reduce_fusion
  439.7 2.1 copy.42
  441.8 0.0 copy-start.4
  441.8 0.0 copy-start.2
  441.8 1.1 copy.43
  442.9 0.7 copy.44
  443.6 0.6 copy.45
  444.3 0.6 copy.46
  444.9 0.7 copy.47
  445.6 1.2 copy.48
  446.8 0.9 copy-done.1
  447.7 1.2 copy.49
  448.9 0.9 copy-done
  449.8 1.2 copy.50
  (15 shorter events, 0.1 us)
Async XLA Ops:
  0.6 6.0 %copy-start.9 = (bf16[96,128]{1,0:T(8,128)(2,1)S(1)}, bf16[96,128]{1,0:T(8,128)(2,1)}, u32[]{:S(2)}) copy-start(bf16[96,128]{1,0:T(8,128)(2,1)} %param.18) | copy-start | bytes 73732
  0.7 6.0 %copy-start.10 = (bf16[96,128]{1,0:T(8,128)(2,1)S(1)}, bf16[96,128]{1,0:T(8,128)(2,1)}, u32[]{:S(2)}) copy-start(bf16[96,128]{1,0:T(8,128)(2,1)} %param.17) | copy-start | bytes 73732
  0.7 6.0 %copy-start.6 = (bf16[96,768]{1,0:T(8,128)(2,1)S(1)}, bf16[96,768]{1,0:T(8,128)(2,1)}, u32[]{:S(2)}) copy-start(bf16[96,768]{1,0:T(8,128)(2,1)} %param.16) | copy-start | bytes 442372
  435.5 6.2 %copy-start.3 = (f32[256,1536]{1,0:T(8,128)S(1)}, f32[256,1536]{1,0:T(8,128)}, u32[]{:S(2)}) copy-start(f32[256,1536]{1,0:T(8,128)} %get-tuple-element.55) | copy-start | bytes 4718596
  441.8 1.2 copy-start.5
  441.8 1.9 copy-start.8
  441.8 2.5 copy-start.7
  441.8 3.1 copy-start.4
  441.8 3.8 copy-start.2
  445.6 2.1 copy-start.1
  447.7 2.1 copy-start

commit v5 on v4

--- a/solution.py
+++ b/solution.py
@@ -1088,8 +1088,8 @@
     st[...] = lin_back((1 - y) * T).astype(BF)
     y_copy(st, ar.at[1], 3).start()
     Chunk(NF - 3).line.cross_give()
+    part_o.send_along()
     part_b.send_x()
-    part_o.send_along()
     Chunk(NF - 4).line.last_take()
     grad_lin = nacc.at[rows_of(*order[0], c), :]
     grad_lin[...] = lin_back(y * T)
@@ -1160,8 +1160,8 @@
     def layer_out(a, total):
         tk[a, :] = (mid[a, :] + total).astype(BF)
 
-    sum_close(1, layer_out)
-    local(tk, mixed_ref, loc.at[2]).start()
+    Chunk(NF - 1).line.cross_take()
+    Chunk(NF - 1).line.cross_give()
     for dq, dy in peers:
         small_from(dq, dy).wait_recv()
         small(dq, dy).wait_send()
@@ -1176,11 +1176,11 @@
     for step in range(1, O):
         small_along(step).start()
     svz[o] = sv[...]
-    Chunk(NF - 1).line.cross_take()
-    Chunk(NF - 1).line.cross_give()
     for part in (part_o, part_a, part_b):
         part.line.cross_take()
         part.line.cross_give()
+    sum_close(1, layer_out)
+    local(tk, mixed_ref, loc.at[2]).start()
     head.collect()
     loop(NF - 1, lambda kk: Chunk(kk).collect())
     Chunk(NF - 1).finish()

time: 453 us -> 453 us (level)
  no operation moved by 1% of the time
where the time goes in v5:
time: 453 us; the launch traced here: 448 us
  Pallas kernels  425 us (94%)
  local copies, waits for them, and re-layouts  20 us (4%)
    pallas_call x1, Pallas kernels, layer(): pl.pallas_call(lambda *refs: layer_kernel(sz, *refs), out_shape=outs, in_...  425 us
    unnamed x31, local copies, waits for them, and re-layouts  11.3 us

profile of v5, /device:TPU:0, one launch (start us, length us, event | category | flops | bytes accessed | tf_op | source)
XLA Modules:
  0.0 447.6 jit_solution(4703081275152700546)
XLA Ops:
  0.6 0.0 copy-start.9
  0.7 0.0 copy-start.10
  0.7 0.0 copy-start.6
  0.7 0.8 fusion.15
  1.4 0.7 stack.32
  2.1 0.7 stack.33
  2.8 0.6 fusion.10.refs_8_
  3.5 0.9 slice_bitcast_fusion.2
  4.4 0.9 slice_bitcast_fusion
  5.3 0.1 reshape.34
  5.4 0.3 copy.32
  5.7 1.0 reshape.35.refs_4_
  6.7 0.0 copy-done.9
  6.7 0.0 copy-done.6
  6.7 0.7 pad_maximum_fusion.refs_2_
  7.4 424.7 %layer.1 = (f32[96,4480]{1,0:T(8,128)}, f32[96,4480]{1,0:T(8,128)}, f32[96,4480]{1,0:T(8,128)}, f32[96,768]{1,0:T(8,128)}, f32[96,128]{1,0:T(8,128)}, /*index=5*...) custom-call(bf16[256,1536]{1,0:T(8,128)(2,1)} %refs_0_.1, ...), custom_call_target="tpu_custom_call" | custom-call | tf_op jit(solution)/shard_map/layer/pallas_call | solution.py:1355
  432.1 1.3 slice_bitcast_fusion.3
  433.5 1.3 slice_reduce_fusion.2
  434.8 1.5 slice_reduce_fusion
  436.3 2.1 copy.42
  438.4 0.0 copy-done.3
  438.4 1.1 copy.43
  439.5 0.7 copy.44
  440.3 0.0 copy-done.8
  440.3 0.6 copy.45
  440.9 0.6 copy.46
  441.5 0.7 copy.47
  442.2 1.2 copy.48
  443.4 0.9 copy-done.1
  444.3 1.2 copy.49
  445.5 0.9 copy-done
  446.4 1.2 copy.50
  (15 shorter events, 0.1 us)
Async XLA Ops:
  0.6 6.0 %copy-start.9 = (bf16[96,128]{1,0:T(8,128)(2,1)S(1)}, bf16[96,128]{1,0:T(8,128)(2,1)}, u32[]{:S(2)}) copy-start(bf16[96,128]{1,0:T(8,128)(2,1)} %param.18) | copy-start | bytes 73732
  0.7 6.0 %copy-start.10 = (bf16[96,128]{1,0:T(8,128)(2,1)S(1)}, bf16[96,128]{1,0:T(8,128)(2,1)}, u32[]{:S(2)}) copy-start(bf16[96,128]{1,0:T(8,128)(2,1)} %param.17) | copy-start | bytes 73732
  0.7 6.0 %copy-start.6 = (bf16[96,768]{1,0:T(8,128)(2,1)S(1)}, bf16[96,768]{1,0:T(8,128)(2,1)}, u32[]{:S(2)}) copy-start(bf16[96,768]{1,0:T(8,128)(2,1)} %param.16) | copy-start | bytes 442372
  432.1 6.2 %copy-start.3 = (f32[256,1536]{1,0:T(8,128)S(1)}, f32[256,1536]{1,0:T(8,128)}, u32[]{:S(2)}) copy-start(f32[256,1536]{1,0:T(8,128)} %get-tuple-element.55) | copy-start | bytes 4718596
  438.4 1.2 copy-start.5
  438.4 1.9 copy-start.8
  438.4 2.5 copy-start.7
  438.4 3.1 copy-start.4
  438.4 3.8 copy-start.2
  442.2 2.1 copy-start.1
  444.3 2.1 copy-start
